TPU v7x, 512 devices: a whole 4x8x8 slice. The times are simulated.
512 devices in a mesh: line: 256 (over x, y, z), rhs: 2 (over core).
Axes of the slice: x: 4, y: 8, z: 8, core: 2. Of those that a mesh axis runs over, the one named last changes fastest.
Arguments:
- diag_blocks: float32 [256, 256, 256], P('line'), may hold values from -1 to 6, as said below
- lower_blocks: float32 [256, 256, 256], P('line'), may hold values from -1.7 to 1.7
- right_sides: float32 [256, 256, 64], P('line', None, 'rhs'), may hold values from -1.5 to 1.5
Outputs:
- solution: float32 [256, 256, 64], P('line', None, 'rhs')
Inputs may be any that keep to these rules, and one draw needn't show every extreme that they name: `diag_blocks`: each diagonal block is symmetric, and K is symmetric positive definite.
All inputs are finite; a program needn't handle non-finite values.
Results may differ from a plain program's by a relative error of at most 0.0013.
Values sent between devices are 32-bit elements; how exact they have to be, the bound alone decides.
No kernel may reach another device: no remote copies, remote signals or barrier semaphores. Data moves between devices by JAX's collectives and lax.ppermute only.
A program may use at most 64 MiB of HBM per device.

v0:
```python
import jax
import jax.numpy as jnp
from jax import lax
from jax.sharding import PartitionSpec as P


def shifted(block, axis, distance):
    devices = range(lax.axis_size(axis))
    route = [(i - distance, i) for i in devices if i - distance in devices]
    return lax.ppermute(block, axis, route)


def contract(left, right):
    return jnp.dot(left, right, precision=lax.Precision.HIGHEST, preferred_element_type=jnp.float32)


def cross_gram(left, right):
    return lax.dot_general(
        left,
        right,
        (((1,), (1,)), ((), ())),
        precision=lax.Precision.HIGHEST,
        preferred_element_type=jnp.float32,
    )


def inner_gram(left, right):
    return lax.dot_general(
        left,
        right,
        (((0,), (0,)), ((), ())),
        precision=lax.Precision.HIGHEST,
        preferred_element_type=jnp.float32,
    )


def factorize(matrix):
    extent = matrix.shape[0]
    if extent <= 128 or extent % 2 == 1:
        return jnp.linalg.cholesky(matrix)
    middle = extent // 2
    leading = factorize(matrix[:middle, :middle])
    side = lax.linalg.triangular_solve(
        leading, matrix[middle:, :middle], left_side=False, lower=True, transpose_a=True
    )
    trailing = factorize(matrix[middle:, middle:] - cross_gram(side, side))
    upper_part = jnp.concatenate(
        [leading, jnp.zeros((middle, extent - middle), jnp.float32)], axis=1
    )
    lower_part = jnp.concatenate([side, trailing], axis=1)
    return jnp.concatenate([upper_part, lower_part], axis=0)


def on_device(diag_blocks, lower_blocks, right_sides):
    diagonal = diag_blocks[0]
    coupling = lower_blocks[0]
    source = right_sides[0]
    order = diagonal.shape[0]
    position = lax.axis_index("line")
    line_size = lax.axis_size("line")
    coupling = jnp.where(position == 0, jnp.zeros_like(coupling), coupling)
    identity = jnp.eye(order, dtype=jnp.float32)
    stride = 1
    while stride < line_size:
        factor = factorize(diagonal)
        spread = lax.linalg.triangular_solve(factor, coupling, left_side=True, lower=True)
        whitened = lax.linalg.triangular_solve(factor, source, left_side=True, lower=True)
        load_term = inner_gram(spread, whitened)
        inside = position >= stride
        gram_term = inner_gram(spread, spread)
        below_factor, below_spread, below_whitened = shifted(
            (factor, spread, whitened), "line", stride
        )
        above_gram, above_load = shifted((gram_term, load_term), "line", -stride)
        below_factor = jnp.where(inside, below_factor, identity)
        crossed = lax.linalg.triangular_solve(
            below_factor, coupling, left_side=False, lower=True, transpose_a=True
        )
        diagonal = diagonal - cross_gram(crossed, crossed) - above_gram
        source = source - contract(crossed, below_whitened) - above_load
        coupling = -contract(crossed, below_spread)
        stride = stride * 2
    factor = factorize(diagonal)
    halfway = lax.linalg.triangular_solve(factor, source, left_side=True, lower=True)
    answer = lax.linalg.triangular_solve(
        factor, halfway, left_side=True, lower=True, transpose_a=True
    )
    return answer[None]


def solution(mesh):
    placed = (P("line", None, None), P("line", None, None), P("line", None, "rhs"))
    return jax.shard_map(
        on_device, mesh=mesh, in_specs=placed, out_specs=P("line", None, "rhs"), check_vma=False
    )
```

profile of v0, /device:TPU:68, one launch (start us, length us, event | category | flops | bytes accessed | tf_op | source)
XLA Modules:
  0.0 986.0 jit_solution(15906493495841870902)
XLA Ops:
  1.2 11.7 %cholesky.284 = f32[128,128]{1,0:T(8,128)S(1)} custom-call(f32[128,128]{1,0:T(8,128)S(1)} %fusion.132), custom_call_target="Cholesky" | custom-call | tf_op jit(solution)/shard_map/jit(cholesky)/cholesky | solution.py:40
  24.8 11.7 %cholesky.295 = f32[128,128]{1,0:T(8,128)S(1)} custom-call(f32[128,128]{1,0:T(8,128)S(1)} %fusion.130), custom_call_target="Cholesky" | custom-call | tf_op jit(solution)/shard_map/jit(cholesky)/cholesky | solution.py:40
  42.2 19.7 %custom-call.50 = f32[2,128,128]{1,2,0:T(8,128)S(1)} custom-call(f32[2,128,128]{2,1,0:T(8,128)S(1)} %get-tuple-element.175), custom_call_target="InvertDiagBlocksLowerTriangular" | custom-call | tf_op jit(solution)/shard_map/triangular_solve/custom-call.3 | solution.py:66
  63.7 18.1 %collective-permute-start.24 = (f32[256,32]{0,1:T(8,128)S(1)}, f32[256,32]{0,1:T(8,128)S(1)}, u32[]{:S(2)}, u32[]{:S(2)}) collective-permute-start(f32[256,32]{0,1:T(8,128)S(1)} %fusion.291), channel_id=1, source_target_pairs={{2,0},{4,2},{6,4},{8,6},{10,8},{12,10},{14,12},{16,14},{18,16},{20... | collective-permute-start | bytes 98312 | tf_op jit(solution)/shard_map/ppermute | solution.py:10
  85.7 15.8 %collective-permute-start.23 = (f32[256,32]{0,1:T(8,128)S(1)}, f32[256,32]{0,1:T(8,128)S(1)}, u32[]{:S(2)}, u32[]{:S(2)}) collective-permute-start(f32[256,32]{0,1:T(8,128)S(1)} %pad_maximum_fusion.41), channel_id=1, source_target_pairs={{0,2},{2,4},{4,6},{6,8},{8,10},{10,12},{12,14},{14,16},{16,18},{18... | collective-permute-start | bytes 98312 | tf_op jit(solution)/shard_map/ppermute | solution.py:10
  102.2 16.7 %collective-permute-start.1 = (f32[256,256]{0,1:T(8,128)S(1)}, f32[256,256]{0,1:T(8,128)S(1)}, u32[]{:S(2)}, u32[]{:S(2)}) collective-permute-start(f32[256,256]{0,1:T(8,128)S(1)} %fusion.298), channel_id=1, source_target_pairs={{2,0},{4,2},{6,4},{8,6},{10,8},{12,10},{14,12},{16,14},{18,16},{20... | collective-permute-start | bytes 786440 | tf_op jit(solution)/shard_map/ppermute | solution.py:10
  126.9 19.9 %custom-call.49 = f32[2,128,128]{1,2,0:T(8,128)S(1)} custom-call(f32[2,128,128]{2,1,0:T(8,128)S(1)} %get-tuple-element.174), custom_call_target="InvertDiagBlocksLowerTriangular" | custom-call | tf_op jit(solution)/shard_map/triangular_solve/custom-call.2 | solution.py:76
  148.6 11.7 %cholesky.306 = f32[128,128]{1,0:T(8,128)S(1)} custom-call(f32[128,128]{1,0:T(8,128)S(1)} %fusion.129), custom_call_target="Cholesky" | custom-call | tf_op jit(solution)/shard_map/jit(cholesky)/cholesky | solution.py:40
  172.1 11.7 %cholesky.317 = f32[128,128]{1,0:T(8,128)S(1)} custom-call(f32[128,128]{1,0:T(8,128)S(1)} %fusion.127), custom_call_target="Cholesky" | custom-call | tf_op jit(solution)/shard_map/jit(cholesky)/cholesky | solution.py:40
  188.9 20.1 %custom-call.53 = f32[2,128,128]{1,2,0:T(8,128)S(1)} custom-call(f32[2,128,128]{2,1,0:T(8,128)S(1)} %get-tuple-element.177), custom_call_target="InvertDiagBlocksLowerTriangular" | custom-call | tf_op jit(solution)/shard_map/triangular_solve/custom-call.3 | solution.py:66
  241.3 19.8 %custom-call.52 = f32[2,128,128]{1,2,0:T(8,128)S(1)} custom-call(f32[2,128,128]{2,1,0:T(8,128)S(1)} %get-tuple-element.176), custom_call_target="InvertDiagBlocksLowerTriangular" | custom-call | tf_op jit(solution)/shard_map/triangular_solve/custom-call.2 | solution.py:76
  263.0 11.7 %cholesky.328 = f32[128,128]{1,0:T(8,128)S(1)} custom-call(f32[128,128]{1,0:T(8,128)S(1)} %fusion.126), custom_call_target="Cholesky" | custom-call | tf_op jit(solution)/shard_map/jit(cholesky)/cholesky | solution.py:40
  286.6 11.7 %cholesky.339 = f32[128,128]{1,0:T(8,128)S(1)} custom-call(f32[128,128]{1,0:T(8,128)S(1)} %fusion.124), custom_call_target="Cholesky" | custom-call | tf_op jit(solution)/shard_map/jit(cholesky)/cholesky | solution.py:40
  303.8 19.9 %custom-call.56 = f32[2,128,128]{1,2,0:T(8,128)S(1)} custom-call(f32[2,128,128]{2,1,0:T(8,128)S(1)} %get-tuple-element.179), custom_call_target="InvertDiagBlocksLowerTriangular" | custom-call | tf_op jit(solution)/shard_map/triangular_solve/custom-call.3 | solution.py:66
  362.1 20.1 %custom-call.55 = f32[2,128,128]{1,2,0:T(8,128)S(1)} custom-call(f32[2,128,128]{2,1,0:T(8,128)S(1)} %get-tuple-element.178), custom_call_target="InvertDiagBlocksLowerTriangular" | custom-call | tf_op jit(solution)/shard_map/triangular_solve/custom-call.2 | solution.py:76
  384.0 11.7 %cholesky.350 = f32[128,128]{1,0:T(8,128)S(1)} custom-call(f32[128,128]{1,0:T(8,128)S(1)} %fusion.123), custom_call_target="Cholesky" | custom-call | tf_op jit(solution)/shard_map/jit(cholesky)/cholesky | solution.py:40
  407.6 11.7 %cholesky.361 = f32[128,128]{1,0:T(8,128)S(1)} custom-call(f32[128,128]{1,0:T(8,128)S(1)} %fusion.121), custom_call_target="Cholesky" | custom-call | tf_op jit(solution)/shard_map/jit(cholesky)/cholesky | solution.py:40
  424.8 19.8 %custom-call.59 = f32[2,128,128]{1,2,0:T(8,128)S(1)} custom-call(f32[2,128,128]{2,1,0:T(8,128)S(1)} %get-tuple-element.181), custom_call_target="InvertDiagBlocksLowerTriangular" | custom-call | tf_op jit(solution)/shard_map/triangular_solve/custom-call.3 | solution.py:66
  469.0 19.9 %custom-call.58 = f32[2,128,128]{1,2,0:T(8,128)S(1)} custom-call(f32[2,128,128]{2,1,0:T(8,128)S(1)} %get-tuple-element.180), custom_call_target="InvertDiagBlocksLowerTriangular" | custom-call | tf_op jit(solution)/shard_map/triangular_solve/custom-call.2 | solution.py:76
  490.7 11.7 %cholesky.372 = f32[128,128]{1,0:T(8,128)S(1)} custom-call(f32[128,128]{1,0:T(8,128)S(1)} %fusion.120), custom_call_target="Cholesky" | custom-call | tf_op jit(solution)/shard_map/jit(cholesky)/cholesky | solution.py:40
  514.2 11.7 %cholesky.383 = f32[128,128]{1,0:T(8,128)S(1)} custom-call(f32[128,128]{1,0:T(8,128)S(1)} %fusion.118), custom_call_target="Cholesky" | custom-call | tf_op jit(solution)/shard_map/jit(cholesky)/cholesky | solution.py:40
  531.1 20.1 %custom-call.62 = f32[2,128,128]{1,2,0:T(8,128)S(1)} custom-call(f32[2,128,128]{2,1,0:T(8,128)S(1)} %get-tuple-element.183), custom_call_target="InvertDiagBlocksLowerTriangular" | custom-call | tf_op jit(solution)/shard_map/triangular_solve/custom-call.3 | solution.py:66
  581.5 19.8 %custom-call.61 = f32[2,128,128]{1,2,0:T(8,128)S(1)} custom-call(f32[2,128,128]{2,1,0:T(8,128)S(1)} %get-tuple-element.182), custom_call_target="InvertDiagBlocksLowerTriangular" | custom-call | tf_op jit(solution)/shard_map/triangular_solve/custom-call.2 | solution.py:76
  603.1 11.7 %cholesky.394 = f32[128,128]{1,0:T(8,128)S(1)} custom-call(f32[128,128]{1,0:T(8,128)S(1)} %fusion.117), custom_call_target="Cholesky" | custom-call | tf_op jit(solution)/shard_map/jit(cholesky)/cholesky | solution.py:40
  626.6 11.7 %cholesky.405 = f32[128,128]{1,0:T(8,128)S(1)} custom-call(f32[128,128]{1,0:T(8,128)S(1)} %fusion.115), custom_call_target="Cholesky" | custom-call | tf_op jit(solution)/shard_map/jit(cholesky)/cholesky | solution.py:40
  643.5 19.9 %custom-call.65 = f32[2,128,128]{1,2,0:T(8,128)S(1)} custom-call(f32[2,128,128]{2,1,0:T(8,128)S(1)} %get-tuple-element.185), custom_call_target="InvertDiagBlocksLowerTriangular" | custom-call | tf_op jit(solution)/shard_map/triangular_solve/custom-call.3 | solution.py:66
  696.7 20.1 %custom-call.64 = f32[2,128,128]{1,2,0:T(8,128)S(1)} custom-call(f32[2,128,128]{2,1,0:T(8,128)S(1)} %get-tuple-element.184), custom_call_target="InvertDiagBlocksLowerTriangular" | custom-call | tf_op jit(solution)/shard_map/triangular_solve/custom-call.2 | solution.py:76
  759.1 19.8 %custom-call.68 = f32[2,128,128]{1,2,0:T(8,128)S(1)} custom-call(f32[2,128,128]{2,1,0:T(8,128)S(1)} %get-tuple-element.187), custom_call_target="InvertDiagBlocksLowerTriangular" | custom-call | tf_op jit(solution)/shard_map/triangular_solve/custom-call.3 | solution.py:66
  801.6 19.9 %custom-call.67 = f32[2,128,128]{1,2,0:T(8,128)S(1)} custom-call(f32[2,128,128]{2,1,0:T(8,128)S(1)} %get-tuple-element.186), custom_call_target="InvertDiagBlocksLowerTriangular" | custom-call | tf_op jit(solution)/shard_map/triangular_solve/custom-call.2 | solution.py:76
  864.0 20.1 %custom-call.71 = f32[2,128,128]{1,2,0:T(8,128)S(1)} custom-call(f32[2,128,128]{2,1,0:T(8,128)S(1)} %get-tuple-element.189), custom_call_target="InvertDiagBlocksLowerTriangular" | custom-call | tf_op jit(solution)/shard_map/triangular_solve/custom-call.3 | solution.py:66
  901.2 19.8 %custom-call.70 = f32[2,128,128]{1,2,0:T(8,128)S(1)} custom-call(f32[2,128,128]{2,1,0:T(8,128)S(1)} %get-tuple-element.188), custom_call_target="InvertDiagBlocksLowerTriangular" | custom-call | tf_op jit(solution)/shard_map/triangular_solve/custom-call.2 | solution.py:76
  963.8 19.9 %custom-call.17 = f32[2,128,128]{1,2,0:T(8,128)S(1)} custom-call(f32[2,128,128]{2,1,0:T(8,128)S(1)} %get-tuple-element.41), custom_call_target="InvertDiagBlocksLowerTriangular" | custom-call | tf_op jit(solution)/shard_map/triangular_solve | solution.py:85
  (501 shorter events, 519.7 us)
Async XLA Ops:
  63.7 145.3 %collective-permute-start.24 = (f32[256,32]{0,1:T(8,128)S(1)}, f32[256,32]{0,1:T(8,128)S(1)}, u32[]{:S(2)}, u32[]{:S(2)}) collective-permute-start(f32[256,32]{0,1:T(8,128)S(1)} %fusion.291), channel_id=1, source_target_pairs={{2,0},{4,2},{6,4},{8,6},{10,8},{12,10},{14,12},{16,14},{18,16},{20... | collective-permute-start | bytes 98312 | tf_op jit(solution)/shard_map/ppermute | solution.py:10
  81.8 41.1 %collective-permute-start = (f32[256,256]{1,0:T(8,128)S(1)}, f32[256,256]{1,0:T(8,128)S(1)}, u32[]{:S(2)}, u32[]{:S(2)}) collective-permute-start(f32[256,256]{1,0:T(8,128)S(1)} %get-tuple-element.401), channel_id=1, source_target_pairs={{0,2},{2,4},{4,6},{6,8},{8,10},{10,12},{12,14},{14,16},{16,18},{18... | collective-permute-start | bytes 786440 | tf_op jit(solution)/shard_map/ppermute | solution.py:10
  85.7 123.3 %collective-permute-start.23 = (f32[256,32]{0,1:T(8,128)S(1)}, f32[256,32]{0,1:T(8,128)S(1)}, u32[]{:S(2)}, u32[]{:S(2)}) collective-permute-start(f32[256,32]{0,1:T(8,128)S(1)} %pad_maximum_fusion.41), channel_id=1, source_target_pairs={{0,2},{2,4},{4,6},{6,8},{8,10},{10,12},{12,14},{14,16},{16,18},{18... | collective-permute-start | bytes 98312 | tf_op jit(solution)/shard_map/ppermute | solution.py:10
  102.2 45.7 %collective-permute-start.1 = (f32[256,256]{0,1:T(8,128)S(1)}, f32[256,256]{0,1:T(8,128)S(1)}, u32[]{:S(2)}, u32[]{:S(2)}) collective-permute-start(f32[256,256]{0,1:T(8,128)S(1)} %fusion.298), channel_id=1, source_target_pairs={{2,0},{4,2},{6,4},{8,6},{10,8},{12,10},{14,12},{16,14},{18,16},{20... | collective-permute-start | bytes 786440 | tf_op jit(solution)/shard_map/ppermute | solution.py:10
  118.9 97.5 %collective-permute-start.3 = (f32[256,256]{1,0:T(8,128)S(1)}, f32[256,256]{1,0:T(8,128)S(1)}, u32[]{:S(2)}, u32[]{:S(2)}) collective-permute-start(f32[256,256]{1,0:T(8,128)S(1)} %pad_maximum_fusion.1), channel_id=1, source_target_pairs={{0,2},{2,4},{4,6},{6,8},{8,10},{10,12},{12,14},{14,16},{16,18},{18... | collective-permute-start | bytes 786440 | tf_op jit(solution)/shard_map/ppermute | solution.py:10
  209.9 113.8 %collective-permute-start.25 = (f32[256,32]{0,1:T(8,128)S(1)}, f32[256,32]{0,1:T(8,128)S(1)}, u32[]{:S(2)}, u32[]{:S(2)}) collective-permute-start(f32[256,32]{0,1:T(8,128)S(1)} %pad_maximum_fusion.42), channel_id=1, source_target_pairs={{0,4},{2,6},{4,8},{6,10},{8,12},{10,14},{12,16},{14,18},{16,20},{1... | collective-permute-start | bytes 98312 | tf_op jit(solution)/shard_map/ppermute | solution.py:10
  221.8 101.9 %collective-permute-start.26 = (f32[256,32]{0,1:T(8,128)S(1)}, f32[256,32]{0,1:T(8,128)S(1)}, u32[]{:S(2)}, u32[]{:S(2)}) collective-permute-start(f32[256,32]{0,1:T(8,128)S(1)} %fusion.290), channel_id=1, source_target_pairs={{4,0},{6,2},{8,4},{10,6},{12,8},{14,10},{16,12},{18,14},{20,16},{2... | collective-permute-start | bytes 98312 | tf_op jit(solution)/shard_map/ppermute | solution.py:10
  229.8 32.4 %collective-permute-start.4 = (f32[256,256]{0,1:T(8,128)S(1)}, f32[256,256]{0,1:T(8,128)S(1)}, u32[]{:S(2)}, u32[]{:S(2)}) collective-permute-start(f32[256,256]{0,1:T(8,128)S(1)} %fusion.297), channel_id=1, source_target_pairs={{4,0},{6,2},{8,4},{10,6},{12,8},{14,10},{16,12},{18,14},{20,16},{2... | collective-permute-start | bytes 786440 | tf_op jit(solution)/shard_map/ppermute | solution.py:10
  231.8 94.7 %collective-permute-start.6 = (f32[256,256]{1,0:T(8,128)S(1)}, f32[256,256]{1,0:T(8,128)S(1)}, u32[]{:S(2)}, u32[]{:S(2)}) collective-permute-start(f32[256,256]{1,0:T(8,128)S(1)} %pad_maximum_fusion.3), channel_id=1, source_target_pairs={{0,4},{2,6},{4,8},{6,10},{8,12},{10,14},{12,16},{14,18},{16,20},{1... | collective-permute-start | bytes 786440 | tf_op jit(solution)/shard_map/ppermute | solution.py:10
  324.5 120.1 %collective-permute-start.27 = (f32[256,32]{0,1:T(8,128)S(1)}, f32[256,32]{0,1:T(8,128)S(1)}, u32[]{:S(2)}, u32[]{:S(2)}) collective-permute-start(f32[256,32]{0,1:T(8,128)S(1)} %pad_maximum_fusion.43), channel_id=1, source_target_pairs={{0,8},{2,10},{4,12},{6,14},{8,16},{10,18},{12,20},{14,22},{16,24},... | collective-permute-start | bytes 98312 | tf_op jit(solution)/shard_map/ppermute | solution.py:10
  328.0 30.1 %collective-permute-start.5 = (f32[256,256]{1,0:T(8,128)S(1)}, f32[256,256]{1,0:T(8,128)S(1)}, u32[]{:S(2)}, u32[]{:S(2)}) collective-permute-start(f32[256,256]{1,0:T(8,128)S(1)} %get-tuple-element.397), channel_id=1, source_target_pairs={{0,8},{2,10},{4,12},{6,14},{8,16},{10,18},{12,20},{14,22},{16,24},... | collective-permute-start | bytes 786440 | tf_op jit(solution)/shard_map/ppermute | solution.py:10
  334.4 110.3 %collective-permute-start.28 = (f32[256,32]{0,1:T(8,128)S(1)}, f32[256,32]{0,1:T(8,128)S(1)}, u32[]{:S(2)}, u32[]{:S(2)}) collective-permute-start(f32[256,32]{0,1:T(8,128)S(1)} %fusion.289), channel_id=1, source_target_pairs={{8,0},{10,2},{12,4},{14,6},{16,8},{18,10},{20,12},{22,14},{24,16},... | collective-permute-start | bytes 98312 | tf_op jit(solution)/shard_map/ppermute | solution.py:10
  341.6 41.6 %collective-permute-start.7 = (f32[256,256]{0,1:T(8,128)S(1)}, f32[256,256]{0,1:T(8,128)S(1)}, u32[]{:S(2)}, u32[]{:S(2)}) collective-permute-start(f32[256,256]{0,1:T(8,128)S(1)} %fusion.296), channel_id=1, source_target_pairs={{8,0},{10,2},{12,4},{14,6},{16,8},{18,10},{20,12},{22,14},{24,16},... | collective-permute-start | bytes 786440 | tf_op jit(solution)/shard_map/ppermute | solution.py:10
  349.5 97.9 %collective-permute-start.9 = (f32[256,256]{1,0:T(8,128)S(1)}, f32[256,256]{1,0:T(8,128)S(1)}, u32[]{:S(2)}, u32[]{:S(2)}) collective-permute-start(f32[256,256]{1,0:T(8,128)S(1)} %pad_maximum_fusion.5), channel_id=1, source_target_pairs={{0,8},{2,10},{4,12},{6,14},{8,16},{10,18},{12,20},{14,22},{16,24},... | collective-permute-start | bytes 786440 | tf_op jit(solution)/shard_map/ppermute | solution.py:10
  445.5 105.7 %collective-permute-start.29 = (f32[256,32]{0,1:T(8,128)S(1)}, f32[256,32]{0,1:T(8,128)S(1)}, u32[]{:S(2)}, u32[]{:S(2)}) collective-permute-start(f32[256,32]{0,1:T(8,128)S(1)} %pad_maximum_fusion.44), channel_id=1, source_target_pairs={{0,16},{2,18},{4,20},{6,22},{8,24},{10,26},{12,28},{14,30},{16,32}... | collective-permute-start | bytes 98312 | tf_op jit(solution)/shard_map/ppermute | solution.py:10
  451.1 100.1 %collective-permute-start.30 = (f32[256,32]{0,1:T(8,128)S(1)}, f32[256,32]{0,1:T(8,128)S(1)}, u32[]{:S(2)}, u32[]{:S(2)}) collective-permute-start(f32[256,32]{0,1:T(8,128)S(1)} %fusion.288), channel_id=1, source_target_pairs={{16,0},{18,2},{20,4},{22,6},{24,8},{26,10},{28,12},{30,14},{32,16}... | collective-permute-start | bytes 98312 | tf_op jit(solution)/shard_map/ppermute | solution.py:10
  458.9 31.1 %collective-permute-start.10 = (f32[256,256]{0,1:T(8,128)S(1)}, f32[256,256]{0,1:T(8,128)S(1)}, u32[]{:S(2)}, u32[]{:S(2)}) collective-permute-start(f32[256,256]{0,1:T(8,128)S(1)} %fusion.295), channel_id=1, source_target_pairs={{16,0},{18,2},{20,4},{22,6},{24,8},{26,10},{28,12},{30,14},{32,16}... | collective-permute-start | bytes 786440 | tf_op jit(solution)/shard_map/ppermute | solution.py:10
  462.9 96.4 %collective-permute-start.12 = (f32[256,256]{1,0:T(8,128)S(1)}, f32[256,256]{1,0:T(8,128)S(1)}, u32[]{:S(2)}, u32[]{:S(2)}) collective-permute-start(f32[256,256]{1,0:T(8,128)S(1)} %pad_maximum_fusion.7), channel_id=1, source_target_pairs={{0,16},{2,18},{4,20},{6,22},{8,24},{10,26},{12,28},{14,30},{16,32}... | collective-permute-start | bytes 786440 | tf_op jit(solution)/shard_map/ppermute | solution.py:10
  552.0 111.4 %collective-permute-start.31 = (f32[256,32]{0,1:T(8,128)S(1)}, f32[256,32]{0,1:T(8,128)S(1)}, u32[]{:S(2)}, u32[]{:S(2)}) collective-permute-start(f32[256,32]{0,1:T(8,128)S(1)} %pad_maximum_fusion.45), channel_id=1, source_target_pairs={{0,32},{2,34},{4,36},{6,38},{8,40},{10,42},{12,44},{14,46},{16,48}... | collective-permute-start | bytes 98312 | tf_op jit(solution)/shard_map/ppermute | solution.py:10
  565.7 97.8 %collective-permute-start.32 = (f32[256,32]{0,1:T(8,128)S(1)}, f32[256,32]{0,1:T(8,128)S(1)}, u32[]{:S(2)}, u32[]{:S(2)}) collective-permute-start(f32[256,32]{0,1:T(8,128)S(1)} %fusion.287), channel_id=1, source_target_pairs={{32,0},{34,2},{36,4},{38,6},{40,8},{42,10},{44,12},{46,14},{48,16}... | collective-permute-start | bytes 98312 | tf_op jit(solution)/shard_map/ppermute | solution.py:10
  570.5 31.8 %collective-permute-start.13 = (f32[256,256]{0,1:T(8,128)S(1)}, f32[256,256]{0,1:T(8,128)S(1)}, u32[]{:S(2)}, u32[]{:S(2)}) collective-permute-start(f32[256,256]{0,1:T(8,128)S(1)} %fusion.294), channel_id=1, source_target_pairs={{32,0},{34,2},{36,4},{38,6},{40,8},{42,10},{44,12},{46,14},{48,16}... | collective-permute-start | bytes 786440 | tf_op jit(solution)/shard_map/ppermute | solution.py:10
  572.5 95.6 %collective-permute-start.15 = (f32[256,256]{1,0:T(8,128)S(1)}, f32[256,256]{1,0:T(8,128)S(1)}, u32[]{:S(2)}, u32[]{:S(2)}) collective-permute-start(f32[256,256]{1,0:T(8,128)S(1)} %pad_maximum_fusion.9), channel_id=1, source_target_pairs={{0,32},{2,34},{4,36},{6,38},{8,40},{10,42},{12,44},{14,46},{16,48}... | collective-permute-start | bytes 786440 | tf_op jit(solution)/shard_map/ppermute | solution.py:10
  664.3 114.7 %collective-permute-start.33 = (f32[256,32]{0,1:T(8,128)S(1)}, f32[256,32]{0,1:T(8,128)S(1)}, u32[]{:S(2)}, u32[]{:S(2)}) collective-permute-start(f32[256,32]{0,1:T(8,128)S(1)} %pad_maximum_fusion.46), channel_id=1, source_target_pairs={{0,64},{2,66},{4,68},{6,70},{8,72},{10,74},{12,76},{14,78},{16,80}... | collective-permute-start | bytes 98312 | tf_op jit(solution)/shard_map/ppermute | solution.py:10
  676.5 102.5 %collective-permute-start.34 = (f32[256,32]{0,1:T(8,128)S(1)}, f32[256,32]{0,1:T(8,128)S(1)}, u32[]{:S(2)}, u32[]{:S(2)}) collective-permute-start(f32[256,32]{0,1:T(8,128)S(1)} %fusion.286), channel_id=1, source_target_pairs={{64,0},{66,2},{68,4},{70,6},{72,8},{74,10},{76,12},{78,14},{80,16}... | collective-permute-start | bytes 98312 | tf_op jit(solution)/shard_map/ppermute | solution.py:10
  681.2 36.6 %collective-permute-start.16 = (f32[256,256]{0,1:T(8,128)S(1)}, f32[256,256]{0,1:T(8,128)S(1)}, u32[]{:S(2)}, u32[]{:S(2)}) collective-permute-start(f32[256,256]{0,1:T(8,128)S(1)} %fusion.293), channel_id=1, source_target_pairs={{64,0},{66,2},{68,4},{70,6},{72,8},{74,10},{76,12},{78,14},{80,16}... | collective-permute-start | bytes 786440 | tf_op jit(solution)/shard_map/ppermute | solution.py:10
  687.1 96.2 %collective-permute-start.18 = (f32[256,256]{1,0:T(8,128)S(1)}, f32[256,256]{1,0:T(8,128)S(1)}, u32[]{:S(2)}, u32[]{:S(2)}) collective-permute-start(f32[256,256]{1,0:T(8,128)S(1)} %pad_maximum_fusion.11), channel_id=1, source_target_pairs={{0,64},{2,66},{4,68},{6,70},{8,72},{10,74},{12,76},{14,78},{16,80}... | collective-permute-start | bytes 786440 | tf_op jit(solution)/shard_map/ppermute | solution.py:10
  779.9 104.2 %collective-permute-start.35 = (f32[256,32]{0,1:T(8,128)S(1)}, f32[256,32]{0,1:T(8,128)S(1)}, u32[]{:S(2)}, u32[]{:S(2)}) collective-permute-start(f32[256,32]{0,1:T(8,128)S(1)} %pad_maximum_fusion.47), channel_id=1, source_target_pairs={{0,128},{2,130},{4,132},{6,134},{8,136},{10,138},{12,140},{14,142}... | collective-permute-start | bytes 98312 | tf_op jit(solution)/shard_map/ppermute | solution.py:10
  787.1 97.0 %collective-permute-start.36 = (f32[256,32]{0,1:T(8,128)S(1)}, f32[256,32]{0,1:T(8,128)S(1)}, u32[]{:S(2)}, u32[]{:S(2)}) collective-permute-start(f32[256,32]{0,1:T(8,128)S(1)} %fusion.285), channel_id=1, source_target_pairs={{128,0},{130,2},{132,4},{134,6},{136,8},{138,10},{140,12},{142,14}... | collective-permute-start | bytes 98312 | tf_op jit(solution)/shard_map/ppermute | solution.py:10
  791.6 30.9 %collective-permute-start.19 = (f32[256,256]{0,1:T(8,128)S(1)}, f32[256,256]{0,1:T(8,128)S(1)}, u32[]{:S(2)}, u32[]{:S(2)}) collective-permute-start(f32[256,256]{0,1:T(8,128)S(1)} %fusion.292), channel_id=1, source_target_pairs={{128,0},{130,2},{132,4},{134,6},{136,8},{138,10},{140,12},{142,14}... | collective-permute-start | bytes 786440 | tf_op jit(solution)/shard_map/ppermute | solution.py:10
  794.0 92.3 %collective-permute-start.21 = (f32[256,256]{1,0:T(8,128)S(1)}, f32[256,256]{1,0:T(8,128)S(1)}, u32[]{:S(2)}, u32[]{:S(2)}) collective-permute-start(f32[256,256]{1,0:T(8,128)S(1)} %pad_maximum_fusion.13), channel_id=1, source_target_pairs={{0,128},{2,130},{4,132},{6,134},{8,136},{10,138},{12,140},{14,142}... | collective-permute-start | bytes 786440 | tf_op jit(solution)/shard_map/ppermute | solution.py:10
  885.0 98.8 %collective-permute-start.37 = (f32[256,32]{0,1:T(8,128)S(1)}, f32[256,32]{0,1:T(8,128)S(1)}, u32[]{:S(2)}, u32[]{:S(2)}) collective-permute-start(f32[256,32]{0,1:T(8,128)S(1)} %pad_maximum_fusion.48), channel_id=1, source_target_pairs={{0,256},{2,258},{4,260},{6,262},{8,264},{10,266},{12,268},{14,270}... | collective-permute-start | bytes 98312 | tf_op jit(solution)/shard_map/ppermute | solution.py:10
  889.3 94.4 %collective-permute-start.38 = (f32[256,32]{0,1:T(8,128)S(1)}, f32[256,32]{0,1:T(8,128)S(1)}, u32[]{:S(2)}, u32[]{:S(2)}) collective-permute-start(f32[256,32]{0,1:T(8,128)S(1)} %fusion.33), channel_id=1, source_target_pairs={{256,0},{258,2},{260,4},{262,6},{264,8},{266,10},{268,12},{270,14}... | collective-permute-start | bytes 98312 | tf_op jit(solution)/shard_map/ppermute | solution.py:10
  (9 other events, 167.8 us)
where the time goes:
time: 995 us; the launch traced here: 986 us
  other arithmetic  663 us (67%)
  starting transfers between devices  196 us (20%)
  local copies, waits for them, and re-layouts  69.6 us (7%)
  matrix products  43.4 us (4%)
    another operation x54, other arithmetic, factorize(): return jnp.linalg.cholesky(matrix)  223 us
    ppermute x39, starting transfers between devices, shifted(): return lax.ppermute(block, axis, route)  196 us
    another operation x17, other arithmetic, on_device(): lax.linalg.triangular_solve(below_factor, coupling, left_side=False, lowe...  160 us
    another operation x15, other arithmetic, on_device(): lax.linalg.triangular_solve(factor, coupling, left_side=True, lower=True)  160 us
    another operation x18, other arithmetic, factorize(): lax.linalg.triangular_solve(leading, matrix[middle:, :middle], left_side=...  93.9 us
    another operation x66, local copies, waits for them, and re-layouts, on_device(): lax.linalg.triangular_solve(below_factor, coupling, left_side=False, lowe...  31.5 us
    another operation x48, local copies, waits for them, and re-layouts, on_device(): lax.linalg.triangular_solve(factor, coupling, left_side=True, lower=True)  31.3 us
    another operation x2, other arithmetic, on_device(): lax.linalg.triangular_solve(factor, halfway, left_side=True, lower=True,...  19.9 us
  transfers between devices with their start and end apart: 39, of which 3 were waited for; matrix products, arithmetic and copies ran while one was open for 72% of the time, Pallas kernels for 0%

commit v1 on v0

v1 whole, which is shorter than its diff:
```python
import functools
import jax
import jax.numpy as jnp
from jax import lax
from jax.experimental import pallas as pl
from jax.experimental.pallas import tpu as pltpu
from jax.sharding import PartitionSpec as P

F32 = jnp.float32
BF16 = jnp.bfloat16
BOTH = ("line", "rhs")
DOUBLINGS = (0, 4, 4, 4, 4, 4, 3, 1, 0)
RESIDUAL_MAX = 1.0e-2
SLOW_STEPS = 80


def split(x, terms):
    parts = []
    for i in range(terms):
        part = x.astype(BF16)
        parts.append(part)
        if i + 1 < terms:
            x = x - part.astype(F32)
    return parts


def one(a, b):
    return jnp.dot(a, b, preferred_element_type=F32)


def product(a, b):
    terms = len(a)
    total = None
    for order in range(terms - 1, -1, -1):
        for i in range(order + 1):
            term = one(a[i], b[order - i])
            total = term if total is None else total + term
    return total


def unit(n):
    rows = lax.broadcasted_iota(jnp.int32, (n, n), 0)
    cols = lax.broadcasted_iota(jnp.int32, (n, n), 1)
    return (rows == cols).astype(F32)


def left_lanes(rows, half):
    return lax.broadcasted_iota(jnp.int32, (rows, 2 * half), 1) < half


def pack(x, tail, out):
    n = x.shape[0]
    h = n // 2
    corner = x[h:, h:]
    left = left_lanes(h, h // 2)
    out[:, :h] = x[:, :h]
    out[:h, h:] = jnp.where(left, corner, tail[:h])
    out[h:, h:] = jnp.where(left, pltpu.roll(corner, h // 2, 1), tail[h:])


def unpack(m):
    n = m.shape[0]
    h = n // 2
    tail = m[:, h:]
    left = left_lanes(h, h // 2)
    corner = jnp.where(left, tail[:h], pltpu.roll(tail[h:], h // 2, 1))
    low = m[h:, :h]
    top = jnp.concatenate([m[:h, :h], low.T], axis=1)
    bottom = jnp.concatenate([low, corner], axis=1)
    return jnp.concatenate([top, bottom], axis=0), tail


def invert(d, guess, doublings, x_ref):
    identity = unit(d.shape[0])
    d_parts = split(d, 3)
    error = identity - product(d_parts[:2], split(guess, 2))
    power = error.astype(BF16)
    series = identity + error
    for _ in range(doublings):
        power = one(power, power).astype(BF16)
        series = series + one(series.astype(BF16), power)
    x = one(guess.astype(BF16), series.astype(BF16))
    x = 0.5 * (x + x.T)
    residual = identity - product(d_parts[:2], split(x, 2))
    x = x + one(x.astype(BF16), residual.astype(BF16))
    residual = identity - product(d_parts, split(x, 3))
    x_ref[...] = x + one(x.astype(BF16), residual.astype(BF16))
    size = jnp.sum(residual * residual)

    @pl.when(jnp.logical_not(size < RESIDUAL_MAX * RESIDUAL_MAX))
    def _():
        x_ref[...] = guess

        def keep_on(state):
            step, worst = state
            return jnp.logical_and(step < SLOW_STEPS, worst > 1.0e-6)

        def improve(state):
            step, _ = state
            x = x_ref[...]
            rest = identity - product(d_parts, split(x, 3))
            x = x + product(split(x, 3), split(rest, 3))
            x_ref[...] = 0.5 * (x + x.T)
            return step + 1, jnp.sum(rest * rest)

        lax.while_loop(keep_on, improve, (0, jnp.float32(1.0)))


def first_guess(d):
    identity = unit(d.shape[0])
    diagonal = jnp.sum(d * identity, axis=1, keepdims=True)
    reach = jnp.max(jnp.sum(jnp.abs(d), axis=1, keepdims=True) / diagonal)
    return identity * (jnp.minimum(1.0, 1.9 / reach) / diagonal)


def start_kernel(doublings, d_ref, b_ref, m_ref, x_ref, b_out):
    d = d_ref[...]
    invert(d, first_guess(d), doublings, x_ref)
    b0, b1 = b_ref[0], b_ref[1]
    b = jnp.concatenate([jnp.zeros((b0.shape[0], 2 * b0.shape[1]), F32), b0, b1], axis=1)
    b_out[...] = b
    x = x_ref[...]
    pack(x, product(split(x, 3), split(b, 3)), m_ref)


def reduce_rows(d_ref, b_ref, t_ref):
    n = d_ref.shape[0]
    first, first_tail = unpack(t_ref[:n])
    second, second_tail = unpack(t_ref[n:])
    b = b_ref[...] - first_tail - second_tail
    b = jnp.where(left_lanes(b.shape[0], b.shape[1] // 2), 0.0, b)
    return d_ref[...] - first - second, b


def level_kernel(doublings, d_ref, b_ref, t_ref, guess_ref, m_ref, x_ref, d_out, b_out):
    d, b = reduce_rows(d_ref, b_ref, t_ref)
    d_out[...] = d
    b_out[...] = b
    invert(d, guess_ref[...], doublings, x_ref)
    x = x_ref[...]
    pack(x, product(split(x, 3), split(b, 3)), m_ref)


def end_kernel(doublings, info, d_ref, b_ref, t_ref, guess_ref, out_ref, x_ref):
    d, b = reduce_rows(d_ref, b_ref, t_ref)
    invert(d, guess_ref[...], doublings, x_ref)
    answer = product(split(x_ref[...], 3), split(b, 3))
    w = out_ref.shape[1]
    out_ref[...] = jnp.where(info[1] == 0, answer[:, 2 * w : 3 * w], answer[:, 3 * w :])


def transfer(c, info, m_ref, t_ref):
    n = c.shape[0]
    m = jnp.where(info[1] == 0, m_ref[n:], m_ref[:n])
    x, tail = unpack(m)
    c_parts = split(c, 3)
    z = product(c_parts, split(x, 3))
    z_parts = split(z, 3)
    t = product(z_parts, split(c.T, 3))
    pack(t, product(c_parts, split(tail, 3)), t_ref)
    return z_parts


def first_coupling_kernel(info, m_ref, low_ref, near_ref, far_ref, t_ref, c_out):
    below = info[1] == 0
    c = jnp.where(below, low_ref[...], near_ref[...].T)
    c = jnp.where(jnp.logical_and(below, info[0] == 0), 0.0, c)
    far = far_ref[...]
    far = jnp.where(below, far, far.T)
    far = jnp.where(jnp.logical_and(below, info[0] == 1), 0.0, far)
    z_parts = transfer(c, info, m_ref, t_ref)
    c_out[...] = -product(z_parts, split(far, 3))


def coupling_kernel(info, m_ref, c_ref, far_ref, t_ref, c_out):
    z_parts = transfer(c_ref[...], info, m_ref, t_ref)
    c_out[...] = -product(z_parts, split(far_ref[...], 3))


def last_coupling_kernel(info, m_ref, c_ref, t_ref):
    transfer(c_ref[...], info, m_ref, t_ref)


def call(kernel, name, operands, outs, scratch=(), scalars=False):
    specs = [pl.BlockSpec(memory_space=pltpu.VMEM)] * (len(operands) - int(scalars))
    if scalars:
        specs = [pl.BlockSpec(memory_space=pltpu.SMEM)] + specs
    shapes = [jax.ShapeDtypeStruct(shape, F32) for shape in outs]
    return pl.pallas_call(
        kernel,
        name=name,
        in_specs=specs,
        out_specs=[pl.BlockSpec(memory_space=pltpu.VMEM)] * len(outs),
        out_shape=shapes,
        scratch_shapes=[pltpu.VMEM(shape, F32) for shape in scratch],
        compiler_params=pltpu.CompilerParams(vmem_limit_bytes=40 * 2**20),
    )(*operands)


def pairs(line, stride):
    if 2 * stride < line:
        return [[2 * p, 2 * ((p - stride) % line) + 1] for p in range(line)]
    real = [[2 * p, 2 * (p - stride) + 1] for p in range(stride, line)]
    quarter = line // 4
    idle = [[2 * p, 2 * (p + (3 * quarter if p < quarter else quarter)) + 1] for p in range(stride)]
    return real + idle


def outward(line, stride, core0, core1):
    route = []
    for p in range(line):
        if core0 and p + core0 * stride < line:
            route.append((2 * p, 2 * (p + core0 * stride)))
        if p - core1 * stride >= 0:
            route.append((2 * p + 1, 2 * (p - core1 * stride) + 1))
    return route


def on_device(diag_blocks, lower_blocks, right_sides):
    d, low, b = diag_blocks[0], lower_blocks[0], right_sides[0]
    n, w = b.shape
    line = lax.axis_size("line")
    info = jnp.stack([lax.axis_index("line"), lax.axis_index("rhs")]).astype(jnp.int32)
    near = lax.ppermute(low, BOTH, outward(line, 1, 0, 1))
    far = lax.ppermute(low, BOTH, outward(line, 1, 1, 2))
    sides = lax.all_gather(b, "rhs")
    square, tall = (n, n), (n, 4 * w)
    level, stride = 0, 1
    message, x, b = call(
        functools.partial(start_kernel, DOUBLINGS[0]), "start", (d, sides), (square, square, tall)
    )
    while stride < line:
        both = lax.all_gather(message, BOTH, axis_index_groups=pairs(line, stride), tiled=True)
        if stride == 1:
            term, c = call(
                first_coupling_kernel, "couple0", (info, both, low, near, far), (square, square), scalars=True
            )
        elif 2 * stride < line:
            far = lax.ppermute(c, BOTH, outward(line, stride, 1, 1))
            term, c = call(
                coupling_kernel, f"couple{level}", (info, both, c, far), (square, square), scalars=True
            )
        else:
            (term,) = call(
                last_coupling_kernel, f"couple{level}", (info, both, c), (square,), scalars=True
            )
        terms = lax.all_gather(term, "rhs", tiled=True)
        level, stride = level + 1, 2 * stride
        doublings = DOUBLINGS[min(level, len(DOUBLINGS) - 1)]
        if stride < line:
            message, x, d, b = call(
                functools.partial(level_kernel, doublings),
                f"invert{level}",
                (d, b, terms, x),
                (square, square, square, tall),
            )
        else:
            (answer,) = call(
                functools.partial(end_kernel, doublings),
                "end",
                (info, d, b, terms, x),
                ((n, w),),
                scratch=(square,),
                scalars=True,
            )
    return answer[None]


def solution(mesh):
    placed = (P("line", None, None), P("line", None, None), P("line", None, "rhs"))
    return jax.shard_map(
        on_device, mesh=mesh, in_specs=placed, out_specs=P("line", None, "rhs"), check_vma=False
    )
```

time: 995 us -> 203 us (0.20)
  the two profiles are of different devices: /device:TPU:68 before, /device:TPU:7 now
where the time goes in v1:
time: 203 us; the launch traced here: 199 us
  blocking collectives  105 us (52%)
  starting transfers between devices  51.9 us (26%)
  Pallas kernels  41.6 us (20%)
    all_gather x8, blocking collectives, on_device(): lax.all_gather(message, BOTH, axis_index_groups=pairs(line, stride), tile...  78.9 us
    pallas_call x17, Pallas kernels, call(): pl.pallas_call(kernel, name=name, in_specs=specs, out_specs=[pl.BlockSpec...  41.6 us
    ppermute x6, starting transfers between devices, on_device(): far = lax.ppermute(c, BOTH, outward(line, stride, 1, 1))  35.7 us
    all_gather x8, blocking collectives, on_device(): terms = lax.all_gather(term, 'rhs', tiled=True)  23.6 us
    ppermute x1, starting transfers between devices, on_device(): far = lax.ppermute(low, BOTH, outward(line, 1, 1, 2))  13.9 us
  transfers between devices with their start and end apart: 8, of which 0 were waited for; matrix products, arithmetic and copies ran while one was open for 0% of the time, Pallas kernels for 11%

profile of v1, /device:TPU:7, one launch (start us, length us, event | category | flops | bytes accessed | tf_op | source)
XLA Modules:
  0.0 199.2 jit_solution(9680926860974749358)
XLA Ops:
  0.0 13.9 %collective-permute-start.1 = (f32[256,256]{1,0:T(8,128)}, f32[256,256]{1,0:T(8,128)S(1)}, u32[]{:S(2)}, u32[]{:S(2)}) collective-permute-start(f32[256,256]{1,0:T(8,128)} %bitcast.8), channel_id=1, source_target_pairs={{0,2},{2,4},{4,6},{5,1},{6,8},{7,3},{8,10},{9,5},{10,12},{11,7},{1... | collective-permute-start | bytes 786440 | tf_op jit(solution)/shard_map/ppermute | solution.py:225
  14.0 2.2 %collective-permute-start = (f32[256,256]{1,0:T(8,128)}, f32[256,256]{1,0:T(8,128)S(1)}, u32[]{:S(2)}, u32[]{:S(2)}) collective-permute-start(f32[256,256]{1,0:T(8,128)} %bitcast.9), channel_id=1, source_target_pairs={{3,1},{5,3},{7,5},{9,7},{11,9},{13,11},{15,13},{17,15},{19,17},{21... | collective-permute-start | bytes 786440 | tf_op jit(solution)/shard_map/ppermute | solution.py:224
  16.2 2.1 %all_gather.51 = f32[2,256,32]{1,2,0:T(8,128)S(1)} all-gather(f32[1,256,32]{1,2,0:T(8,128)} %param.5), channel_id=1, replica_groups=mesh['line'=256,'rhs'=2] {'rhs'}, dimensions={0}, use_global_device_ids=true | all-gather | bytes 98304 | tf_op jit(solution)/shard_map/all_gather | solution.py:226
  18.4 2.6 %start.1 = (f32[256,256]{1,0:T(8,128)S(1)}, f32[256,256]{1,0:T(8,128)S(1)}, f32[256,128]{1,0:T(8,128)S(1)}) custom-call(f32[256,256]{1,0:T(8,128)S(1)} %bitcast.5, f32[2,256,32]{2,1,0:T(8,128)S(1)} %copy.6.b_ref), custom_call_target="tpu_custom_call" | custom-call | tf_op jit(solution)/shard_map/start/pallas_call | solution.py:189
  21.0 6.9 %all_gather.52.m_ref = f32[512,256]{1,0:T(8,128)S(1)} all-gather(f32[256,256]{1,0:T(8,128)S(1)} %get-tuple-element.51), channel_id=1, replica_groups={{0,511},{2,1},{4,3},{6,5},{8,7},{10,9},{12,11},{14,13},{16,15},{18,17},..., dimensions={0}, use_global_device_ids=true | all-gather | bytes 786432 | tf_op jit(solution)/shard_map/all_gather | solution.py:233
  31.6 5.9 %all_gather.53.t_ref = f32[512,256]{1,0:T(8,128)S(1)} all-gather(f32[256,256]{1,0:T(8,128)S(1)} %get-tuple-element.52), channel_id=1, replica_groups=mesh['line'=256,'rhs'=2] {'rhs'}, dimensions={0}, use_global_device_ids=true | all-gather | bytes 786432 | tf_op jit(solution)/shard_map/all_gather | solution.py:247
  37.4 3.3 %invert1.1 = (f32[256,256]{1,0:T(8,128)S(1)}, f32[256,256]{1,0:T(8,128)S(1)}, f32[256,256]{1,0:T(8,128)S(1)}, f32[256,128]{1,0:T(8,128)S(1)}) custom-call(f32[256,256]{1,0:T(8,128)S(1)} %bitcast.6, f32[256,128]{1,0:T(8,128)S(1)} %get-tuple-element.50.b_ref, f32[512,256]{1,0:T(8,128)S(1)} %all_gather.53.t_ref, f32[256,256]{1,0:T(8,128)S(1)} %get-tuple-element.53.guess_ref), custom_call_target="tpu_custom_call" | custom-call | tf_op jit(solution)/shard_map/invert1/pallas_call | solution.py:189
  40.8 8.0 %all_gather.54.m_ref = f32[512,256]{1,0:T(8,128)S(1)} all-gather(f32[256,256]{1,0:T(8,128)S(1)} %get-tuple-element.56), channel_id=1, replica_groups={{0,509},{2,511},{4,1},{6,3},{8,5},{10,7},{12,9},{14,11},{16,13},{18,15}..., dimensions={0}, use_global_device_ids=true | all-gather | bytes 786432 | tf_op jit(solution)/shard_map/all_gather | solution.py:233
  50.4 7.9 %collective-permute-start.3 = (f32[256,256]{1,0:T(8,128)S(1)}, f32[256,256]{1,0:T(8,128)S(1)}, u32[]{:S(2)}, u32[]{:S(2)}) collective-permute-start(f32[256,256]{1,0:T(8,128)S(1)} %get-tuple-element.63.c_ref), channel_id=1, source_target_pairs={{0,8},{2,10},{4,12},{6,14},{8,16},{9,1},{10,18},{11,3},{12,20},{13... | collective-permute-start | bytes 786440 | tf_op jit(solution)/shard_map/ppermute | solution.py:239
  58.3 2.7 %all_gather.55.t_ref = f32[512,256]{1,0:T(8,128)S(1)} all-gather(f32[256,256]{1,0:T(8,128)S(1)} %get-tuple-element.58), channel_id=1, replica_groups=mesh['line'=256,'rhs'=2] {'rhs'}, dimensions={0}, use_global_device_ids=true | all-gather | bytes 786432 | tf_op jit(solution)/shard_map/all_gather | solution.py:247
  61.0 3.3 %invert2.1 = (f32[256,256]{1,0:T(8,128)S(1)}, f32[256,256]{1,0:T(8,128)S(1)}, f32[256,256]{1,0:T(8,128)S(1)}, f32[256,128]{1,0:T(8,128)S(1)}) custom-call(f32[256,256]{1,0:T(8,128)S(1)} %get-tuple-element.54.d_ref, f32[256,128]{1,0:T(8,128)S(1)} %get-tuple-element.55.b_ref, f32[512,256]{1,0:T(8,128)S(1)} %all_gather.55.t_ref, ...), custom_call_target="tpu_custom_call" | custom-call | tf_op jit(solution)/shard_map/invert2/pallas_call | solution.py:189
  64.3 14.7 %all_gather.56.m_ref = f32[512,256]{1,0:T(8,128)S(1)} all-gather(f32[256,256]{1,0:T(8,128)S(1)} %get-tuple-element.62), channel_id=1, replica_groups={{0,505},{2,507},{4,509},{6,511},{8,1},{10,3},{12,5},{14,7},{16,9},{18,1..., dimensions={0}, use_global_device_ids=true | all-gather | bytes 786432 | tf_op jit(solution)/shard_map/all_gather | solution.py:233
  80.8 9.2 %collective-permute-start.4 = (f32[256,256]{1,0:T(8,128)S(1)}, f32[256,256]{1,0:T(8,128)S(1)}, u32[]{:S(2)}, u32[]{:S(2)}) collective-permute-start(f32[256,256]{1,0:T(8,128)S(1)} %get-tuple-element.69.c_ref), channel_id=1, source_target_pairs={{0,16},{2,18},{4,20},{6,22},{8,24},{10,26},{12,28},{14,30},{16,32}... | collective-permute-start | bytes 786440 | tf_op jit(solution)/shard_map/ppermute | solution.py:239
  90.0 2.4 %all_gather.57.t_ref = f32[512,256]{1,0:T(8,128)S(1)} all-gather(f32[256,256]{1,0:T(8,128)S(1)} %get-tuple-element.64), channel_id=1, replica_groups=mesh['line'=256,'rhs'=2] {'rhs'}, dimensions={0}, use_global_device_ids=true | all-gather | bytes 786432 | tf_op jit(solution)/shard_map/all_gather | solution.py:247
  92.4 3.3 %invert3.1 = (f32[256,256]{1,0:T(8,128)S(1)}, f32[256,256]{1,0:T(8,128)S(1)}, f32[256,256]{1,0:T(8,128)S(1)}, f32[256,128]{1,0:T(8,128)S(1)}) custom-call(f32[256,256]{1,0:T(8,128)S(1)} %get-tuple-element.60.d_ref, f32[256,128]{1,0:T(8,128)S(1)} %get-tuple-element.61.b_ref, f32[512,256]{1,0:T(8,128)S(1)} %all_gather.57.t_ref, ...), custom_call_target="tpu_custom_call" | custom-call | tf_op jit(solution)/shard_map/invert3/pallas_call | solution.py:189
  95.7 6.8 %all_gather.58.m_ref = f32[512,256]{1,0:T(8,128)S(1)} all-gather(f32[256,256]{1,0:T(8,128)S(1)} %get-tuple-element.68), channel_id=1, replica_groups={{0,497},{2,499},{4,501},{6,503},{8,505},{10,507},{12,509},{14,511},{16,..., dimensions={0}, use_global_device_ids=true | all-gather | bytes 786432 | tf_op jit(solution)/shard_map/all_gather | solution.py:233
  106.1 3.8 %all_gather.59.t_ref = f32[512,256]{1,0:T(8,128)S(1)} all-gather(f32[256,256]{1,0:T(8,128)S(1)} %get-tuple-element.70), channel_id=1, replica_groups=mesh['line'=256,'rhs'=2] {'rhs'}, dimensions={0}, use_global_device_ids=true | all-gather | bytes 786432 | tf_op jit(solution)/shard_map/all_gather | solution.py:247
  109.9 3.3 %invert4.1 = (f32[256,256]{1,0:T(8,128)S(1)}, f32[256,256]{1,0:T(8,128)S(1)}, f32[256,256]{1,0:T(8,128)S(1)}, f32[256,128]{1,0:T(8,128)S(1)}) custom-call(f32[256,256]{1,0:T(8,128)S(1)} %get-tuple-element.66.d_ref, f32[256,128]{1,0:T(8,128)S(1)} %get-tuple-element.67.b_ref, f32[512,256]{1,0:T(8,128)S(1)} %all_gather.59.t_ref, ...), custom_call_target="tpu_custom_call" | custom-call | tf_op jit(solution)/shard_map/invert4/pallas_call | solution.py:189
  113.2 9.9 %all_gather.60.m_ref = f32[512,256]{1,0:T(8,128)S(1)} all-gather(f32[256,256]{1,0:T(8,128)S(1)} %get-tuple-element.74), channel_id=1, replica_groups={{0,481},{2,483},{4,485},{6,487},{8,489},{10,491},{12,493},{14,495},{16,..., dimensions={0}, use_global_device_ids=true | all-gather | bytes 786432 | tf_op jit(solution)/shard_map/all_gather | solution.py:233
  124.8 5.2 %collective-permute-start.6 = (f32[256,256]{1,0:T(8,128)S(1)}, f32[256,256]{1,0:T(8,128)S(1)}, u32[]{:S(2)}, u32[]{:S(2)}) collective-permute-start(f32[256,256]{1,0:T(8,128)S(1)} %get-tuple-element.81.c_ref), channel_id=1, source_target_pairs={{0,64},{2,66},{4,68},{6,70},{8,72},{10,74},{12,76},{14,78},{16,80}... | collective-permute-start | bytes 786440 | tf_op jit(solution)/shard_map/ppermute | solution.py:239
  130.0 2.2 %all_gather.61.t_ref = f32[512,256]{1,0:T(8,128)S(1)} all-gather(f32[256,256]{1,0:T(8,128)S(1)} %get-tuple-element.76), channel_id=1, replica_groups=mesh['line'=256,'rhs'=2] {'rhs'}, dimensions={0}, use_global_device_ids=true | all-gather | bytes 786432 | tf_op jit(solution)/shard_map/all_gather | solution.py:247
  132.2 3.3 %invert5.1 = (f32[256,256]{1,0:T(8,128)S(1)}, f32[256,256]{1,0:T(8,128)S(1)}, f32[256,256]{1,0:T(8,128)S(1)}, f32[256,128]{1,0:T(8,128)S(1)}) custom-call(f32[256,256]{1,0:T(8,128)S(1)} %get-tuple-element.72.d_ref, f32[256,128]{1,0:T(8,128)S(1)} %get-tuple-element.73.b_ref, f32[512,256]{1,0:T(8,128)S(1)} %all_gather.61.t_ref, ...), custom_call_target="tpu_custom_call" | custom-call | tf_op jit(solution)/shard_map/invert5/pallas_call | solution.py:189
  135.5 14.8 %all_gather.62.m_ref = f32[512,256]{1,0:T(8,128)S(1)} all-gather(f32[256,256]{1,0:T(8,128)S(1)} %get-tuple-element.80), channel_id=1, replica_groups={{0,449},{2,451},{4,453},{6,455},{8,457},{10,459},{12,461},{14,463},{16,..., dimensions={0}, use_global_device_ids=true | all-gather | bytes 786432 | tf_op jit(solution)/shard_map/all_gather | solution.py:233
  152.0 9.5 %collective-permute-start.7 = (f32[256,256]{1,0:T(8,128)S(1)}, f32[256,256]{1,0:T(8,128)S(1)}, u32[]{:S(2)}, u32[]{:S(2)}) collective-permute-start(f32[256,256]{1,0:T(8,128)S(1)} %get-tuple-element.87.c_ref), channel_id=1, source_target_pairs={{0,128},{2,130},{4,132},{6,134},{8,136},{10,138},{12,140},{14,142}... | collective-permute-start | bytes 786440 | tf_op jit(solution)/shard_map/ppermute | solution.py:239
  161.5 2.4 %all_gather.63.t_ref = f32[512,256]{1,0:T(8,128)S(1)} all-gather(f32[256,256]{1,0:T(8,128)S(1)} %get-tuple-element.82), channel_id=1, replica_groups=mesh['line'=256,'rhs'=2] {'rhs'}, dimensions={0}, use_global_device_ids=true | all-gather | bytes 786432 | tf_op jit(solution)/shard_map/all_gather | solution.py:247
  163.9 3.1 %invert6.1 = (f32[256,256]{1,0:T(8,128)S(1)}, f32[256,256]{1,0:T(8,128)S(1)}, f32[256,256]{1,0:T(8,128)S(1)}, f32[256,128]{1,0:T(8,128)S(1)}) custom-call(f32[256,256]{1,0:T(8,128)S(1)} %get-tuple-element.78.d_ref, f32[256,128]{1,0:T(8,128)S(1)} %get-tuple-element.79.b_ref, f32[512,256]{1,0:T(8,128)S(1)} %all_gather.63.t_ref, ...), custom_call_target="tpu_custom_call" | custom-call | tf_op jit(solution)/shard_map/invert6/pallas_call | solution.py:189
  167.1 7.7 %all_gather.64.m_ref = f32[512,256]{1,0:T(8,128)S(1)} all-gather(f32[256,256]{1,0:T(8,128)S(1)} %get-tuple-element.86), channel_id=1, replica_groups={{0,385},{2,387},{4,389},{6,391},{8,393},{10,395},{12,397},{14,399},{16,..., dimensions={0}, use_global_device_ids=true | all-gather | bytes 786432 | tf_op jit(solution)/shard_map/all_gather | solution.py:233
  176.5 2.2 %all_gather.65.t_ref = f32[512,256]{1,0:T(8,128)S(1)} all-gather(f32[256,256]{1,0:T(8,128)S(1)} %get-tuple-element.88), channel_id=1, replica_groups=mesh['line'=256,'rhs'=2] {'rhs'}, dimensions={0}, use_global_device_ids=true | all-gather | bytes 786432 | tf_op jit(solution)/shard_map/all_gather | solution.py:247
  178.6 2.7 %invert7.1 = (f32[256,256]{1,0:T(8,128)S(1)}, f32[256,256]{1,0:T(8,128)S(1)}, f32[256,256]{1,0:T(8,128)S(1)}, f32[256,128]{1,0:T(8,128)S(1)}) custom-call(f32[256,256]{1,0:T(8,128)S(1)} %get-tuple-element.84.d_ref, f32[256,128]{1,0:T(8,128)S(1)} %get-tuple-element.85.b_ref, f32[512,256]{1,0:T(8,128)S(1)} %all_gather.65.t_ref, ...), custom_call_target="tpu_custom_call" | custom-call | tf_op jit(solution)/shard_map/invert7/pallas_call | solution.py:189
  181.3 10.2 %all_gather.66.m_ref = f32[512,256]{1,0:T(8,128)S(1)} all-gather(f32[256,256]{1,0:T(8,128)S(1)} %get-tuple-element.92), channel_id=1, replica_groups={{256,1},{258,3},{260,5},{262,7},{264,9},{266,11},{268,13},{270,15},{272..., dimensions={0}, use_global_device_ids=true | all-gather | bytes 786432 | tf_op jit(solution)/shard_map/all_gather | solution.py:233
  193.4 2.2 %all_gather.67.t_ref = f32[512,256]{1,0:T(8,128)S(1)} all-gather(f32[256,256]{1,0:T(8,128)S(1)} %couple7.1), channel_id=1, replica_groups=mesh['line'=256,'rhs'=2] {'rhs'}, dimensions={0}, use_global_device_ids=true | all-gather | bytes 786432 | tf_op jit(solution)/shard_map/all_gather | solution.py:247
  195.6 3.0 %end.1 = f32[256,32]{1,0:T(8,128)S(1)} custom-call(s32[2]{0:T(128)S(1)} %pad_add_fusion.info, f32[256,256]{1,0:T(8,128)S(1)} %get-tuple-element.90.d_ref, f32[256,128]{1,0:T(8,128)S(1)} %get-tuple-element.91.b_ref, f32[512,256]{1,0:T(8,128)S(1)} %all_gather.67.t_ref, f32[256,256]{1,0:T(8,128)S(1)} %get-tuple-element.94.guess_ref), custom_call_target="tpu_custom_call" | custom-call | tf_op jit(solution)/shard_map/end/pallas_call | solution.py:189
  (25 shorter events, 18.5 us)
Async XLA Ops:
  0.0 18.4 %copy-start = (f32[1,256,256]{2,1,0:T(8,128)S(1)}, f32[1,256,256]{2,1,0:T(8,128)}, u32[]{:S(2)}) copy-start(f32[1,256,256]{2,1,0:T(8,128)} %param.3) | copy-start | bytes 786436
  0.0 27.9 %collective-permute-start.1 = (f32[256,256]{1,0:T(8,128)}, f32[256,256]{1,0:T(8,128)S(1)}, u32[]{:S(2)}, u32[]{:S(2)}) collective-permute-start(f32[256,256]{1,0:T(8,128)} %bitcast.8), channel_id=1, source_target_pairs={{0,2},{2,4},{4,6},{5,1},{6,8},{7,3},{8,10},{9,5},{10,12},{11,7},{1... | collective-permute-start | bytes 786440 | tf_op jit(solution)/shard_map/ppermute | solution.py:225
  14.0 14.0 %collective-permute-start = (f32[256,256]{1,0:T(8,128)}, f32[256,256]{1,0:T(8,128)S(1)}, u32[]{:S(2)}, u32[]{:S(2)}) collective-permute-start(f32[256,256]{1,0:T(8,128)} %bitcast.9), channel_id=1, source_target_pairs={{3,1},{5,3},{7,5},{9,7},{11,9},{13,11},{15,13},{17,15},{19,17},{21... | collective-permute-start | bytes 786440 | tf_op jit(solution)/shard_map/ppermute | solution.py:224
  21.0 6.9 %copy-start.1 = (f32[1,256,256]{2,1,0:T(8,128)S(1)}, f32[1,256,256]{2,1,0:T(8,128)}, u32[]{:S(2)}) copy-start(f32[1,256,256]{2,1,0:T(8,128)} %param.4) | copy-start | bytes 786436
  29.6 19.1 %collective-permute-start.2 = (f32[256,256]{1,0:T(8,128)S(1)}, f32[256,256]{1,0:T(8,128)S(1)}, u32[]{:S(2)}, u32[]{:S(2)}) collective-permute-start(f32[256,256]{1,0:T(8,128)S(1)} %get-tuple-element.57.c_ref), channel_id=1, source_target_pairs={{0,4},{2,6},{4,8},{5,1},{6,10},{7,3},{8,12},{9,5},{10,14},{11,7},{... | collective-permute-start | bytes 786440 | tf_op jit(solution)/shard_map/ppermute | solution.py:239
  50.4 28.6 %collective-permute-start.3 = (f32[256,256]{1,0:T(8,128)S(1)}, f32[256,256]{1,0:T(8,128)S(1)}, u32[]{:S(2)}, u32[]{:S(2)}) collective-permute-start(f32[256,256]{1,0:T(8,128)S(1)} %get-tuple-element.63.c_ref), channel_id=1, source_target_pairs={{0,8},{2,10},{4,12},{6,14},{8,16},{9,1},{10,18},{11,3},{12,20},{13... | collective-permute-start | bytes 786440 | tf_op jit(solution)/shard_map/ppermute | solution.py:239
  80.8 21.7 %collective-permute-start.4 = (f32[256,256]{1,0:T(8,128)S(1)}, f32[256,256]{1,0:T(8,128)S(1)}, u32[]{:S(2)}, u32[]{:S(2)}) collective-permute-start(f32[256,256]{1,0:T(8,128)S(1)} %get-tuple-element.69.c_ref), channel_id=1, source_target_pairs={{0,16},{2,18},{4,20},{6,22},{8,24},{10,26},{12,28},{14,30},{16,32}... | collective-permute-start | bytes 786440 | tf_op jit(solution)/shard_map/ppermute | solution.py:239
  104.2 18.9 %collective-permute-start.5 = (f32[256,256]{1,0:T(8,128)S(1)}, f32[256,256]{1,0:T(8,128)S(1)}, u32[]{:S(2)}, u32[]{:S(2)}) collective-permute-start(f32[256,256]{1,0:T(8,128)S(1)} %get-tuple-element.75.c_ref), channel_id=1, source_target_pairs={{0,32},{2,34},{4,36},{6,38},{8,40},{10,42},{12,44},{14,46},{16,48}... | collective-permute-start | bytes 786440 | tf_op jit(solution)/shard_map/ppermute | solution.py:239
  124.8 25.5 %collective-permute-start.6 = (f32[256,256]{1,0:T(8,128)S(1)}, f32[256,256]{1,0:T(8,128)S(1)}, u32[]{:S(2)}, u32[]{:S(2)}) collective-permute-start(f32[256,256]{1,0:T(8,128)S(1)} %get-tuple-element.81.c_ref), channel_id=1, source_target_pairs={{0,64},{2,66},{4,68},{6,70},{8,72},{10,74},{12,76},{14,78},{16,80}... | collective-permute-start | bytes 786440 | tf_op jit(solution)/shard_map/ppermute | solution.py:239
  152.0 22.8 %collective-permute-start.7 = (f32[256,256]{1,0:T(8,128)S(1)}, f32[256,256]{1,0:T(8,128)S(1)}, u32[]{:S(2)}, u32[]{:S(2)}) collective-permute-start(f32[256,256]{1,0:T(8,128)S(1)} %get-tuple-element.87.c_ref), channel_id=1, source_target_pairs={{0,128},{2,130},{4,132},{6,134},{8,136},{10,138},{12,140},{14,142}... | collective-permute-start | bytes 786440 | tf_op jit(solution)/shard_map/ppermute | solution.py:239

commit v2 on v1

--- a/solution.py
+++ b/solution.py
@@ -9,8 +9,9 @@
 F32 = jnp.float32
 BF16 = jnp.bfloat16
 BOTH = ("line", "rhs")
-DOUBLINGS = (0, 4, 4, 4, 4, 4, 3, 1, 0)
-RESIDUAL_MAX = 1.0e-2
+DOUBLINGS = (0, 2, 2, 3, 3, 2, 2, 0, 0)
+STRETCH = (1.0, 1.5, 1.5, 1.5, 1.5, 1.5, 1.0, 1.0, 1.0)
+RESIDUAL_MAX = 5.0e-3
 SLOW_STEPS = 80
 
 
@@ -28,12 +29,16 @@
     return jnp.dot(a, b, preferred_element_type=F32)
 
 
-def product(a, b):
+def one_nt(a, b):
+    return lax.dot_general(a, b, (((1,), (1,)), ((), ())), preferred_element_type=F32)
+
+
+def product(a, b, dot=one):
     terms = len(a)
     total = None
     for order in range(terms - 1, -1, -1):
         for i in range(order + 1):
-            term = one(a[i], b[order - i])
+            term = dot(a[i], b[order - i])
             total = term if total is None else total + term
     return total
 
@@ -73,23 +78,25 @@
 def invert(d, guess, doublings, x_ref):
     identity = unit(d.shape[0])
     d_parts = split(d, 3)
-    error = identity - product(d_parts[:2], split(guess, 2))
+    guess_low = guess.astype(BF16)
+    error = identity - one(d_parts[0], guess_low)
     power = error.astype(BF16)
     series = identity + error
     for _ in range(doublings):
         power = one(power, power).astype(BF16)
         series = series + one(series.astype(BF16), power)
-    x = one(guess.astype(BF16), series.astype(BF16))
-    x = 0.5 * (x + x.T)
-    residual = identity - product(d_parts[:2], split(x, 2))
-    x = x + one(x.astype(BF16), residual.astype(BF16))
-    residual = identity - product(d_parts, split(x, 3))
-    x_ref[...] = x + one(x.astype(BF16), residual.astype(BF16))
+    x = one(guess_low, series.astype(BF16))
+    x_parts = split(x, 2)
+    residual = identity - product(d_parts[:2], x_parts)
+    x = x + one(x_parts[0], residual.astype(BF16))
+    x_parts = split(x, 3)
+    residual = identity - product(d_parts, x_parts)
+    x_ref[...] = x + one(x_parts[0], residual.astype(BF16))
     size = jnp.sum(residual * residual)
 
     @pl.when(jnp.logical_not(size < RESIDUAL_MAX * RESIDUAL_MAX))
     def _():
-        x_ref[...] = guess
+        x_ref[...] = jnp.where(size < 0.25, x, guess)
 
         def keep_on(state):
             step, worst = state
@@ -116,8 +123,8 @@
 def start_kernel(doublings, d_ref, b_ref, m_ref, x_ref, b_out):
     d = d_ref[...]
     invert(d, first_guess(d), doublings, x_ref)
-    b0, b1 = b_ref[0], b_ref[1]
-    b = jnp.concatenate([jnp.zeros((b0.shape[0], 2 * b0.shape[1]), F32), b0, b1], axis=1)
+    sides = b_ref[...]
+    b = jnp.concatenate([jnp.zeros_like(sides), sides], axis=0).T
     b_out[...] = b
     x = x_ref[...]
     pack(x, product(split(x, 3), split(b, 3)), m_ref)
@@ -132,21 +139,22 @@
     return d_ref[...] - first - second, b
 
 
-def level_kernel(doublings, d_ref, b_ref, t_ref, guess_ref, m_ref, x_ref, d_out, b_out):
+def level_kernel(doublings, stretch, d_ref, b_ref, t_ref, guess_ref, m_ref, x_ref, d_out, b_out):
     d, b = reduce_rows(d_ref, b_ref, t_ref)
     d_out[...] = d
     b_out[...] = b
-    invert(d, guess_ref[...], doublings, x_ref)
+    invert(d, stretch * guess_ref[...], doublings, x_ref)
     x = x_ref[...]
     pack(x, product(split(x, 3), split(b, 3)), m_ref)
 
 
-def end_kernel(doublings, info, d_ref, b_ref, t_ref, guess_ref, out_ref, x_ref):
+def end_kernel(doublings, stretch, info, d_ref, b_ref, t_ref, guess_ref, out_ref, x_ref):
     d, b = reduce_rows(d_ref, b_ref, t_ref)
-    invert(d, guess_ref[...], doublings, x_ref)
+    invert(d, stretch * guess_ref[...], doublings, x_ref)
     answer = product(split(x_ref[...], 3), split(b, 3))
     w = out_ref.shape[1]
-    out_ref[...] = jnp.where(info[1] == 0, answer[:, 2 * w : 3 * w], answer[:, 3 * w :])
+    answer = answer.T
+    out_ref[0] = jnp.where(info[1] == 0, answer[2 * w : 3 * w], answer[3 * w :])
 
 
 def transfer(c, info, m_ref, t_ref):
@@ -155,10 +163,12 @@
     x, tail = unpack(m)
     c_parts = split(c, 3)
     z = product(c_parts, split(x, 3))
-    z_parts = split(z, 3)
-    t = product(z_parts, split(c.T, 3))
-    pack(t, product(c_parts, split(tail, 3)), t_ref)
-    return z_parts
+    pack(product(split(z, 3), c_parts, one_nt), product(c_parts, split(tail, 3)), t_ref)
+    return z
+
+
+def following(z, far):
+    return -product(split(z, 3), split(far, 3))
 
 
 def first_coupling_kernel(info, m_ref, low_ref, near_ref, far_ref, t_ref, c_out):
@@ -168,17 +178,21 @@
     far = far_ref[...]
     far = jnp.where(below, far, far.T)
     far = jnp.where(jnp.logical_and(below, info[0] == 1), 0.0, far)
-    z_parts = transfer(c, info, m_ref, t_ref)
-    c_out[...] = -product(z_parts, split(far, 3))
-
-
-def coupling_kernel(info, m_ref, c_ref, far_ref, t_ref, c_out):
-    z_parts = transfer(c_ref[...], info, m_ref, t_ref)
-    c_out[...] = -product(z_parts, split(far_ref[...], 3))
-
-
-def last_coupling_kernel(info, m_ref, c_ref, t_ref):
-    transfer(c_ref[...], info, m_ref, t_ref)
+    c_out[...] = following(transfer(c, info, m_ref, t_ref), far)
+
+
+def second_coupling_kernel(info, m_ref, c_ref, t_ref, z_out):
+    z_out[...] = transfer(c_ref[...], info, m_ref, t_ref)
+
+
+def coupling_kernel(info, m_ref, z_ref, far_ref, t_ref, z_out, c_out):
+    c = following(z_ref[...], far_ref[...])
+    c_out[...] = c
+    z_out[...] = transfer(c, info, m_ref, t_ref)
+
+
+def last_coupling_kernel(info, m_ref, z_ref, far_ref, t_ref):
+    transfer(following(z_ref[...], far_ref[...]), info, m_ref, t_ref)
 
 
 def call(kernel, name, operands, outs, scratch=(), scalars=False):
@@ -223,7 +237,7 @@
     info = jnp.stack([lax.axis_index("line"), lax.axis_index("rhs")]).astype(jnp.int32)
     near = lax.ppermute(low, BOTH, outward(line, 1, 0, 1))
     far = lax.ppermute(low, BOTH, outward(line, 1, 1, 2))
-    sides = lax.all_gather(b, "rhs")
+    sides = lax.all_gather(b.T, "rhs", tiled=True)
     square, tall = (n, n), (n, 4 * w)
     level, stride = 0, 1
     message, x, b = call(
@@ -231,39 +245,43 @@
     )
     while stride < line:
         both = lax.all_gather(message, BOTH, axis_index_groups=pairs(line, stride), tiled=True)
-        if stride == 1:
+        if level == 0:
             term, c = call(
                 first_coupling_kernel, "couple0", (info, both, low, near, far), (square, square), scalars=True
             )
+        elif level == 1:
+            term, z = call(second_coupling_kernel, "couple1", (info, both, c), (square, square), scalars=True)
         elif 2 * stride < line:
-            far = lax.ppermute(c, BOTH, outward(line, stride, 1, 1))
-            term, c = call(
-                coupling_kernel, f"couple{level}", (info, both, c, far), (square, square), scalars=True
+            term, z, c = call(
+                coupling_kernel, f"couple{level}", (info, both, z, far), (square,) * 3, scalars=True
             )
         else:
             (term,) = call(
-                last_coupling_kernel, f"couple{level}", (info, both, c), (square,), scalars=True
-            )
+                last_coupling_kernel, f"couple{level}", (info, both, z, far), (square,), scalars=True
+            )
+        if level > 0 and 2 * stride < line:
+            far = lax.ppermute(c, BOTH, outward(line, stride, 1, 1))
         terms = lax.all_gather(term, "rhs", tiled=True)
         level, stride = level + 1, 2 * stride
-        doublings = DOUBLINGS[min(level, len(DOUBLINGS) - 1)]
+        place = min(level, len(DOUBLINGS) - 1)
+        doublings, stretch = DOUBLINGS[place], STRETCH[place]
         if stride < line:
             message, x, d, b = call(
-                functools.partial(level_kernel, doublings),
+                functools.partial(level_kernel, doublings, stretch),
                 f"invert{level}",
                 (d, b, terms, x),
                 (square, square, square, tall),
             )
         else:
             (answer,) = call(
-                functools.partial(end_kernel, doublings),
+                functools.partial(end_kernel, doublings, stretch),
                 "end",
                 (info, d, b, terms, x),
-                ((n, w),),
+                ((1, w, n),),
                 scratch=(square,),
                 scalars=True,
             )
-    return answer[None]
+    return jnp.swapaxes(answer, 1, 2)
 
 
 def solution(mesh):

time: 203 us -> 205 us (level)
  the two profiles are of different devices: /device:TPU:7 before, /device:TPU:11 now
where the time goes in v2:
time: 205 us; the launch traced here: 204 us
  blocking collectives  111 us (54%)
  Pallas kernels  52.4 us (26%)
  starting transfers between devices  37.5 us (18%)
    all_gather x8, blocking collectives, on_device(): lax.all_gather(message, BOTH, axis_index_groups=pairs(line, stride), tile...  84.5 us
    pallas_call x17, Pallas kernels, call(): pl.pallas_call(kernel, name=name, in_specs=specs, out_specs=[pl.BlockSpec...  52.4 us
    ppermute x6, starting transfers between devices, on_device(): far = lax.ppermute(c, BOTH, outward(line, stride, 1, 1))  24.8 us
    all_gather x8, blocking collectives, on_device(): terms = lax.all_gather(term, 'rhs', tiled=True)  24.6 us
    ppermute x1, starting transfers between devices, on_device(): far = lax.ppermute(low, BOTH, outward(line, 1, 1, 2))  10.5 us
  transfers between devices with their start and end apart: 8, of which 1 were waited for; matrix products, arithmetic and copies ran while one was open for 0% of the time, Pallas kernels for 16%

profile of v2, /device:TPU:11, one launch (start us, length us, event | category | flops | bytes accessed | tf_op | source)
XLA Modules:
  0.0 204.1 jit_solution(4372161612451073295)
XLA Ops:
  0.0 10.5 %collective-permute-start.1 = (f32[256,256]{1,0:T(8,128)}, f32[256,256]{1,0:T(8,128)S(1)}, u32[]{:S(2)}, u32[]{:S(2)}) collective-permute-start(f32[256,256]{1,0:T(8,128)} %bitcast.10), channel_id=1, source_target_pairs={{0,2},{2,4},{4,6},{5,1},{6,8},{7,3},{8,10},{9,5},{10,12},{11,7},{1... | collective-permute-start | bytes 786440 | tf_op jit(solution)/shard_map/ppermute | solution.py:239
  10.5 2.2 %collective-permute-start = (f32[256,256]{1,0:T(8,128)}, f32[256,256]{1,0:T(8,128)S(1)}, u32[]{:S(2)}, u32[]{:S(2)}) collective-permute-start(f32[256,256]{1,0:T(8,128)} %bitcast.11), channel_id=1, source_target_pairs={{3,1},{5,3},{7,5},{9,7},{11,9},{13,11},{15,13},{17,15},{19,17},{21... | collective-permute-start | bytes 786440 | tf_op jit(solution)/shard_map/ppermute | solution.py:238
  15.8 2.3 %start.1 = (f32[256,256]{1,0:T(8,128)S(1)}, f32[256,256]{1,0:T(8,128)S(1)}, f32[256,128]{1,0:T(8,128)S(1)}) custom-call(f32[256,256]{1,0:T(8,128)S(1)} %bitcast.8, f32[64,256]{1,0:T(8,128)S(1)} %all_gather.51.b_ref), custom_call_target="tpu_custom_call" | custom-call | tf_op jit(solution)/shard_map/start/pallas_call | solution.py:203
  18.1 6.9 %all_gather.52.m_ref = f32[512,256]{1,0:T(8,128)S(1)} all-gather(f32[256,256]{1,0:T(8,128)S(1)} %get-tuple-element.56), channel_id=1, replica_groups={{0,511},{2,1},{4,3},{6,5},{8,7},{10,9},{12,11},{14,13},{16,15},{18,17},..., dimensions={0}, use_global_device_ids=true | all-gather | bytes 786432 | tf_op jit(solution)/shard_map/all_gather | solution.py:247
  26.8 3.9 %all_gather.53.t_ref = f32[512,256]{1,0:T(8,128)S(1)} all-gather(f32[256,256]{1,0:T(8,128)S(1)} %get-tuple-element.57), channel_id=1, replica_groups=mesh['line'=256,'rhs'=2] {'rhs'}, dimensions={0}, use_global_device_ids=true | all-gather | bytes 786432 | tf_op jit(solution)/shard_map/all_gather | solution.py:264
  32.6 2.7 %invert1.1 = (f32[256,256]{1,0:T(8,128)S(1)}, f32[256,256]{1,0:T(8,128)S(1)}, f32[256,256]{1,0:T(8,128)S(1)}, f32[256,128]{1,0:T(8,128)S(1)}) custom-call(f32[256,256]{1,0:T(8,128)S(1)} %bitcast.9, f32[256,128]{1,0:T(8,128)S(1)} %get-tuple-element.55.b_ref, f32[512,256]{1,0:T(8,128)S(1)} %all_gather.53.t_ref, f32[256,256]{1,0:T(8,128)S(1)} %get-tuple-element.58.guess_ref), custom_call_target="tpu_custom_call" | custom-call | tf_op jit(solution)/shard_map/invert1/pallas_call | solution.py:203
  35.3 13.1 %all_gather.54.m_ref = f32[512,256]{1,0:T(8,128)S(1)} all-gather(f32[256,256]{1,0:T(8,128)S(1)} %get-tuple-element.61), channel_id=1, replica_groups={{0,509},{2,511},{4,1},{6,3},{8,5},{10,7},{12,9},{14,11},{16,13},{18,15}..., dimensions={0}, use_global_device_ids=true | all-gather | bytes 786432 | tf_op jit(solution)/shard_map/all_gather | solution.py:247
  50.2 3.2 %all_gather.55.t_ref = f32[512,256]{1,0:T(8,128)S(1)} all-gather(f32[256,256]{1,0:T(8,128)S(1)} %get-tuple-element.63), channel_id=1, replica_groups=mesh['line'=256,'rhs'=2] {'rhs'}, dimensions={0}, use_global_device_ids=true | all-gather | bytes 786432 | tf_op jit(solution)/shard_map/all_gather | solution.py:264
  53.4 2.7 %invert2.1 = (f32[256,256]{1,0:T(8,128)S(1)}, f32[256,256]{1,0:T(8,128)S(1)}, f32[256,256]{1,0:T(8,128)S(1)}, f32[256,128]{1,0:T(8,128)S(1)}) custom-call(f32[256,256]{1,0:T(8,128)S(1)} %get-tuple-element.59.d_ref, f32[256,128]{1,0:T(8,128)S(1)} %get-tuple-element.60.b_ref, f32[512,256]{1,0:T(8,128)S(1)} %all_gather.55.t_ref, ...), custom_call_target="tpu_custom_call" | custom-call | tf_op jit(solution)/shard_map/invert2/pallas_call | solution.py:203
  56.0 19.0 %all_gather.56.m_ref = f32[512,256]{1,0:T(8,128)S(1)} all-gather(f32[256,256]{1,0:T(8,128)S(1)} %get-tuple-element.67), channel_id=1, replica_groups={{0,505},{2,507},{4,509},{6,511},{8,1},{10,3},{12,5},{14,7},{16,9},{18,1..., dimensions={0}, use_global_device_ids=true | all-gather | bytes 786432 | tf_op jit(solution)/shard_map/all_gather | solution.py:247
  79.1 2.2 %all_gather.57.t_ref = f32[512,256]{1,0:T(8,128)S(1)} all-gather(f32[256,256]{1,0:T(8,128)S(1)} %get-tuple-element.69), channel_id=1, replica_groups=mesh['line'=256,'rhs'=2] {'rhs'}, dimensions={0}, use_global_device_ids=true | all-gather | bytes 786432 | tf_op jit(solution)/shard_map/all_gather | solution.py:264
  81.3 3.0 %invert3.1 = (f32[256,256]{1,0:T(8,128)S(1)}, f32[256,256]{1,0:T(8,128)S(1)}, f32[256,256]{1,0:T(8,128)S(1)}, f32[256,128]{1,0:T(8,128)S(1)}) custom-call(f32[256,256]{1,0:T(8,128)S(1)} %get-tuple-element.65.d_ref, f32[256,128]{1,0:T(8,128)S(1)} %get-tuple-element.66.b_ref, f32[512,256]{1,0:T(8,128)S(1)} %all_gather.57.t_ref, ...), custom_call_target="tpu_custom_call" | custom-call | tf_op jit(solution)/shard_map/invert3/pallas_call | solution.py:203
  84.4 6.8 %all_gather.58.m_ref = f32[512,256]{1,0:T(8,128)S(1)} all-gather(f32[256,256]{1,0:T(8,128)S(1)} %get-tuple-element.73), channel_id=1, replica_groups={{0,497},{2,499},{4,501},{6,503},{8,505},{10,507},{12,509},{14,511},{16,..., dimensions={0}, use_global_device_ids=true | all-gather | bytes 786432 | tf_op jit(solution)/shard_map/all_gather | solution.py:247
  92.9 2.1 %couple3.1 = (f32[256,256]{1,0:T(8,128)S(1)}, f32[256,256]{1,0:T(8,128)S(1)}, f32[256,256]{1,0:T(8,128)S(1)}) custom-call(s32[2]{0:T(128)S(1)} %pad_add_fusion.info, f32[512,256]{1,0:T(8,128)S(1)} %all_gather.58.m_ref, f32[256,256]{1,0:T(8,128)S(1)} %get-tuple-element.74.z_ref, f32[256,256]{1,0:T(8,128)S(1)} %collective-permute-done.3.far_ref), custom_call_target="tpu_custom_call" | custom-call | tf_op jit(solution)/shard_map/couple3/pallas_call | solution.py:203
  95.0 7.2 %collective-permute-start.4 = (f32[256,256]{1,0:T(8,128)S(1)}, f32[256,256]{1,0:T(8,128)S(1)}, u32[]{:S(2)}, u32[]{:S(2)}) collective-permute-start(f32[256,256]{1,0:T(8,128)S(1)} %get-tuple-element.82), channel_id=1, source_target_pairs={{0,16},{2,18},{4,20},{6,22},{8,24},{10,26},{12,28},{14,30},{16,32}... | collective-permute-start | bytes 786440 | tf_op jit(solution)/shard_map/ppermute | solution.py:263
  102.3 2.2 %all_gather.59.t_ref = f32[512,256]{1,0:T(8,128)S(1)} all-gather(f32[256,256]{1,0:T(8,128)S(1)} %get-tuple-element.76), channel_id=1, replica_groups=mesh['line'=256,'rhs'=2] {'rhs'}, dimensions={0}, use_global_device_ids=true | all-gather | bytes 786432 | tf_op jit(solution)/shard_map/all_gather | solution.py:264
  104.5 5.2 %invert4.1 = (f32[256,256]{1,0:T(8,128)S(1)}, f32[256,256]{1,0:T(8,128)S(1)}, f32[256,256]{1,0:T(8,128)S(1)}, f32[256,128]{1,0:T(8,128)S(1)}) custom-call(f32[256,256]{1,0:T(8,128)S(1)} %get-tuple-element.71.d_ref, f32[256,128]{1,0:T(8,128)S(1)} %get-tuple-element.72.b_ref, f32[512,256]{1,0:T(8,128)S(1)} %all_gather.59.t_ref, ...), custom_call_target="tpu_custom_call" | custom-call | tf_op jit(solution)/shard_map/invert4/pallas_call | solution.py:203
  109.7 7.7 %all_gather.60.m_ref = f32[512,256]{1,0:T(8,128)S(1)} all-gather(f32[256,256]{1,0:T(8,128)S(1)} %get-tuple-element.80), channel_id=1, replica_groups={{0,481},{2,483},{4,485},{6,487},{8,489},{10,491},{12,493},{14,495},{16,..., dimensions={0}, use_global_device_ids=true | all-gather | bytes 786432 | tf_op jit(solution)/shard_map/all_gather | solution.py:247
  119.5 5.9 %collective-permute-start.5 = (f32[256,256]{1,0:T(8,128)S(1)}, f32[256,256]{1,0:T(8,128)S(1)}, u32[]{:S(2)}, u32[]{:S(2)}) collective-permute-start(f32[256,256]{1,0:T(8,128)S(1)} %get-tuple-element.89), channel_id=1, source_target_pairs={{0,32},{2,34},{4,36},{6,38},{8,40},{10,42},{12,44},{14,46},{16,48}... | collective-permute-start | bytes 786440 | tf_op jit(solution)/shard_map/ppermute | solution.py:263
  125.4 2.2 %all_gather.61.t_ref = f32[512,256]{1,0:T(8,128)S(1)} all-gather(f32[256,256]{1,0:T(8,128)S(1)} %get-tuple-element.83), channel_id=1, replica_groups=mesh['line'=256,'rhs'=2] {'rhs'}, dimensions={0}, use_global_device_ids=true | all-gather | bytes 786432 | tf_op jit(solution)/shard_map/all_gather | solution.py:264
  127.6 5.0 %invert5.1 = (f32[256,256]{1,0:T(8,128)S(1)}, f32[256,256]{1,0:T(8,128)S(1)}, f32[256,256]{1,0:T(8,128)S(1)}, f32[256,128]{1,0:T(8,128)S(1)}) custom-call(f32[256,256]{1,0:T(8,128)S(1)} %get-tuple-element.78.d_ref, f32[256,128]{1,0:T(8,128)S(1)} %get-tuple-element.79.b_ref, f32[512,256]{1,0:T(8,128)S(1)} %all_gather.61.t_ref, ...), custom_call_target="tpu_custom_call" | custom-call | tf_op jit(solution)/shard_map/invert5/pallas_call | solution.py:203
  132.6 10.7 %all_gather.62.m_ref = f32[512,256]{1,0:T(8,128)S(1)} all-gather(f32[256,256]{1,0:T(8,128)S(1)} %get-tuple-element.87), channel_id=1, replica_groups={{0,449},{2,451},{4,453},{6,455},{8,457},{10,459},{12,461},{14,463},{16,..., dimensions={0}, use_global_device_ids=true | all-gather | bytes 786432 | tf_op jit(solution)/shard_map/all_gather | solution.py:247
  145.4 5.9 %collective-permute-start.6 = (f32[256,256]{1,0:T(8,128)S(1)}, f32[256,256]{1,0:T(8,128)S(1)}, u32[]{:S(2)}, u32[]{:S(2)}) collective-permute-start(f32[256,256]{1,0:T(8,128)S(1)} %get-tuple-element.96), channel_id=1, source_target_pairs={{0,64},{2,66},{4,68},{6,70},{8,72},{10,74},{12,76},{14,78},{16,80}... | collective-permute-start | bytes 786440 | tf_op jit(solution)/shard_map/ppermute | solution.py:263
  151.3 3.0 %all_gather.63.t_ref = f32[512,256]{1,0:T(8,128)S(1)} all-gather(f32[256,256]{1,0:T(8,128)S(1)} %get-tuple-element.90), channel_id=1, replica_groups=mesh['line'=256,'rhs'=2] {'rhs'}, dimensions={0}, use_global_device_ids=true | all-gather | bytes 786432 | tf_op jit(solution)/shard_map/all_gather | solution.py:264
  154.3 5.2 %invert6.1 = (f32[256,256]{1,0:T(8,128)S(1)}, f32[256,256]{1,0:T(8,128)S(1)}, f32[256,256]{1,0:T(8,128)S(1)}, f32[256,128]{1,0:T(8,128)S(1)}) custom-call(f32[256,256]{1,0:T(8,128)S(1)} %get-tuple-element.85.d_ref, f32[256,128]{1,0:T(8,128)S(1)} %get-tuple-element.86.b_ref, f32[512,256]{1,0:T(8,128)S(1)} %all_gather.63.t_ref, ...), custom_call_target="tpu_custom_call" | custom-call | tf_op jit(solution)/shard_map/invert6/pallas_call | solution.py:203
  159.5 12.3 %all_gather.64.m_ref = f32[512,256]{1,0:T(8,128)S(1)} all-gather(f32[256,256]{1,0:T(8,128)S(1)} %get-tuple-element.94), channel_id=1, replica_groups={{0,385},{2,387},{4,389},{6,391},{8,393},{10,395},{12,397},{14,399},{16,..., dimensions={0}, use_global_device_ids=true | all-gather | bytes 786432 | tf_op jit(solution)/shard_map/all_gather | solution.py:247
  175.9 4.7 %all_gather.65.t_ref = f32[512,256]{1,0:T(8,128)S(1)} all-gather(f32[256,256]{1,0:T(8,128)S(1)} %get-tuple-element.97), channel_id=1, replica_groups=mesh['line'=256,'rhs'=2] {'rhs'}, dimensions={0}, use_global_device_ids=true | all-gather | bytes 786432 | tf_op jit(solution)/shard_map/all_gather | solution.py:264
  180.5 4.4 %invert7.1 = (f32[256,256]{1,0:T(8,128)S(1)}, f32[256,256]{1,0:T(8,128)S(1)}, f32[256,256]{1,0:T(8,128)S(1)}, f32[256,128]{1,0:T(8,128)S(1)}) custom-call(f32[256,256]{1,0:T(8,128)S(1)} %get-tuple-element.92.d_ref, f32[256,128]{1,0:T(8,128)S(1)} %get-tuple-element.93.b_ref, f32[512,256]{1,0:T(8,128)S(1)} %all_gather.65.t_ref, ...), custom_call_target="tpu_custom_call" | custom-call | tf_op jit(solution)/shard_map/invert7/pallas_call | solution.py:203
  184.9 8.1 %all_gather.66.m_ref = f32[512,256]{1,0:T(8,128)S(1)} all-gather(f32[256,256]{1,0:T(8,128)S(1)} %get-tuple-element.101), channel_id=1, replica_groups={{256,1},{258,3},{260,5},{262,7},{264,9},{266,11},{268,13},{270,15},{272..., dimensions={0}, use_global_device_ids=true | all-gather | bytes 786432 | tf_op jit(solution)/shard_map/all_gather | solution.py:247
  193.0 2.1 %couple7.1 = f32[256,256]{1,0:T(8,128)S(1)} custom-call(s32[2]{0:T(128)S(1)} %pad_add_fusion.info, f32[512,256]{1,0:T(8,128)S(1)} %all_gather.66.m_ref, f32[256,256]{1,0:T(8,128)S(1)} %get-tuple-element.102.z_ref, f32[256,256]{1,0:T(8,128)S(1)} %collective-permute-done.7.far_ref), custom_call_target="tpu_custom_call" | custom-call | tf_op jit(solution)/shard_map/couple7/pallas_call | solution.py:203
  195.1 3.4 %all_gather.67.t_ref = f32[512,256]{1,0:T(8,128)S(1)} all-gather(f32[256,256]{1,0:T(8,128)S(1)} %couple7.1), channel_id=1, replica_groups=mesh['line'=256,'rhs'=2] {'rhs'}, dimensions={0}, use_global_device_ids=true | all-gather | bytes 786432 | tf_op jit(solution)/shard_map/all_gather | solution.py:264
  198.5 5.6 %end.1 = f32[1,32,256]{2,1,0:T(8,128)} custom-call(s32[2]{0:T(128)S(1)} %pad_add_fusion.info, f32[256,256]{1,0:T(8,128)S(1)} %get-tuple-element.99.d_ref, f32[256,128]{1,0:T(8,128)S(1)} %get-tuple-element.100.b_ref, f32[512,256]{1,0:T(8,128)S(1)} %all_gather.67.t_ref, f32[256,256]{1,0:T(8,128)S(1)} %get-tuple-element.104.guess_ref), custom_call_target="tpu_custom_call" | custom-call | tf_op jit(solution)/shard_map/end/pallas_call | solution.py:203
  (25 shorter events, 22.7 us)
Async XLA Ops:
  0.0 25.0 %collective-permute-start.1 = (f32[256,256]{1,0:T(8,128)}, f32[256,256]{1,0:T(8,128)S(1)}, u32[]{:S(2)}, u32[]{:S(2)}) collective-permute-start(f32[256,256]{1,0:T(8,128)} %bitcast.10), channel_id=1, source_target_pairs={{0,2},{2,4},{4,6},{5,1},{6,8},{7,3},{8,10},{9,5},{10,12},{11,7},{1... | collective-permute-start | bytes 786440 | tf_op jit(solution)/shard_map/ppermute | solution.py:239
  10.5 14.5 %collective-permute-start = (f32[256,256]{1,0:T(8,128)}, f32[256,256]{1,0:T(8,128)S(1)}, u32[]{:S(2)}, u32[]{:S(2)}) collective-permute-start(f32[256,256]{1,0:T(8,128)} %bitcast.11), channel_id=1, source_target_pairs={{3,1},{5,3},{7,5},{9,7},{11,9},{13,11},{15,13},{17,15},{19,17},{21... | collective-permute-start | bytes 786440 | tf_op jit(solution)/shard_map/ppermute | solution.py:238
  14.8 1.0 copy-start
  18.1 6.9 %copy-start.2 = (f32[1,256,256]{2,1,0:T(8,128)S(1)}, f32[1,256,256]{2,1,0:T(8,128)}, u32[]{:S(2)}) copy-start(f32[1,256,256]{2,1,0:T(8,128)} %param.4) | copy-start | bytes 786436
  26.8 5.8 %copy-start.1 = (f32[1,256,256]{2,1,0:T(8,128)S(1)}, f32[1,256,256]{2,1,0:T(8,128)}, u32[]{:S(2)}) copy-start(f32[1,256,256]{2,1,0:T(8,128)} %param.3) | copy-start | bytes 786436
  30.7 44.4 %collective-permute-start.2 = (f32[256,256]{1,0:T(8,128)S(1)}, f32[256,256]{1,0:T(8,128)S(1)}, u32[]{:S(2)}, u32[]{:S(2)}) collective-permute-start(f32[256,256]{1,0:T(8,128)S(1)} %get-tuple-element.62.c_ref), channel_id=1, source_target_pairs={{0,4},{2,6},{4,8},{5,1},{6,10},{7,3},{8,12},{9,5},{10,14},{11,7},{... | collective-permute-start | bytes 786440 | tf_op jit(solution)/shard_map/ppermute | solution.py:263
  77.2 15.7 %collective-permute-start.3 = (f32[256,256]{1,0:T(8,128)S(1)}, f32[256,256]{1,0:T(8,128)S(1)}, u32[]{:S(2)}, u32[]{:S(2)}) collective-permute-start(f32[256,256]{1,0:T(8,128)S(1)} %get-tuple-element.75), channel_id=1, source_target_pairs={{0,8},{2,10},{4,12},{6,14},{8,16},{9,1},{10,18},{11,3},{12,20},{13... | collective-permute-start | bytes 786440 | tf_op jit(solution)/shard_map/ppermute | solution.py:263
  95.0 22.4 %collective-permute-start.4 = (f32[256,256]{1,0:T(8,128)S(1)}, f32[256,256]{1,0:T(8,128)S(1)}, u32[]{:S(2)}, u32[]{:S(2)}) collective-permute-start(f32[256,256]{1,0:T(8,128)S(1)} %get-tuple-element.82), channel_id=1, source_target_pairs={{0,16},{2,18},{4,20},{6,22},{8,24},{10,26},{12,28},{14,30},{16,32}... | collective-permute-start | bytes 786440 | tf_op jit(solution)/shard_map/ppermute | solution.py:263
  119.5 23.8 %collective-permute-start.5 = (f32[256,256]{1,0:T(8,128)S(1)}, f32[256,256]{1,0:T(8,128)S(1)}, u32[]{:S(2)}, u32[]{:S(2)}) collective-permute-start(f32[256,256]{1,0:T(8,128)S(1)} %get-tuple-element.89), channel_id=1, source_target_pairs={{0,32},{2,34},{4,36},{6,38},{8,40},{10,42},{12,44},{14,46},{16,48}... | collective-permute-start | bytes 786440 | tf_op jit(solution)/shard_map/ppermute | solution.py:263
  145.4 26.4 %collective-permute-start.6 = (f32[256,256]{1,0:T(8,128)S(1)}, f32[256,256]{1,0:T(8,128)S(1)}, u32[]{:S(2)}, u32[]{:S(2)}) collective-permute-start(f32[256,256]{1,0:T(8,128)S(1)} %get-tuple-element.96), channel_id=1, source_target_pairs={{0,64},{2,66},{4,68},{6,70},{8,72},{10,74},{12,76},{14,78},{16,80}... | collective-permute-start | bytes 786440 | tf_op jit(solution)/shard_map/ppermute | solution.py:263
  173.9 19.1 %collective-permute-start.7 = (f32[256,256]{1,0:T(8,128)S(1)}, f32[256,256]{1,0:T(8,128)S(1)}, u32[]{:S(2)}, u32[]{:S(2)}) collective-permute-start(f32[256,256]{1,0:T(8,128)S(1)} %get-tuple-element.103), channel_id=1, source_target_pairs={{0,128},{2,130},{4,132},{6,134},{8,136},{10,138},{12,140},{14,142}... | collective-permute-start | bytes 786440 | tf_op jit(solution)/shard_map/ppermute | solution.py:263

commit v3 on v2

--- a/solution.py
+++ b/solution.py
@@ -54,30 +54,33 @@
 
 
 def pack(x, tail, out):
-    n = x.shape[0]
-    h = n // 2
-    corner = x[h:, h:]
-    left = left_lanes(h, h // 2)
-    out[:, :h] = x[:, :h]
-    out[:h, h:] = jnp.where(left, corner, tail[:h])
-    out[h:, h:] = jnp.where(left, pltpu.roll(corner, h // 2, 1), tail[h:])
+    h = x.shape[0] // 2
+    q = h // 2
+    left = left_lanes(q, q)
+    out[:q] = jnp.where(left, x[:q, :h], pltpu.roll(x[h : h + q, h:], q, 1))
+    out[q:h] = x[q:h, :h]
+    out[h : 2 * h] = x[h:, :h]
+    out[2 * h : 2 * h + q] = x[h + q :, h:]
+    out[2 * h + q :] = jnp.where(left_lanes(h, q), pltpu.roll(tail[:h], q, 1), tail[h:])
 
 
 def unpack(m):
-    n = m.shape[0]
-    h = n // 2
-    tail = m[:, h:]
-    left = left_lanes(h, h // 2)
-    corner = jnp.where(left, tail[:h], pltpu.roll(tail[h:], h // 2, 1))
-    low = m[h:, :h]
-    top = jnp.concatenate([m[:h, :h], low.T], axis=1)
+    h = 2 * m.shape[0] // 7
+    q = h // 2
+    left = left_lanes(q, q)
+    first, low, last, tail = m[:h], m[h : 2 * h], m[2 * h : 2 * h + q], m[2 * h + q :]
+    upper = jnp.concatenate([jnp.where(left, first[:q], first.T[:q]), first[q:]], axis=0)
+    mirrored = jnp.concatenate([last, last], axis=0).T[:q]
+    corner = jnp.concatenate([jnp.where(left, pltpu.roll(first[:q], q, 1), mirrored), last], axis=0)
+    top = jnp.concatenate([upper, low.T], axis=1)
     bottom = jnp.concatenate([low, corner], axis=1)
-    return jnp.concatenate([top, bottom], axis=0), tail
-
-
-def invert(d, guess, doublings, x_ref):
+    return jnp.concatenate([top, bottom], axis=0), jnp.concatenate([pltpu.roll(tail, q, 1), tail], axis=0)
+
+
+def invert(d, guess, b, doublings, x_ref, finish):
     identity = unit(d.shape[0])
     d_parts = split(d, 3)
+    b_parts = split(b, 3)
     guess_low = guess.astype(BF16)
     error = identity - one(d_parts[0], guess_low)
     power = error.astype(BF16)
@@ -91,7 +94,11 @@
     x = x + one(x_parts[0], residual.astype(BF16))
     x_parts = split(x, 3)
     residual = identity - product(d_parts, x_parts)
-    x_ref[...] = x + one(x_parts[0], residual.astype(BF16))
+    rest = residual.astype(BF16)
+    y = product(x_parts, b_parts) + one(x_parts[0], one(rest, b_parts[0]).astype(BF16))
+    close = x + one(x_parts[0], rest)
+    x_ref[...] = close
+    finish(close, y)
     size = jnp.sum(residual * residual)
 
     @pl.when(jnp.logical_not(size < RESIDUAL_MAX * RESIDUAL_MAX))
@@ -111,6 +118,7 @@
             return step + 1, jnp.sum(rest * rest)
 
         lax.while_loop(keep_on, improve, (0, jnp.float32(1.0)))
+        finish(x_ref[...], product(split(x_ref[...], 3), b_parts))
 
 
 def first_guess(d):
@@ -122,44 +130,41 @@
 
 def start_kernel(doublings, d_ref, b_ref, m_ref, x_ref, b_out):
     d = d_ref[...]
-    invert(d, first_guess(d), doublings, x_ref)
     sides = b_ref[...]
     b = jnp.concatenate([jnp.zeros_like(sides), sides], axis=0).T
     b_out[...] = b
-    x = x_ref[...]
-    pack(x, product(split(x, 3), split(b, 3)), m_ref)
+    invert(d, first_guess(d), b, doublings, x_ref, lambda x, y: pack(x, y, m_ref))
 
 
 def reduce_rows(d_ref, b_ref, t_ref):
-    n = d_ref.shape[0]
-    first, first_tail = unpack(t_ref[:n])
-    second, second_tail = unpack(t_ref[n:])
-    b = b_ref[...] - first_tail - second_tail
+    half = t_ref.shape[0] // 2
+    term, tail = unpack(t_ref[:half] + t_ref[half:])
+    b = b_ref[...] - tail
     b = jnp.where(left_lanes(b.shape[0], b.shape[1] // 2), 0.0, b)
-    return d_ref[...] - first - second, b
+    return d_ref[...] - term, b
 
 
 def level_kernel(doublings, stretch, d_ref, b_ref, t_ref, guess_ref, m_ref, x_ref, d_out, b_out):
     d, b = reduce_rows(d_ref, b_ref, t_ref)
     d_out[...] = d
     b_out[...] = b
-    invert(d, stretch * guess_ref[...], doublings, x_ref)
-    x = x_ref[...]
-    pack(x, product(split(x, 3), split(b, 3)), m_ref)
+    invert(d, stretch * guess_ref[...], b, doublings, x_ref, lambda x, y: pack(x, y, m_ref))
 
 
 def end_kernel(doublings, stretch, info, d_ref, b_ref, t_ref, guess_ref, out_ref, x_ref):
     d, b = reduce_rows(d_ref, b_ref, t_ref)
-    invert(d, stretch * guess_ref[...], doublings, x_ref)
-    answer = product(split(x_ref[...], 3), split(b, 3))
     w = out_ref.shape[1]
-    answer = answer.T
-    out_ref[0] = jnp.where(info[1] == 0, answer[2 * w : 3 * w], answer[3 * w :])
+
+    def finish(_, y):
+        y = y.T
+        out_ref[0] = jnp.where(info[1] == 0, y[2 * w : 3 * w], y[3 * w :])
+
+    invert(d, stretch * guess_ref[...], b, doublings, x_ref, finish)
 
 
 def transfer(c, info, m_ref, t_ref):
-    n = c.shape[0]
-    m = jnp.where(info[1] == 0, m_ref[n:], m_ref[:n])
+    half = m_ref.shape[0] // 2
+    m = jnp.where(info[1] == 0, m_ref[half:], m_ref[:half])
     x, tail = unpack(m)
     c_parts = split(c, 3)
     z = product(c_parts, split(x, 3))
@@ -238,26 +243,26 @@
     near = lax.ppermute(low, BOTH, outward(line, 1, 0, 1))
     far = lax.ppermute(low, BOTH, outward(line, 1, 1, 2))
     sides = lax.all_gather(b.T, "rhs", tiled=True)
-    square, tall = (n, n), (n, 4 * w)
+    square, tall, packed = (n, n), (n, 4 * w), (7 * n // 4, n // 2)
     level, stride = 0, 1
     message, x, b = call(
-        functools.partial(start_kernel, DOUBLINGS[0]), "start", (d, sides), (square, square, tall)
+        functools.partial(start_kernel, DOUBLINGS[0]), "start", (d, sides), (packed, square, tall)
     )
     while stride < line:
         both = lax.all_gather(message, BOTH, axis_index_groups=pairs(line, stride), tiled=True)
         if level == 0:
             term, c = call(
-                first_coupling_kernel, "couple0", (info, both, low, near, far), (square, square), scalars=True
+                first_coupling_kernel, "couple0", (info, both, low, near, far), (packed, square), scalars=True
             )
         elif level == 1:
-            term, z = call(second_coupling_kernel, "couple1", (info, both, c), (square, square), scalars=True)
+            term, z = call(second_coupling_kernel, "couple1", (info, both, c), (packed, square), scalars=True)
         elif 2 * stride < line:
             term, z, c = call(
-                coupling_kernel, f"couple{level}", (info, both, z, far), (square,) * 3, scalars=True
+                coupling_kernel, f"couple{level}", (info, both, z, far), (packed, square, square), scalars=True
             )
         else:
             (term,) = call(
-                last_coupling_kernel, f"couple{level}", (info, both, z, far), (square,), scalars=True
+                last_coupling_kernel, f"couple{level}", (info, both, z, far), (packed,), scalars=True
             )
         if level > 0 and 2 * stride < line:
             far = lax.ppermute(c, BOTH, outward(line, stride, 1, 1))
@@ -270,7 +275,7 @@
                 functools.partial(level_kernel, doublings, stretch),
                 f"invert{level}",
                 (d, b, terms, x),
-                (square, square, square, tall),
+                (packed, square, square, tall),
             )
         else:
             (answer,) = call(

time: 205 us -> 199 us (0.971)
  the two profiles are of different devices: /device:TPU:11 before, /device:TPU:5 now
where the time goes in v3:
time: 199 us
  blocking collectives  110 us (55%)
  Pallas kernels  49.2 us (25%)
  starting transfers between devices  38.5 us (19%)
    all_gather x8, blocking collectives, on_device(): lax.all_gather(message, BOTH, axis_index_groups=pairs(line, stride), tile...  75.1 us
    pallas_call x17, Pallas kernels, call(): pl.pallas_call(kernel, name=name, in_specs=specs, out_specs=[pl.BlockSpec...  49.2 us
    all_gather x8, blocking collectives, on_device(): terms = lax.all_gather(term, 'rhs', tiled=True)  32.6 us
    ppermute x6, starting transfers between devices, on_device(): far = lax.ppermute(c, BOTH, outward(line, stride, 1, 1))  22.8 us
    ppermute x1, starting transfers between devices, on_device(): far = lax.ppermute(low, BOTH, outward(line, 1, 1, 2))  13.5 us
  transfers between devices with their start and end apart: 8, of which 0 were waited for; matrix products, arithmetic and copies ran while one was open for 0% of the time, Pallas kernels for 15%

profile of v3, /device:TPU:5, one launch (start us, length us, event | category | flops | bytes accessed | tf_op | source)
XLA Modules:
  0.0 198.6 jit_solution(7664998377004170609)
XLA Ops:
  0.0 13.5 %collective-permute-start.1 = (f32[256,256]{1,0:T(8,128)}, f32[256,256]{1,0:T(8,128)S(1)}, u32[]{:S(2)}, u32[]{:S(2)}) collective-permute-start(f32[256,256]{1,0:T(8,128)} %bitcast.10), channel_id=1, source_target_pairs={{0,2},{2,4},{4,6},{5,1},{6,8},{7,3},{8,10},{9,5},{10,12},{11,7},{1... | collective-permute-start | bytes 786440 | tf_op jit(solution)/shard_map/ppermute | solution.py:244
  13.5 2.2 %collective-permute-start = (f32[256,256]{1,0:T(8,128)}, f32[256,256]{1,0:T(8,128)S(1)}, u32[]{:S(2)}, u32[]{:S(2)}) collective-permute-start(f32[256,256]{1,0:T(8,128)} %bitcast.11), channel_id=1, source_target_pairs={{3,1},{5,3},{7,5},{9,7},{11,9},{13,11},{15,13},{17,15},{19,17},{21... | collective-permute-start | bytes 786440 | tf_op jit(solution)/shard_map/ppermute | solution.py:243
  20.8 6.5 %all_gather.52.m_ref = f32[896,128]{1,0:T(8,128)S(1)} all-gather(f32[448,128]{1,0:T(8,128)S(1)} %get-tuple-element.56), channel_id=1, replica_groups={{0,511},{2,1},{4,3},{6,5},{8,7},{10,9},{12,11},{14,13},{16,15},{18,17},..., dimensions={0}, use_global_device_ids=true | all-gather | bytes 688128 | tf_op jit(solution)/shard_map/all_gather | solution.py:252
  29.2 6.0 %all_gather.53.t_ref = f32[896,128]{1,0:T(8,128)S(1)} all-gather(f32[448,128]{1,0:T(8,128)S(1)} %get-tuple-element.57), channel_id=1, replica_groups=mesh['line'=256,'rhs'=2] {'rhs'}, dimensions={0}, use_global_device_ids=true | all-gather | bytes 688128 | tf_op jit(solution)/shard_map/all_gather | solution.py:269
  37.1 2.4 %invert1.1 = (f32[448,128]{1,0:T(8,128)S(1)}, f32[256,256]{1,0:T(8,128)S(1)}, f32[256,256]{1,0:T(8,128)S(1)}, f32[256,128]{1,0:T(8,128)S(1)}) custom-call(f32[256,256]{1,0:T(8,128)S(1)} %bitcast.9, f32[256,128]{1,0:T(8,128)S(1)} %get-tuple-element.55.b_ref, f32[896,128]{1,0:T(8,128)S(1)} %all_gather.53.t_ref, f32[256,256]{1,0:T(8,128)S(1)} %get-tuple-element.58.guess_ref), custom_call_target="tpu_custom_call" | custom-call | tf_op jit(solution)/shard_map/invert1/pallas_call | solution.py:208
  39.5 10.7 %all_gather.54.m_ref = f32[896,128]{1,0:T(8,128)S(1)} all-gather(f32[448,128]{1,0:T(8,128)S(1)} %get-tuple-element.61), channel_id=1, replica_groups={{0,509},{2,511},{4,1},{6,3},{8,5},{10,7},{12,9},{14,11},{16,13},{18,15}..., dimensions={0}, use_global_device_ids=true | all-gather | bytes 688128 | tf_op jit(solution)/shard_map/all_gather | solution.py:252
  52.2 4.8 %all_gather.55.t_ref = f32[896,128]{1,0:T(8,128)S(1)} all-gather(f32[448,128]{1,0:T(8,128)S(1)} %get-tuple-element.63), channel_id=1, replica_groups=mesh['line'=256,'rhs'=2] {'rhs'}, dimensions={0}, use_global_device_ids=true | all-gather | bytes 688128 | tf_op jit(solution)/shard_map/all_gather | solution.py:269
  57.0 2.4 %invert2.1 = (f32[448,128]{1,0:T(8,128)S(1)}, f32[256,256]{1,0:T(8,128)S(1)}, f32[256,256]{1,0:T(8,128)S(1)}, f32[256,128]{1,0:T(8,128)S(1)}) custom-call(f32[256,256]{1,0:T(8,128)S(1)} %get-tuple-element.59.d_ref, f32[256,128]{1,0:T(8,128)S(1)} %get-tuple-element.60.b_ref, f32[896,128]{1,0:T(8,128)S(1)} %all_gather.55.t_ref, ...), custom_call_target="tpu_custom_call" | custom-call | tf_op jit(solution)/shard_map/invert2/pallas_call | solution.py:208
  59.4 14.3 %all_gather.56.m_ref = f32[896,128]{1,0:T(8,128)S(1)} all-gather(f32[448,128]{1,0:T(8,128)S(1)} %get-tuple-element.67), channel_id=1, replica_groups={{0,505},{2,507},{4,509},{6,511},{8,1},{10,3},{12,5},{14,7},{16,9},{18,1..., dimensions={0}, use_global_device_ids=true | all-gather | bytes 688128 | tf_op jit(solution)/shard_map/all_gather | solution.py:252
  75.9 7.8 %collective-permute-start.3 = (f32[256,256]{1,0:T(8,128)S(1)}, f32[256,256]{1,0:T(8,128)S(1)}, u32[]{:S(2)}, u32[]{:S(2)}) collective-permute-start(f32[256,256]{1,0:T(8,128)S(1)} %get-tuple-element.75), channel_id=1, source_target_pairs={{0,8},{2,10},{4,12},{6,14},{8,16},{9,1},{10,18},{11,3},{12,20},{13... | collective-permute-start | bytes 786440 | tf_op jit(solution)/shard_map/ppermute | solution.py:268
  83.7 2.3 %all_gather.57.t_ref = f32[896,128]{1,0:T(8,128)S(1)} all-gather(f32[448,128]{1,0:T(8,128)S(1)} %get-tuple-element.69), channel_id=1, replica_groups=mesh['line'=256,'rhs'=2] {'rhs'}, dimensions={0}, use_global_device_ids=true | all-gather | bytes 688128 | tf_op jit(solution)/shard_map/all_gather | solution.py:269
  86.0 2.6 %invert3.1 = (f32[448,128]{1,0:T(8,128)S(1)}, f32[256,256]{1,0:T(8,128)S(1)}, f32[256,256]{1,0:T(8,128)S(1)}, f32[256,128]{1,0:T(8,128)S(1)}) custom-call(f32[256,256]{1,0:T(8,128)S(1)} %get-tuple-element.65.d_ref, f32[256,128]{1,0:T(8,128)S(1)} %get-tuple-element.66.b_ref, f32[896,128]{1,0:T(8,128)S(1)} %all_gather.57.t_ref, ...), custom_call_target="tpu_custom_call" | custom-call | tf_op jit(solution)/shard_map/invert3/pallas_call | solution.py:208
  88.6 6.4 %all_gather.58.m_ref = f32[896,128]{1,0:T(8,128)S(1)} all-gather(f32[448,128]{1,0:T(8,128)S(1)} %get-tuple-element.73), channel_id=1, replica_groups={{0,497},{2,499},{4,501},{6,503},{8,505},{10,507},{12,509},{14,511},{16,..., dimensions={0}, use_global_device_ids=true | all-gather | bytes 688128 | tf_op jit(solution)/shard_map/all_gather | solution.py:252
  97.1 3.9 %collective-permute-start.4 = (f32[256,256]{1,0:T(8,128)S(1)}, f32[256,256]{1,0:T(8,128)S(1)}, u32[]{:S(2)}, u32[]{:S(2)}) collective-permute-start(f32[256,256]{1,0:T(8,128)S(1)} %get-tuple-element.82), channel_id=1, source_target_pairs={{0,16},{2,18},{4,20},{6,22},{8,24},{10,26},{12,28},{14,30},{16,32}... | collective-permute-start | bytes 786440 | tf_op jit(solution)/shard_map/ppermute | solution.py:268
  101.0 2.4 %all_gather.59.t_ref = f32[896,128]{1,0:T(8,128)S(1)} all-gather(f32[448,128]{1,0:T(8,128)S(1)} %get-tuple-element.76), channel_id=1, replica_groups=mesh['line'=256,'rhs'=2] {'rhs'}, dimensions={0}, use_global_device_ids=true | all-gather | bytes 688128 | tf_op jit(solution)/shard_map/all_gather | solution.py:269
  103.4 2.6 %invert4.1 = (f32[448,128]{1,0:T(8,128)S(1)}, f32[256,256]{1,0:T(8,128)S(1)}, f32[256,256]{1,0:T(8,128)S(1)}, f32[256,128]{1,0:T(8,128)S(1)}) custom-call(f32[256,256]{1,0:T(8,128)S(1)} %get-tuple-element.71.d_ref, f32[256,128]{1,0:T(8,128)S(1)} %get-tuple-element.72.b_ref, f32[896,128]{1,0:T(8,128)S(1)} %all_gather.59.t_ref, ...), custom_call_target="tpu_custom_call" | custom-call | tf_op jit(solution)/shard_map/invert4/pallas_call | solution.py:208
  106.0 8.5 %all_gather.60.m_ref = f32[896,128]{1,0:T(8,128)S(1)} all-gather(f32[448,128]{1,0:T(8,128)S(1)} %get-tuple-element.80), channel_id=1, replica_groups={{0,481},{2,483},{4,485},{6,487},{8,489},{10,491},{12,493},{14,495},{16,..., dimensions={0}, use_global_device_ids=true | all-gather | bytes 688128 | tf_op jit(solution)/shard_map/all_gather | solution.py:252
  116.7 4.3 %collective-permute-start.5 = (f32[256,256]{1,0:T(8,128)S(1)}, f32[256,256]{1,0:T(8,128)S(1)}, u32[]{:S(2)}, u32[]{:S(2)}) collective-permute-start(f32[256,256]{1,0:T(8,128)S(1)} %get-tuple-element.89), channel_id=1, source_target_pairs={{0,32},{2,34},{4,36},{6,38},{8,40},{10,42},{12,44},{14,46},{16,48}... | collective-permute-start | bytes 786440 | tf_op jit(solution)/shard_map/ppermute | solution.py:268
  121.0 2.9 %all_gather.61.t_ref = f32[896,128]{1,0:T(8,128)S(1)} all-gather(f32[448,128]{1,0:T(8,128)S(1)} %get-tuple-element.83), channel_id=1, replica_groups=mesh['line'=256,'rhs'=2] {'rhs'}, dimensions={0}, use_global_device_ids=true | all-gather | bytes 688128 | tf_op jit(solution)/shard_map/all_gather | solution.py:269
  123.9 5.2 %invert5.1 = (f32[448,128]{1,0:T(8,128)S(1)}, f32[256,256]{1,0:T(8,128)S(1)}, f32[256,256]{1,0:T(8,128)S(1)}, f32[256,128]{1,0:T(8,128)S(1)}) custom-call(f32[256,256]{1,0:T(8,128)S(1)} %get-tuple-element.78.d_ref, f32[256,128]{1,0:T(8,128)S(1)} %get-tuple-element.79.b_ref, f32[896,128]{1,0:T(8,128)S(1)} %all_gather.61.t_ref, ...), custom_call_target="tpu_custom_call" | custom-call | tf_op jit(solution)/shard_map/invert5/pallas_call | solution.py:208
  129.0 13.4 %all_gather.62.m_ref = f32[896,128]{1,0:T(8,128)S(1)} all-gather(f32[448,128]{1,0:T(8,128)S(1)} %get-tuple-element.87), channel_id=1, replica_groups={{0,449},{2,451},{4,453},{6,455},{8,457},{10,459},{12,461},{14,463},{16,..., dimensions={0}, use_global_device_ids=true | all-gather | bytes 688128 | tf_op jit(solution)/shard_map/all_gather | solution.py:252
  142.4 2.1 %couple5.1 = (f32[448,128]{1,0:T(8,128)S(1)}, f32[256,256]{1,0:T(8,128)S(1)}, f32[256,256]{1,0:T(8,128)S(1)}) custom-call(s32[2]{0:T(128)S(1)} %pad_add_fusion.info, f32[896,128]{1,0:T(8,128)S(1)} %all_gather.62.m_ref, f32[256,256]{1,0:T(8,128)S(1)} %get-tuple-element.88.z_ref, f32[256,256]{1,0:T(8,128)S(1)} %collective-permute-done.5.far_ref), custom_call_target="tpu_custom_call" | custom-call | tf_op jit(solution)/shard_map/couple5/pallas_call | solution.py:208
  144.5 3.0 %collective-permute-start.6 = (f32[256,256]{1,0:T(8,128)S(1)}, f32[256,256]{1,0:T(8,128)S(1)}, u32[]{:S(2)}, u32[]{:S(2)}) collective-permute-start(f32[256,256]{1,0:T(8,128)S(1)} %get-tuple-element.96), channel_id=1, source_target_pairs={{0,64},{2,66},{4,68},{6,70},{8,72},{10,74},{12,76},{14,78},{16,80}... | collective-permute-start | bytes 786440 | tf_op jit(solution)/shard_map/ppermute | solution.py:268
  147.6 2.1 %all_gather.63.t_ref = f32[896,128]{1,0:T(8,128)S(1)} all-gather(f32[448,128]{1,0:T(8,128)S(1)} %get-tuple-element.90), channel_id=1, replica_groups=mesh['line'=256,'rhs'=2] {'rhs'}, dimensions={0}, use_global_device_ids=true | all-gather | bytes 688128 | tf_op jit(solution)/shard_map/all_gather | solution.py:269
  149.7 5.2 %invert6.1 = (f32[448,128]{1,0:T(8,128)S(1)}, f32[256,256]{1,0:T(8,128)S(1)}, f32[256,256]{1,0:T(8,128)S(1)}, f32[256,128]{1,0:T(8,128)S(1)}) custom-call(f32[256,256]{1,0:T(8,128)S(1)} %get-tuple-element.85.d_ref, f32[256,128]{1,0:T(8,128)S(1)} %get-tuple-element.86.b_ref, f32[896,128]{1,0:T(8,128)S(1)} %all_gather.63.t_ref, ...), custom_call_target="tpu_custom_call" | custom-call | tf_op jit(solution)/shard_map/invert6/pallas_call | solution.py:208
  154.9 6.5 %all_gather.64.m_ref = f32[896,128]{1,0:T(8,128)S(1)} all-gather(f32[448,128]{1,0:T(8,128)S(1)} %get-tuple-element.94), channel_id=1, replica_groups={{0,385},{2,387},{4,389},{6,391},{8,393},{10,395},{12,397},{14,399},{16,..., dimensions={0}, use_global_device_ids=true | all-gather | bytes 688128 | tf_op jit(solution)/shard_map/all_gather | solution.py:252
  165.5 9.9 %all_gather.65.t_ref = f32[896,128]{1,0:T(8,128)S(1)} all-gather(f32[448,128]{1,0:T(8,128)S(1)} %get-tuple-element.97), channel_id=1, replica_groups=mesh['line'=256,'rhs'=2] {'rhs'}, dimensions={0}, use_global_device_ids=true | all-gather | bytes 688128 | tf_op jit(solution)/shard_map/all_gather | solution.py:269
  175.3 4.6 %invert7.1 = (f32[448,128]{1,0:T(8,128)S(1)}, f32[256,256]{1,0:T(8,128)S(1)}, f32[256,256]{1,0:T(8,128)S(1)}, f32[256,128]{1,0:T(8,128)S(1)}) custom-call(f32[256,256]{1,0:T(8,128)S(1)} %get-tuple-element.92.d_ref, f32[256,128]{1,0:T(8,128)S(1)} %get-tuple-element.93.b_ref, f32[896,128]{1,0:T(8,128)S(1)} %all_gather.65.t_ref, ...), custom_call_target="tpu_custom_call" | custom-call | tf_op jit(solution)/shard_map/invert7/pallas_call | solution.py:208
  179.9 8.6 %all_gather.66.m_ref = f32[896,128]{1,0:T(8,128)S(1)} all-gather(f32[448,128]{1,0:T(8,128)S(1)} %get-tuple-element.101), channel_id=1, replica_groups={{256,1},{258,3},{260,5},{262,7},{264,9},{266,11},{268,13},{270,15},{272..., dimensions={0}, use_global_device_ids=true | all-gather | bytes 688128 | tf_op jit(solution)/shard_map/all_gather | solution.py:252
  188.5 2.1 %couple7.1 = f32[448,128]{1,0:T(8,128)S(1)} custom-call(s32[2]{0:T(128)S(1)} %pad_add_fusion.info, f32[896,128]{1,0:T(8,128)S(1)} %all_gather.66.m_ref, f32[256,256]{1,0:T(8,128)S(1)} %get-tuple-element.102.z_ref, f32[256,256]{1,0:T(8,128)S(1)} %collective-permute-done.7.far_ref), custom_call_target="tpu_custom_call" | custom-call | tf_op jit(solution)/shard_map/couple7/pallas_call | solution.py:208
  190.6 2.1 %all_gather.67.t_ref = f32[896,128]{1,0:T(8,128)S(1)} all-gather(f32[448,128]{1,0:T(8,128)S(1)} %couple7.1), channel_id=1, replica_groups=mesh['line'=256,'rhs'=2] {'rhs'}, dimensions={0}, use_global_device_ids=true | all-gather | bytes 688128 | tf_op jit(solution)/shard_map/all_gather | solution.py:269
  192.8 5.8 %end.1 = f32[1,32,256]{2,1,0:T(8,128)} custom-call(s32[2]{0:T(128)S(1)} %pad_add_fusion.info, f32[256,256]{1,0:T(8,128)S(1)} %get-tuple-element.99.d_ref, f32[256,128]{1,0:T(8,128)S(1)} %get-tuple-element.100.b_ref, f32[896,128]{1,0:T(8,128)S(1)} %all_gather.67.t_ref, f32[256,256]{1,0:T(8,128)S(1)} %get-tuple-element.104.guess_ref), custom_call_target="tpu_custom_call" | custom-call | tf_op jit(solution)/shard_map/end/pallas_call | solution.py:208
  (25 shorter events, 21.0 us)
Async XLA Ops:
  0.0 27.4 %collective-permute-start.1 = (f32[256,256]{1,0:T(8,128)}, f32[256,256]{1,0:T(8,128)S(1)}, u32[]{:S(2)}, u32[]{:S(2)}) collective-permute-start(f32[256,256]{1,0:T(8,128)} %bitcast.10), channel_id=1, source_target_pairs={{0,2},{2,4},{4,6},{5,1},{6,8},{7,3},{8,10},{9,5},{10,12},{11,7},{1... | collective-permute-start | bytes 786440 | tf_op jit(solution)/shard_map/ppermute | solution.py:244
  13.5 13.8 %collective-permute-start = (f32[256,256]{1,0:T(8,128)}, f32[256,256]{1,0:T(8,128)S(1)}, u32[]{:S(2)}, u32[]{:S(2)}) collective-permute-start(f32[256,256]{1,0:T(8,128)} %bitcast.11), channel_id=1, source_target_pairs={{3,1},{5,3},{7,5},{9,7},{11,9},{13,11},{15,13},{17,15},{19,17},{21... | collective-permute-start | bytes 786440 | tf_op jit(solution)/shard_map/ppermute | solution.py:243
  17.8 1.0 copy-start
  20.8 6.5 %copy-start.2 = (f32[1,256,256]{2,1,0:T(8,128)S(1)}, f32[1,256,256]{2,1,0:T(8,128)}, u32[]{:S(2)}) copy-start(f32[1,256,256]{2,1,0:T(8,128)} %param.4) | copy-start | bytes 786436
  29.2 7.9 %copy-start.1 = (f32[1,256,256]{2,1,0:T(8,128)S(1)}, f32[1,256,256]{2,1,0:T(8,128)}, u32[]{:S(2)}) copy-start(f32[1,256,256]{2,1,0:T(8,128)} %param.3) | copy-start | bytes 786436
  35.2 38.6 %collective-permute-start.2 = (f32[256,256]{1,0:T(8,128)S(1)}, f32[256,256]{1,0:T(8,128)S(1)}, u32[]{:S(2)}, u32[]{:S(2)}) collective-permute-start(f32[256,256]{1,0:T(8,128)S(1)} %get-tuple-element.62.c_ref), channel_id=1, source_target_pairs={{0,4},{2,6},{4,8},{5,1},{6,10},{7,3},{8,12},{9,5},{10,14},{11,7},{... | collective-permute-start | bytes 786440 | tf_op jit(solution)/shard_map/ppermute | solution.py:268
  75.9 19.1 %collective-permute-start.3 = (f32[256,256]{1,0:T(8,128)S(1)}, f32[256,256]{1,0:T(8,128)S(1)}, u32[]{:S(2)}, u32[]{:S(2)}) collective-permute-start(f32[256,256]{1,0:T(8,128)S(1)} %get-tuple-element.75), channel_id=1, source_target_pairs={{0,8},{2,10},{4,12},{6,14},{8,16},{9,1},{10,18},{11,3},{12,20},{13... | collective-permute-start | bytes 786440 | tf_op jit(solution)/shard_map/ppermute | solution.py:268
  97.1 17.4 %collective-permute-start.4 = (f32[256,256]{1,0:T(8,128)S(1)}, f32[256,256]{1,0:T(8,128)S(1)}, u32[]{:S(2)}, u32[]{:S(2)}) collective-permute-start(f32[256,256]{1,0:T(8,128)S(1)} %get-tuple-element.82), channel_id=1, source_target_pairs={{0,16},{2,18},{4,20},{6,22},{8,24},{10,26},{12,28},{14,30},{16,32}... | collective-permute-start | bytes 786440 | tf_op jit(solution)/shard_map/ppermute | solution.py:268
  116.7 25.8 %collective-permute-start.5 = (f32[256,256]{1,0:T(8,128)S(1)}, f32[256,256]{1,0:T(8,128)S(1)}, u32[]{:S(2)}, u32[]{:S(2)}) collective-permute-start(f32[256,256]{1,0:T(8,128)S(1)} %get-tuple-element.89), channel_id=1, source_target_pairs={{0,32},{2,34},{4,36},{6,38},{8,40},{10,42},{12,44},{14,46},{16,48}... | collective-permute-start | bytes 786440 | tf_op jit(solution)/shard_map/ppermute | solution.py:268
  144.5 16.9 %collective-permute-start.6 = (f32[256,256]{1,0:T(8,128)S(1)}, f32[256,256]{1,0:T(8,128)S(1)}, u32[]{:S(2)}, u32[]{:S(2)}) collective-permute-start(f32[256,256]{1,0:T(8,128)S(1)} %get-tuple-element.96), channel_id=1, source_target_pairs={{0,64},{2,66},{4,68},{6,70},{8,72},{10,74},{12,76},{14,78},{16,80}... | collective-permute-start | bytes 786440 | tf_op jit(solution)/shard_map/ppermute | solution.py:268
  163.5 25.0 %collective-permute-start.7 = (f32[256,256]{1,0:T(8,128)S(1)}, f32[256,256]{1,0:T(8,128)S(1)}, u32[]{:S(2)}, u32[]{:S(2)}) collective-permute-start(f32[256,256]{1,0:T(8,128)S(1)} %get-tuple-element.103), channel_id=1, source_target_pairs={{0,128},{2,130},{4,132},{6,134},{8,136},{10,138},{12,140},{14,142}... | collective-permute-start | bytes 786440 | tf_op jit(solution)/shard_map/ppermute | solution.py:268

commit v4 on v3

--- a/solution.py
+++ b/solution.py
@@ -13,6 +13,7 @@
 STRETCH = (1.0, 1.5, 1.5, 1.5, 1.5, 1.5, 1.0, 1.0, 1.0)
 RESIDUAL_MAX = 5.0e-3
 SLOW_STEPS = 80
+GATHERED = (0, 2)
 
 
 def split(x, terms):
@@ -96,9 +97,7 @@
     residual = identity - product(d_parts, x_parts)
     rest = residual.astype(BF16)
     y = product(x_parts, b_parts) + one(x_parts[0], one(rest, b_parts[0]).astype(BF16))
-    close = x + one(x_parts[0], rest)
-    x_ref[...] = close
-    finish(close, y)
+    finish(x + one(x_parts[0], rest), y)
     size = jnp.sum(residual * residual)
 
     @pl.when(jnp.logical_not(size < RESIDUAL_MAX * RESIDUAL_MAX))
@@ -121,6 +120,14 @@
         finish(x_ref[...], product(split(x_ref[...], 3), b_parts))
 
 
+def keep(x_ref, m_ref):
+    def finish(x, y):
+        x_ref[...] = x
+        pack(x, y, m_ref)
+
+    return finish
+
+
 def first_guess(d):
     identity = unit(d.shape[0])
     diagonal = jnp.sum(d * identity, axis=1, keepdims=True)
@@ -133,7 +140,7 @@
     sides = b_ref[...]
     b = jnp.concatenate([jnp.zeros_like(sides), sides], axis=0).T
     b_out[...] = b
-    invert(d, first_guess(d), b, doublings, x_ref, lambda x, y: pack(x, y, m_ref))
+    invert(d, first_guess(d), b, doublings, x_ref, keep(x_ref, m_ref))
 
 
 def reduce_rows(d_ref, b_ref, t_ref):
@@ -148,7 +155,7 @@
     d, b = reduce_rows(d_ref, b_ref, t_ref)
     d_out[...] = d
     b_out[...] = b
-    invert(d, stretch * guess_ref[...], b, doublings, x_ref, lambda x, y: pack(x, y, m_ref))
+    invert(d, stretch * guess_ref[...], b, doublings, x_ref, keep(x_ref, m_ref))
 
 
 def end_kernel(doublings, stretch, info, d_ref, b_ref, t_ref, guess_ref, out_ref, x_ref):
@@ -162,14 +169,16 @@
     invert(d, stretch * guess_ref[...], b, doublings, x_ref, finish)
 
 
-def transfer(c, info, m_ref, t_ref):
-    half = m_ref.shape[0] // 2
-    m = jnp.where(info[1] == 0, m_ref[half:], m_ref[:half])
+def transfer(c, m, t_ref):
     x, tail = unpack(m)
     c_parts = split(c, 3)
     z = product(c_parts, split(x, 3))
     pack(product(split(z, 3), c_parts, one_nt), product(c_parts, split(tail, 3)), t_ref)
     return z
+
+
+def received(info, m_ref):
+    return m_ref[...] if len(m_ref.shape) == 2 else jnp.where(info[1] == 0, m_ref[1], m_ref[0])
 
 
 def following(z, far):
@@ -183,21 +192,19 @@
     far = far_ref[...]
     far = jnp.where(below, far, far.T)
     far = jnp.where(jnp.logical_and(below, info[0] == 1), 0.0, far)
-    c_out[...] = following(transfer(c, info, m_ref, t_ref), far)
-
-
-def second_coupling_kernel(info, m_ref, c_ref, t_ref, z_out):
-    z_out[...] = transfer(c_ref[...], info, m_ref, t_ref)
-
-
-def coupling_kernel(info, m_ref, z_ref, far_ref, t_ref, z_out, c_out):
-    c = following(z_ref[...], far_ref[...])
-    c_out[...] = c
-    z_out[...] = transfer(c, info, m_ref, t_ref)
-
-
-def last_coupling_kernel(info, m_ref, z_ref, far_ref, t_ref):
-    transfer(following(z_ref[...], far_ref[...]), info, m_ref, t_ref)
+    c_out[...] = following(transfer(c, received(info, m_ref), t_ref), far)
+
+
+def coupling_kernel(info, m_ref, c_ref, t_ref, z_out):
+    z_out[...] = transfer(c_ref[...], received(info, m_ref), t_ref)
+
+
+def following_kernel(z_ref, far_ref, c_out):
+    c_out[...] = following(z_ref[...], far_ref[...])
+
+
+def last_coupling_kernel(m_ref, c_ref, t_ref):
+    transfer(c_ref[...], m_ref[...], t_ref)
 
 
 def call(kernel, name, operands, outs, scratch=(), scalars=False):
@@ -217,12 +224,12 @@
 
 
 def pairs(line, stride):
-    if 2 * stride < line:
-        return [[2 * p, 2 * ((p - stride) % line) + 1] for p in range(line)]
-    real = [[2 * p, 2 * (p - stride) + 1] for p in range(stride, line)]
-    quarter = line // 4
-    idle = [[2 * p, 2 * (p + (3 * quarter if p < quarter else quarter)) + 1] for p in range(stride)]
-    return real + idle
+    return [[2 * p, 2 * ((p - stride) % line) + 1] for p in range(line)]
+
+
+def swapped(line, stride):
+    both = [(2 * p, 2 * (p - stride) + 1) for p in range(stride, line)]
+    return both + [(b, a) for a, b in both]
 
 
 def outward(line, stride, core0, core1):
@@ -249,23 +256,23 @@
         functools.partial(start_kernel, DOUBLINGS[0]), "start", (d, sides), (packed, square, tall)
     )
     while stride < line:
-        both = lax.all_gather(message, BOTH, axis_index_groups=pairs(line, stride), tiled=True)
+        if level in GATHERED:
+            near_m = lax.all_gather(message, BOTH, axis_index_groups=pairs(line, stride))
+        else:
+            near_m = lax.ppermute(message, BOTH, swapped(line, stride))
+        if level in GATHERED and level > 1:
+            near_m, z = lax.optimization_barrier((near_m, z))
+        if level > 1:
+            (c,) = call(following_kernel, f"follow{level}", (z, far), (square,))
         if level == 0:
             term, c = call(
-                first_coupling_kernel, "couple0", (info, both, low, near, far), (packed, square), scalars=True
+                first_coupling_kernel, "couple0", (info, near_m, low, near, far), (packed, square), scalars=True
             )
-        elif level == 1:
-            term, z = call(second_coupling_kernel, "couple1", (info, both, c), (packed, square), scalars=True)
         elif 2 * stride < line:
-            term, z, c = call(
-                coupling_kernel, f"couple{level}", (info, both, z, far), (packed, square, square), scalars=True
-            )
+            term, z = call(coupling_kernel, f"couple{level}", (info, near_m, c), (packed, square), scalars=True)
+            far = lax.ppermute(c, BOTH, outward(line, stride, 1, 1))
         else:
-            (term,) = call(
-                last_coupling_kernel, f"couple{level}", (info, both, z, far), (packed,), scalars=True
-            )
-        if level > 0 and 2 * stride < line:
-            far = lax.ppermute(c, BOTH, outward(line, stride, 1, 1))
+            (term,) = call(last_coupling_kernel, f"couple{level}", (near_m, c), (packed,))
         terms = lax.all_gather(term, "rhs", tiled=True)
         level, stride = level + 1, 2 * stride
         place = min(level, len(DOUBLINGS) - 1)

time: 199 us -> 196 us (0.985)
  the two profiles are of different devices: /device:TPU:5 before, /device:TPU:7 now
where the time goes in v4:
time: 196 us; the launch traced here: 195 us
  blocking collectives  70.4 us (36%)
  starting transfers between devices  64.6 us (33%)
  Pallas kernels  49.8 us (25%)
  waiting for transfers between devices  9.25 us (5%)
    pallas_call x23, Pallas kernels, call(): pl.pallas_call(kernel, name=name, in_specs=specs, out_specs=[pl.BlockSpec...  49.8 us
    all_gather x8, blocking collectives, on_device(): terms = lax.all_gather(term, 'rhs', tiled=True)  44.8 us
    ppermute x6, starting transfers between devices, on_device(): far = lax.ppermute(c, BOTH, outward(line, stride, 1, 1))  37.6 us
    all_gather x2, blocking collectives, on_device(): lax.all_gather(message, BOTH, axis_index_groups=pairs(line, stride))  23.5 us
    ppermute x1, starting transfers between devices, on_device(): far = lax.ppermute(low, BOTH, outward(line, 1, 1, 2))  13.8 us
    ppermute x6, starting transfers between devices, on_device(): near_m = lax.ppermute(message, BOTH, swapped(line, stride))  11.1 us
    ppermute x6, waiting for transfers between devices, on_device(): near_m = lax.ppermute(message, BOTH, swapped(line, stride))  7.33 us
  transfers between devices with their start and end apart: 14, of which 4 were waited for; matrix products, arithmetic and copies ran while one was open for 0% of the time, Pallas kernels for 19%

profile of v4, /device:TPU:7, one launch (start us, length us, event | category | flops | bytes accessed | tf_op | source)
XLA Modules:
  0.0 195.5 jit_solution(1693851866690327156)
XLA Ops:
  0.0 13.8 %collective-permute-start.1 = (f32[256,256]{1,0:T(8,128)}, f32[256,256]{1,0:T(8,128)S(1)}, u32[]{:S(2)}, u32[]{:S(2)}) collective-permute-start(f32[256,256]{1,0:T(8,128)} %bitcast.14), channel_id=1, source_target_pairs={{0,2},{2,4},{4,6},{5,1},{6,8},{7,3},{8,10},{9,5},{10,12},{11,7},{1... | collective-permute-start | bytes 786440 | tf_op jit(solution)/shard_map/ppermute | solution.py:251
  13.8 2.2 %collective-permute-start = (f32[256,256]{1,0:T(8,128)}, f32[256,256]{1,0:T(8,128)S(1)}, u32[]{:S(2)}, u32[]{:S(2)}) collective-permute-start(f32[256,256]{1,0:T(8,128)} %bitcast.15), channel_id=1, source_target_pairs={{3,1},{5,3},{7,5},{9,7},{11,9},{13,11},{15,13},{17,15},{19,17},{21... | collective-permute-start | bytes 786440 | tf_op jit(solution)/shard_map/ppermute | solution.py:250
  16.0 2.1 %all_gather.39.b_ref = f32[64,256]{1,0:T(8,128)S(1)} all-gather(f32[32,256]{1,0:T(8,128)} %bitcast.17), channel_id=1, replica_groups=mesh['line'=256,'rhs'=2] {'rhs'}, dimensions={0}, use_global_device_ids=true | all-gather | bytes 98304 | tf_op jit(solution)/shard_map/all_gather | solution.py:252
  19.0 2.0 %start.1 = (f32[448,128]{1,0:T(8,128)S(1)}, f32[256,256]{1,0:T(8,128)S(1)}, f32[256,128]{1,0:T(8,128)S(1)}) custom-call(f32[256,256]{1,0:T(8,128)S(1)} %bitcast.12, f32[64,256]{1,0:T(8,128)S(1)} %all_gather.39.b_ref), custom_call_target="tpu_custom_call" | custom-call | tf_op jit(solution)/shard_map/start/pallas_call | solution.py:215
  21.1 6.5 %all-gather = f32[896,128]{1,0:T(8,128)S(1)} all-gather(f32[448,128]{1,0:T(8,128)S(1)} %get-tuple-element.53), channel_id=2, replica_groups={{0,511},{2,1},{4,3},{6,5},{8,7},{10,9},{12,11},{14,13},{16,15},{18,17},..., dimensions={0}, use_global_device_ids=true | all-gather | bytes 688128 | tf_op jit(solution)/shard_map/all_gather | solution.py:260
  29.5 6.0 %all_gather.42.t_ref = f32[896,128]{1,0:T(8,128)S(1)} all-gather(f32[448,128]{1,0:T(8,128)S(1)} %get-tuple-element.54), channel_id=1, replica_groups=mesh['line'=256,'rhs'=2] {'rhs'}, dimensions={0}, use_global_device_ids=true | all-gather | bytes 688128 | tf_op jit(solution)/shard_map/all_gather | solution.py:276
  35.5 2.4 %invert1.1 = (f32[448,128]{1,0:T(8,128)S(1)}, f32[256,256]{1,0:T(8,128)S(1)}, f32[256,256]{1,0:T(8,128)S(1)}, f32[256,128]{1,0:T(8,128)S(1)}) custom-call(f32[256,256]{1,0:T(8,128)S(1)} %bitcast.13, f32[256,128]{1,0:T(8,128)S(1)} %get-tuple-element.52.b_ref, f32[896,128]{1,0:T(8,128)S(1)} %all_gather.42.t_ref, f32[256,256]{1,0:T(8,128)S(1)} %get-tuple-element.55.guess_ref), custom_call_target="tpu_custom_call" | custom-call | tf_op jit(solution)/shard_map/invert1/pallas_call | solution.py:215
  39.8 8.7 %collective-permute-start.3 = (f32[256,256]{1,0:T(8,128)S(1)}, f32[256,256]{1,0:T(8,128)S(1)}, u32[]{:S(2)}, u32[]{:S(2)}) collective-permute-start(f32[256,256]{1,0:T(8,128)S(1)} %get-tuple-element.59.c_ref), channel_id=1, source_target_pairs={{0,4},{2,6},{4,8},{5,1},{6,10},{7,3},{8,12},{9,5},{10,14},{11,7},{... | collective-permute-start | bytes 786440 | tf_op jit(solution)/shard_map/ppermute | solution.py:273
  48.6 2.1 %collective-permute-done.2.m_ref = f32[448,128]{1,0:T(8,128)S(1)} collective-permute-done((f32[448,128]{1,0:T(8,128)S(1)}, f32[448,128]{1,0:T(8,128)S(1)}, u32[]{:S(2)}, u32[]{:S(2)}) %collective-permute-start.2) | collective-permute-done | bytes 229408 | tf_op jit(solution)/shard_map/ppermute | solution.py:262
  52.5 2.5 %all_gather.43.t_ref = f32[896,128]{1,0:T(8,128)S(1)} all-gather(f32[448,128]{1,0:T(8,128)S(1)} %get-tuple-element.60), channel_id=1, replica_groups=mesh['line'=256,'rhs'=2] {'rhs'}, dimensions={0}, use_global_device_ids=true | all-gather | bytes 688128 | tf_op jit(solution)/shard_map/all_gather | solution.py:276
  55.0 2.4 %invert2.1 = (f32[448,128]{1,0:T(8,128)S(1)}, f32[256,256]{1,0:T(8,128)S(1)}, f32[256,256]{1,0:T(8,128)S(1)}, f32[256,128]{1,0:T(8,128)S(1)}) custom-call(f32[256,256]{1,0:T(8,128)S(1)} %get-tuple-element.56.d_ref, f32[256,128]{1,0:T(8,128)S(1)} %get-tuple-element.57.b_ref, f32[896,128]{1,0:T(8,128)S(1)} %all_gather.43.t_ref, ...), custom_call_target="tpu_custom_call" | custom-call | tf_op jit(solution)/shard_map/invert2/pallas_call | solution.py:215
  57.4 17.0 %all-gather.1 = f32[896,128]{1,0:T(8,128)S(1)} all-gather(f32[448,128]{1,0:T(8,128)S(1)} %get-tuple-element.64), channel_id=3, replica_groups={{0,505},{2,507},{4,509},{6,511},{8,1},{10,3},{12,5},{14,7},{16,9},{18,1..., dimensions={0}, use_global_device_ids=true | all-gather | bytes 688128 | tf_op jit(solution)/shard_map/all_gather | solution.py:260
  74.8 2.8 %collective-permute-start.5 = (f32[256,256]{1,0:T(8,128)S(1)}, f32[256,256]{1,0:T(8,128)S(1)}, u32[]{:S(2)}, u32[]{:S(2)}) collective-permute-start(f32[256,256]{1,0:T(8,128)S(1)} %follow2.1.c_ref), channel_id=1, source_target_pairs={{0,8},{2,10},{4,12},{6,14},{8,16},{9,1},{10,18},{11,3},{12,20},{13... | collective-permute-start | bytes 786440 | tf_op jit(solution)/shard_map/ppermute | solution.py:273
  77.7 1.9 couple2.1
  79.6 4.0 %all_gather.46.t_ref = f32[896,128]{1,0:T(8,128)S(1)} all-gather(f32[448,128]{1,0:T(8,128)S(1)} %get-tuple-element.68), channel_id=1, replica_groups=mesh['line'=256,'rhs'=2] {'rhs'}, dimensions={0}, use_global_device_ids=true | all-gather | bytes 688128 | tf_op jit(solution)/shard_map/all_gather | solution.py:276
  83.6 2.6 %invert3.1 = (f32[448,128]{1,0:T(8,128)S(1)}, f32[256,256]{1,0:T(8,128)S(1)}, f32[256,256]{1,0:T(8,128)S(1)}, f32[256,128]{1,0:T(8,128)S(1)}) custom-call(f32[256,256]{1,0:T(8,128)S(1)} %get-tuple-element.62.d_ref, f32[256,128]{1,0:T(8,128)S(1)} %get-tuple-element.63.b_ref, f32[896,128]{1,0:T(8,128)S(1)} %all_gather.46.t_ref, ...), custom_call_target="tpu_custom_call" | custom-call | tf_op jit(solution)/shard_map/invert3/pallas_call | solution.py:215
  90.5 8.1 %collective-permute-start.7 = (f32[256,256]{1,0:T(8,128)S(1)}, f32[256,256]{1,0:T(8,128)S(1)}, u32[]{:S(2)}, u32[]{:S(2)}) collective-permute-start(f32[256,256]{1,0:T(8,128)S(1)} %follow3.1.c_ref), channel_id=1, source_target_pairs={{0,16},{2,18},{4,20},{6,22},{8,24},{10,26},{12,28},{14,30},{16,32}... | collective-permute-start | bytes 786440 | tf_op jit(solution)/shard_map/ppermute | solution.py:273
  100.6 2.1 %all_gather.47.t_ref = f32[896,128]{1,0:T(8,128)S(1)} all-gather(f32[448,128]{1,0:T(8,128)S(1)} %get-tuple-element.74), channel_id=1, replica_groups=mesh['line'=256,'rhs'=2] {'rhs'}, dimensions={0}, use_global_device_ids=true | all-gather | bytes 688128 | tf_op jit(solution)/shard_map/all_gather | solution.py:276
  102.7 2.6 %invert4.1 = (f32[448,128]{1,0:T(8,128)S(1)}, f32[256,256]{1,0:T(8,128)S(1)}, f32[256,256]{1,0:T(8,128)S(1)}, f32[256,128]{1,0:T(8,128)S(1)}) custom-call(f32[256,256]{1,0:T(8,128)S(1)} %get-tuple-element.70.d_ref, f32[256,128]{1,0:T(8,128)S(1)} %get-tuple-element.71.b_ref, f32[896,128]{1,0:T(8,128)S(1)} %all_gather.47.t_ref, ...), custom_call_target="tpu_custom_call" | custom-call | tf_op jit(solution)/shard_map/invert4/pallas_call | solution.py:215
  107.7 6.4 %collective-permute-start.9 = (f32[256,256]{1,0:T(8,128)S(1)}, f32[256,256]{1,0:T(8,128)S(1)}, u32[]{:S(2)}, u32[]{:S(2)}) collective-permute-start(f32[256,256]{1,0:T(8,128)S(1)} %follow4.1.c_ref), channel_id=1, source_target_pairs={{0,32},{2,34},{4,36},{6,38},{8,40},{10,42},{12,44},{14,46},{16,48}... | collective-permute-start | bytes 786440 | tf_op jit(solution)/shard_map/ppermute | solution.py:273
  116.1 10.2 %all_gather.48.t_ref = f32[896,128]{1,0:T(8,128)S(1)} all-gather(f32[448,128]{1,0:T(8,128)S(1)} %get-tuple-element.80), channel_id=1, replica_groups=mesh['line'=256,'rhs'=2] {'rhs'}, dimensions={0}, use_global_device_ids=true | all-gather | bytes 688128 | tf_op jit(solution)/shard_map/all_gather | solution.py:276
  126.4 5.2 %invert5.1 = (f32[448,128]{1,0:T(8,128)S(1)}, f32[256,256]{1,0:T(8,128)S(1)}, f32[256,256]{1,0:T(8,128)S(1)}, f32[256,128]{1,0:T(8,128)S(1)}) custom-call(f32[256,256]{1,0:T(8,128)S(1)} %get-tuple-element.76.d_ref, f32[256,128]{1,0:T(8,128)S(1)} %get-tuple-element.77.b_ref, f32[896,128]{1,0:T(8,128)S(1)} %all_gather.48.t_ref, ...), custom_call_target="tpu_custom_call" | custom-call | tf_op jit(solution)/shard_map/invert5/pallas_call | solution.py:215
  131.6 4.0 %collective-permute-start.8 = (f32[448,128]{1,0:T(8,128)S(1)}, f32[448,128]{1,0:T(8,128)S(1)}, u32[]{:S(2)}, u32[]{:S(2)}) collective-permute-start(f32[448,128]{1,0:T(8,128)S(1)} %get-tuple-element.84), channel_id=1, source_target_pairs={{64,1},{66,3},{68,5},{70,7},{72,9},{74,11},{76,13},{78,15},{80,17}... | collective-permute-start | bytes 688136 | tf_op jit(solution)/shard_map/ppermute | solution.py:262
  136.0 6.6 %collective-permute-start.11 = (f32[256,256]{1,0:T(8,128)S(1)}, f32[256,256]{1,0:T(8,128)S(1)}, u32[]{:S(2)}, u32[]{:S(2)}) collective-permute-start(f32[256,256]{1,0:T(8,128)S(1)} %follow5.1.c_ref), channel_id=1, source_target_pairs={{0,64},{2,66},{4,68},{6,70},{8,72},{10,74},{12,76},{14,78},{16,80}... | collective-permute-start | bytes 786440 | tf_op jit(solution)/shard_map/ppermute | solution.py:273
  142.5 5.1 %collective-permute-done.8.m_ref = f32[448,128]{1,0:T(8,128)S(1)} collective-permute-done((f32[448,128]{1,0:T(8,128)S(1)}, f32[448,128]{1,0:T(8,128)S(1)}, u32[]{:S(2)}, u32[]{:S(2)}) %collective-permute-start.8) | collective-permute-done | bytes 229408 | tf_op jit(solution)/shard_map/ppermute | solution.py:262
  149.5 6.6 %all_gather.49.t_ref = f32[896,128]{1,0:T(8,128)S(1)} all-gather(f32[448,128]{1,0:T(8,128)S(1)} %get-tuple-element.86), channel_id=1, replica_groups=mesh['line'=256,'rhs'=2] {'rhs'}, dimensions={0}, use_global_device_ids=true | all-gather | bytes 688128 | tf_op jit(solution)/shard_map/all_gather | solution.py:276
  156.2 5.2 %invert6.1 = (f32[448,128]{1,0:T(8,128)S(1)}, f32[256,256]{1,0:T(8,128)S(1)}, f32[256,256]{1,0:T(8,128)S(1)}, f32[256,128]{1,0:T(8,128)S(1)}) custom-call(f32[256,256]{1,0:T(8,128)S(1)} %get-tuple-element.82.d_ref, f32[256,128]{1,0:T(8,128)S(1)} %get-tuple-element.83.b_ref, f32[896,128]{1,0:T(8,128)S(1)} %all_gather.49.t_ref, ...), custom_call_target="tpu_custom_call" | custom-call | tf_op jit(solution)/shard_map/invert6/pallas_call | solution.py:215
  162.4 4.9 %collective-permute-start.13 = (f32[256,256]{1,0:T(8,128)S(1)}, f32[256,256]{1,0:T(8,128)S(1)}, u32[]{:S(2)}, u32[]{:S(2)}) collective-permute-start(f32[256,256]{1,0:T(8,128)S(1)} %follow6.1.c_ref), channel_id=1, source_target_pairs={{0,128},{2,130},{4,132},{6,134},{8,136},{10,138},{12,140},{14,142}... | collective-permute-start | bytes 786440 | tf_op jit(solution)/shard_map/ppermute | solution.py:273
  169.2 3.5 %all_gather.50.t_ref = f32[896,128]{1,0:T(8,128)S(1)} all-gather(f32[448,128]{1,0:T(8,128)S(1)} %get-tuple-element.92), channel_id=1, replica_groups=mesh['line'=256,'rhs'=2] {'rhs'}, dimensions={0}, use_global_device_ids=true | all-gather | bytes 688128 | tf_op jit(solution)/shard_map/all_gather | solution.py:276
  172.7 4.6 %invert7.1 = (f32[448,128]{1,0:T(8,128)S(1)}, f32[256,256]{1,0:T(8,128)S(1)}, f32[256,256]{1,0:T(8,128)S(1)}, f32[256,128]{1,0:T(8,128)S(1)}) custom-call(f32[256,256]{1,0:T(8,128)S(1)} %get-tuple-element.88.d_ref, f32[256,128]{1,0:T(8,128)S(1)} %get-tuple-element.89.b_ref, f32[896,128]{1,0:T(8,128)S(1)} %all_gather.50.t_ref, ...), custom_call_target="tpu_custom_call" | custom-call | tf_op jit(solution)/shard_map/invert7/pallas_call | solution.py:215
  179.8 9.9 %all_gather.51.t_ref = f32[896,128]{1,0:T(8,128)S(1)} all-gather(f32[448,128]{1,0:T(8,128)S(1)} %couple7.1), channel_id=1, replica_groups=mesh['line'=256,'rhs'=2] {'rhs'}, dimensions={0}, use_global_device_ids=true | all-gather | bytes 688128 | tf_op jit(solution)/shard_map/all_gather | solution.py:276
  189.7 5.8 %end.1 = f32[1,32,256]{2,1,0:T(8,128)} custom-call(s32[2]{0:T(128)S(1)} %pad_add_fusion.info, f32[256,256]{1,0:T(8,128)S(1)} %get-tuple-element.94.d_ref, f32[256,128]{1,0:T(8,128)S(1)} %get-tuple-element.95.b_ref, f32[896,128]{1,0:T(8,128)S(1)} %all_gather.51.t_ref, f32[256,256]{1,0:T(8,128)S(1)} %get-tuple-element.98.guess_ref), custom_call_target="tpu_custom_call" | custom-call | tf_op jit(solution)/shard_map/end/pallas_call | solution.py:215
  (37 shorter events, 25.2 us)
Async XLA Ops:
  0.0 27.7 %collective-permute-start.1 = (f32[256,256]{1,0:T(8,128)}, f32[256,256]{1,0:T(8,128)S(1)}, u32[]{:S(2)}, u32[]{:S(2)}) collective-permute-start(f32[256,256]{1,0:T(8,128)} %bitcast.14), channel_id=1, source_target_pairs={{0,2},{2,4},{4,6},{5,1},{6,8},{7,3},{8,10},{9,5},{10,12},{11,7},{1... | collective-permute-start | bytes 786440 | tf_op jit(solution)/shard_map/ppermute | solution.py:251
  13.8 13.9 %collective-permute-start = (f32[256,256]{1,0:T(8,128)}, f32[256,256]{1,0:T(8,128)S(1)}, u32[]{:S(2)}, u32[]{:S(2)}) collective-permute-start(f32[256,256]{1,0:T(8,128)} %bitcast.15), channel_id=1, source_target_pairs={{3,1},{5,3},{7,5},{9,7},{11,9},{13,11},{15,13},{17,15},{19,17},{21... | collective-permute-start | bytes 786440 | tf_op jit(solution)/shard_map/ppermute | solution.py:250
  18.1 1.0 copy-start
  21.1 6.5 %copy-start.2 = (f32[1,256,256]{2,1,0:T(8,128)S(1)}, f32[1,256,256]{2,1,0:T(8,128)}, u32[]{:S(2)}) copy-start(f32[1,256,256]{2,1,0:T(8,128)} %param.4) | copy-start | bytes 786436
  29.5 6.0 %copy-start.1 = (f32[1,256,256]{2,1,0:T(8,128)S(1)}, f32[1,256,256]{2,1,0:T(8,128)}, u32[]{:S(2)}) copy-start(f32[1,256,256]{2,1,0:T(8,128)} %param.3) | copy-start | bytes 786436
  37.9 12.7 %collective-permute-start.2 = (f32[448,128]{1,0:T(8,128)S(1)}, f32[448,128]{1,0:T(8,128)S(1)}, u32[]{:S(2)}, u32[]{:S(2)}) collective-permute-start(f32[448,128]{1,0:T(8,128)S(1)} %get-tuple-element.58), channel_id=1, source_target_pairs={{4,1},{6,3},{8,5},{10,7},{12,9},{14,11},{16,13},{18,15},{20,17},{2... | collective-permute-start | bytes 688136 | tf_op jit(solution)/shard_map/ppermute | solution.py:262
  39.8 34.6 %collective-permute-start.3 = (f32[256,256]{1,0:T(8,128)S(1)}, f32[256,256]{1,0:T(8,128)S(1)}, u32[]{:S(2)}, u32[]{:S(2)}) collective-permute-start(f32[256,256]{1,0:T(8,128)S(1)} %get-tuple-element.59.c_ref), channel_id=1, source_target_pairs={{0,4},{2,6},{4,8},{5,1},{6,10},{7,3},{8,12},{9,5},{10,14},{11,7},{... | collective-permute-start | bytes 786440 | tf_op jit(solution)/shard_map/ppermute | solution.py:273
  74.8 15.3 %collective-permute-start.5 = (f32[256,256]{1,0:T(8,128)S(1)}, f32[256,256]{1,0:T(8,128)S(1)}, u32[]{:S(2)}, u32[]{:S(2)}) collective-permute-start(f32[256,256]{1,0:T(8,128)S(1)} %follow2.1.c_ref), channel_id=1, source_target_pairs={{0,8},{2,10},{4,12},{6,14},{8,16},{9,1},{10,18},{11,3},{12,20},{13... | collective-permute-start | bytes 786440 | tf_op jit(solution)/shard_map/ppermute | solution.py:273
  86.3 12.4 %collective-permute-start.4 = (f32[448,128]{1,0:T(8,128)S(1)}, f32[448,128]{1,0:T(8,128)S(1)}, u32[]{:S(2)}, u32[]{:S(2)}) collective-permute-start(f32[448,128]{1,0:T(8,128)S(1)} %get-tuple-element.72), channel_id=1, source_target_pairs={{16,1},{18,3},{20,5},{22,7},{24,9},{26,11},{28,13},{30,15},{32,17}... | collective-permute-start | bytes 688136 | tf_op jit(solution)/shard_map/ppermute | solution.py:262
  90.5 16.8 %collective-permute-start.7 = (f32[256,256]{1,0:T(8,128)S(1)}, f32[256,256]{1,0:T(8,128)S(1)}, u32[]{:S(2)}, u32[]{:S(2)}) collective-permute-start(f32[256,256]{1,0:T(8,128)S(1)} %follow3.1.c_ref), channel_id=1, source_target_pairs={{0,16},{2,18},{4,20},{6,22},{8,24},{10,26},{12,28},{14,30},{16,32}... | collective-permute-start | bytes 786440 | tf_op jit(solution)/shard_map/ppermute | solution.py:273
  105.3 8.9 %collective-permute-start.6 = (f32[448,128]{1,0:T(8,128)S(1)}, f32[448,128]{1,0:T(8,128)S(1)}, u32[]{:S(2)}, u32[]{:S(2)}) collective-permute-start(f32[448,128]{1,0:T(8,128)S(1)} %get-tuple-element.78), channel_id=1, source_target_pairs={{32,1},{34,3},{36,5},{38,7},{40,9},{42,11},{44,13},{46,15},{48,17}... | collective-permute-start | bytes 688136 | tf_op jit(solution)/shard_map/ppermute | solution.py:262
  107.7 27.9 %collective-permute-start.9 = (f32[256,256]{1,0:T(8,128)S(1)}, f32[256,256]{1,0:T(8,128)S(1)}, u32[]{:S(2)}, u32[]{:S(2)}) collective-permute-start(f32[256,256]{1,0:T(8,128)S(1)} %follow4.1.c_ref), channel_id=1, source_target_pairs={{0,32},{2,34},{4,36},{6,38},{8,40},{10,42},{12,44},{14,46},{16,48}... | collective-permute-start | bytes 786440 | tf_op jit(solution)/shard_map/ppermute | solution.py:273
  131.6 16.1 %collective-permute-start.8 = (f32[448,128]{1,0:T(8,128)S(1)}, f32[448,128]{1,0:T(8,128)S(1)}, u32[]{:S(2)}, u32[]{:S(2)}) collective-permute-start(f32[448,128]{1,0:T(8,128)S(1)} %get-tuple-element.84), channel_id=1, source_target_pairs={{64,1},{66,3},{68,5},{70,7},{72,9},{74,11},{76,13},{78,15},{80,17}... | collective-permute-start | bytes 688136 | tf_op jit(solution)/shard_map/ppermute | solution.py:262
  136.0 26.1 %collective-permute-start.11 = (f32[256,256]{1,0:T(8,128)S(1)}, f32[256,256]{1,0:T(8,128)S(1)}, u32[]{:S(2)}, u32[]{:S(2)}) collective-permute-start(f32[256,256]{1,0:T(8,128)S(1)} %follow5.1.c_ref), channel_id=1, source_target_pairs={{0,64},{2,66},{4,68},{6,70},{8,72},{10,74},{12,76},{14,78},{16,80}... | collective-permute-start | bytes 786440 | tf_op jit(solution)/shard_map/ppermute | solution.py:273
  161.3 6.0 %collective-permute-start.10 = (f32[448,128]{1,0:T(8,128)S(1)}, f32[448,128]{1,0:T(8,128)S(1)}, u32[]{:S(2)}, u32[]{:S(2)}) collective-permute-start(f32[448,128]{1,0:T(8,128)S(1)} %get-tuple-element.90), channel_id=1, source_target_pairs={{128,1},{130,3},{132,5},{134,7},{136,9},{138,11},{140,13},{142,15}... | collective-permute-start | bytes 688136 | tf_op jit(solution)/shard_map/ppermute | solution.py:262
  162.4 15.6 %collective-permute-start.13 = (f32[256,256]{1,0:T(8,128)S(1)}, f32[256,256]{1,0:T(8,128)S(1)}, u32[]{:S(2)}, u32[]{:S(2)}) collective-permute-start(f32[256,256]{1,0:T(8,128)S(1)} %follow6.1.c_ref), channel_id=1, source_target_pairs={{0,128},{2,130},{4,132},{6,134},{8,136},{10,138},{12,140},{14,142}... | collective-permute-start | bytes 786440 | tf_op jit(solution)/shard_map/ppermute | solution.py:273
  177.3 1.1 collective-permute-start.12

commit v5 on v4

--- a/solution.py
+++ b/solution.py
@@ -13,7 +13,7 @@
 STRETCH = (1.0, 1.5, 1.5, 1.5, 1.5, 1.5, 1.0, 1.0, 1.0)
 RESIDUAL_MAX = 5.0e-3
 SLOW_STEPS = 80
-GATHERED = (0, 2)
+HELD = (2,)
 
 
 def split(x, terms):
@@ -177,10 +177,6 @@
     return z
 
 
-def received(info, m_ref):
-    return m_ref[...] if len(m_ref.shape) == 2 else jnp.where(info[1] == 0, m_ref[1], m_ref[0])
-
-
 def following(z, far):
     return -product(split(z, 3), split(far, 3))
 
@@ -192,11 +188,11 @@
     far = far_ref[...]
     far = jnp.where(below, far, far.T)
     far = jnp.where(jnp.logical_and(below, info[0] == 1), 0.0, far)
-    c_out[...] = following(transfer(c, received(info, m_ref), t_ref), far)
-
-
-def coupling_kernel(info, m_ref, c_ref, t_ref, z_out):
-    z_out[...] = transfer(c_ref[...], received(info, m_ref), t_ref)
+    c_out[...] = following(transfer(c, m_ref[...], t_ref), far)
+
+
+def coupling_kernel(m_ref, c_ref, t_ref, z_out):
+    z_out[...] = transfer(c_ref[...], m_ref[...], t_ref)
 
 
 def following_kernel(z_ref, far_ref, c_out):
@@ -223,10 +219,6 @@
     )(*operands)
 
 
-def pairs(line, stride):
-    return [[2 * p, 2 * ((p - stride) % line) + 1] for p in range(line)]
-
-
 def swapped(line, stride):
     both = [(2 * p, 2 * (p - stride) + 1) for p in range(stride, line)]
     return both + [(b, a) for a, b in both]
@@ -256,20 +248,17 @@
         functools.partial(start_kernel, DOUBLINGS[0]), "start", (d, sides), (packed, square, tall)
     )
     while stride < line:
-        if level in GATHERED:
-            near_m = lax.all_gather(message, BOTH, axis_index_groups=pairs(line, stride))
-        else:
-            near_m = lax.ppermute(message, BOTH, swapped(line, stride))
-        if level in GATHERED and level > 1:
-            near_m, z = lax.optimization_barrier((near_m, z))
+        near_m = lax.ppermute(message, BOTH, swapped(line, stride))
         if level > 1:
             (c,) = call(following_kernel, f"follow{level}", (z, far), (square,))
+        if level in HELD:
+            near_m, c = lax.optimization_barrier((near_m, c))
         if level == 0:
             term, c = call(
                 first_coupling_kernel, "couple0", (info, near_m, low, near, far), (packed, square), scalars=True
             )
         elif 2 * stride < line:
-            term, z = call(coupling_kernel, f"couple{level}", (info, near_m, c), (packed, square), scalars=True)
+            term, z = call(coupling_kernel, f"couple{level}", (near_m, c), (packed, square))
             far = lax.ppermute(c, BOTH, outward(line, stride, 1, 1))
         else:
             (term,) = call(last_coupling_kernel, f"couple{level}", (near_m, c), (packed,))

time: 196 us -> 195 us (level)
  blocking collectives: 70.4 us -> 44.1 us
  starting transfers between devices: 64.6 us -> 81 us
  waiting for transfers between devices: 9.25 us -> 19.8 us
  Pallas kernels: 49.8 us -> 46.5 us
    all_gather x2 -> x0, blocking collectives: 23.5 us -> none  [on_device(): lax.all_gather(message, BOTH, axis_index_groups=pairs(line, stride))]
    ppermute x6 -> x8, waiting for transfers between devices: 7.33 us -> 19.8 us  [on_device(): near_m = lax.ppermute(message, BOTH, swapped(line, stride))]
    ppermute x6 -> x8, starting transfers between devices: 11.1 us -> 20.4 us  [on_device(): near_m = lax.ppermute(message, BOTH, swapped(line, stride))]
    ppermute x6, starting transfers between devices: 37.6 us -> 44.6 us  [on_device(): far = lax.ppermute(c, BOTH, outward(line, stride, 1, 1))]
    pallas_call x23, Pallas kernels: 49.8 us -> 46.5 us  [call(): pl.pallas_call(kernel, name=name, in_specs=specs, out_specs=[pl.BlockSpec...]
    all_gather x8, blocking collectives: 44.8 us -> 42 us  [on_device(): terms = lax.all_gather(term, 'rhs', tiled=True)]
  transfers between devices with their start and end apart: 14 -> 16, of which waited for: 4 -> 5; matrix products, arithmetic and copies ran while one was open for 0% -> 0% of each run, Pallas kernels for 19% -> 18%
where the time goes in v5:
time: 195 us; the launch traced here: 193 us
  starting transfers between devices  81 us (42%)
  Pallas kernels  46.5 us (24%)
  blocking collectives  44.1 us (23%)
  waiting for transfers between devices  19.8 us (10%)
    pallas_call x23, Pallas kernels, call(): pl.pallas_call(kernel, name=name, in_specs=specs, out_specs=[pl.BlockSpec...  46.5 us
    ppermute x6, starting transfers between devices, on_device(): far = lax.ppermute(c, BOTH, outward(line, stride, 1, 1))  44.6 us
    all_gather x8, blocking collectives, on_device(): terms = lax.all_gather(term, 'rhs', tiled=True)  42 us
    ppermute x8, starting transfers between devices, on_device(): near_m = lax.ppermute(message, BOTH, swapped(line, stride))  20.4 us
    ppermute x8, waiting for transfers between devices, on_device(): near_m = lax.ppermute(message, BOTH, swapped(line, stride))  19.8 us
    ppermute x1, starting transfers between devices, on_device(): far = lax.ppermute(low, BOTH, outward(line, 1, 1, 2))  13.8 us
  transfers between devices with their start and end apart: 16, of which 5 were waited for; matrix products, arithmetic and copies ran while one was open for 0% of the time, Pallas kernels for 18%

profile of v5, /device:TPU:7, one launch (start us, length us, event | category | flops | bytes accessed | tf_op | source)
XLA Modules:
  0.0 192.7 jit_solution(7590004048846443738)
XLA Ops:
  0.0 13.8 %collective-permute-start.2 = (f32[256,256]{1,0:T(8,128)}, f32[256,256]{1,0:T(8,128)S(1)}, u32[]{:S(2)}, u32[]{:S(2)}) collective-permute-start(f32[256,256]{1,0:T(8,128)} %bitcast.10), channel_id=1, source_target_pairs={{0,2},{2,4},{4,6},{5,1},{6,8},{7,3},{8,10},{9,5},{10,12},{11,7},{1... | collective-permute-start | bytes 786440 | tf_op jit(solution)/shard_map/ppermute | solution.py:243
  13.8 2.2 %collective-permute-start.1 = (f32[256,256]{1,0:T(8,128)}, f32[256,256]{1,0:T(8,128)S(1)}, u32[]{:S(2)}, u32[]{:S(2)}) collective-permute-start(f32[256,256]{1,0:T(8,128)} %bitcast.11), channel_id=1, source_target_pairs={{3,1},{5,3},{7,5},{9,7},{11,9},{13,11},{15,13},{17,15},{19,17},{21... | collective-permute-start | bytes 786440 | tf_op jit(solution)/shard_map/ppermute | solution.py:242
  16.0 2.1 %all_gather.27.b_ref = f32[64,256]{1,0:T(8,128)S(1)} all-gather(f32[32,256]{1,0:T(8,128)} %bitcast.13), channel_id=1, replica_groups=mesh['line'=256,'rhs'=2] {'rhs'}, dimensions={0}, use_global_device_ids=true | all-gather | bytes 98304 | tf_op jit(solution)/shard_map/all_gather | solution.py:244
  21.0 3.1 %collective-permute-start = (f32[448,128]{1,0:T(8,128)S(1)}, f32[448,128]{1,0:T(8,128)S(1)}, u32[]{:S(2)}, u32[]{:S(2)}) collective-permute-start(f32[448,128]{1,0:T(8,128)S(1)} %get-tuple-element.53), channel_id=1, source_target_pairs={{2,1},{4,3},{6,5},{8,7},{10,9},{12,11},{14,13},{16,15},{18,17},{20... | collective-permute-start | bytes 688136 | tf_op jit(solution)/shard_map/ppermute | solution.py:251
  24.3 4.1 %collective-permute-done.m_ref = f32[448,128]{1,0:T(8,128)S(1)} collective-permute-done((f32[448,128]{1,0:T(8,128)S(1)}, f32[448,128]{1,0:T(8,128)S(1)}, u32[]{:S(2)}, u32[]{:S(2)}) %collective-permute-start) | collective-permute-done | bytes 229408 | tf_op jit(solution)/shard_map/ppermute | solution.py:251
  30.2 6.3 %all_gather.28.t_ref = f32[896,128]{1,0:T(8,128)S(1)} all-gather(f32[448,128]{1,0:T(8,128)S(1)} %get-tuple-element.54), channel_id=1, replica_groups=mesh['line'=256,'rhs'=2] {'rhs'}, dimensions={0}, use_global_device_ids=true | all-gather | bytes 688128 | tf_op jit(solution)/shard_map/all_gather | solution.py:265
  36.4 2.4 %invert1.1 = (f32[448,128]{1,0:T(8,128)S(1)}, f32[256,256]{1,0:T(8,128)S(1)}, f32[256,256]{1,0:T(8,128)S(1)}, f32[256,128]{1,0:T(8,128)S(1)}) custom-call(f32[256,256]{1,0:T(8,128)S(1)} %bitcast.9, f32[256,128]{1,0:T(8,128)S(1)} %get-tuple-element.52.b_ref, f32[896,128]{1,0:T(8,128)S(1)} %all_gather.28.t_ref, f32[256,256]{1,0:T(8,128)S(1)} %get-tuple-element.55.guess_ref), custom_call_target="tpu_custom_call" | custom-call | tf_op jit(solution)/shard_map/invert1/pallas_call | solution.py:211
  40.8 8.7 %collective-permute-start.5 = (f32[256,256]{1,0:T(8,128)S(1)}, f32[256,256]{1,0:T(8,128)S(1)}, u32[]{:S(2)}, u32[]{:S(2)}) collective-permute-start(f32[256,256]{1,0:T(8,128)S(1)} %get-tuple-element.59.c_ref), channel_id=1, source_target_pairs={{0,4},{2,6},{4,8},{5,1},{6,10},{7,3},{8,12},{9,5},{10,14},{11,7},{... | collective-permute-start | bytes 786440 | tf_op jit(solution)/shard_map/ppermute | solution.py:262
  49.5 2.1 %collective-permute-done.3.m_ref = f32[448,128]{1,0:T(8,128)S(1)} collective-permute-done((f32[448,128]{1,0:T(8,128)S(1)}, f32[448,128]{1,0:T(8,128)S(1)}, u32[]{:S(2)}, u32[]{:S(2)}) %collective-permute-start.3) | collective-permute-done | bytes 229408 | tf_op jit(solution)/shard_map/ppermute | solution.py:251
  53.0 2.5 %all_gather.29.t_ref = f32[896,128]{1,0:T(8,128)S(1)} all-gather(f32[448,128]{1,0:T(8,128)S(1)} %get-tuple-element.60), channel_id=1, replica_groups=mesh['line'=256,'rhs'=2] {'rhs'}, dimensions={0}, use_global_device_ids=true | all-gather | bytes 688128 | tf_op jit(solution)/shard_map/all_gather | solution.py:265
  55.5 2.4 %invert2.1 = (f32[448,128]{1,0:T(8,128)S(1)}, f32[256,256]{1,0:T(8,128)S(1)}, f32[256,256]{1,0:T(8,128)S(1)}, f32[256,128]{1,0:T(8,128)S(1)}) custom-call(f32[256,256]{1,0:T(8,128)S(1)} %get-tuple-element.56.d_ref, f32[256,128]{1,0:T(8,128)S(1)} %get-tuple-element.57.b_ref, f32[896,128]{1,0:T(8,128)S(1)} %all_gather.29.t_ref, ...), custom_call_target="tpu_custom_call" | custom-call | tf_op jit(solution)/shard_map/invert2/pallas_call | solution.py:211
  57.9 3.4 %collective-permute-start.4 = (f32[448,128]{1,0:T(8,128)S(1)}, f32[448,128]{1,0:T(8,128)S(1)}, u32[]{:S(2)}, u32[]{:S(2)}) collective-permute-start(f32[448,128]{1,0:T(8,128)S(1)} %get-tuple-element.64), channel_id=1, source_target_pairs={{8,1},{10,3},{12,5},{14,7},{16,9},{18,11},{20,13},{22,15},{24,17},... | collective-permute-start | bytes 688136 | tf_op jit(solution)/shard_map/ppermute | solution.py:251
  61.8 9.7 %collective-permute-done.4.m_ref = f32[448,128]{1,0:T(8,128)S(1)} collective-permute-done((f32[448,128]{1,0:T(8,128)S(1)}, f32[448,128]{1,0:T(8,128)S(1)}, u32[]{:S(2)}, u32[]{:S(2)}) %collective-permute-start.4) | collective-permute-done | bytes 229408 | tf_op jit(solution)/shard_map/ppermute | solution.py:251
  71.5 6.2 %collective-permute-start.7 = (f32[256,256]{1,0:T(8,128)S(1)}, f32[256,256]{1,0:T(8,128)S(1)}, u32[]{:S(2)}, u32[]{:S(2)}) collective-permute-start(f32[256,256]{1,0:T(8,128)S(1)} %follow2.1.c_ref), channel_id=1, source_target_pairs={{0,8},{2,10},{4,12},{6,14},{8,16},{9,1},{10,18},{11,3},{12,20},{13... | collective-permute-start | bytes 786440 | tf_op jit(solution)/shard_map/ppermute | solution.py:262
  79.1 3.1 %all_gather.30.t_ref = f32[896,128]{1,0:T(8,128)S(1)} all-gather(f32[448,128]{1,0:T(8,128)S(1)} %get-tuple-element.68), channel_id=1, replica_groups=mesh['line'=256,'rhs'=2] {'rhs'}, dimensions={0}, use_global_device_ids=true | all-gather | bytes 688128 | tf_op jit(solution)/shard_map/all_gather | solution.py:265
  82.2 2.6 %invert3.1 = (f32[448,128]{1,0:T(8,128)S(1)}, f32[256,256]{1,0:T(8,128)S(1)}, f32[256,256]{1,0:T(8,128)S(1)}, f32[256,128]{1,0:T(8,128)S(1)}) custom-call(f32[256,256]{1,0:T(8,128)S(1)} %get-tuple-element.62.d_ref, f32[256,128]{1,0:T(8,128)S(1)} %get-tuple-element.63.b_ref, f32[896,128]{1,0:T(8,128)S(1)} %all_gather.30.t_ref, ...), custom_call_target="tpu_custom_call" | custom-call | tf_op jit(solution)/shard_map/invert3/pallas_call | solution.py:211
  87.2 11.4 %collective-permute-start.9 = (f32[256,256]{1,0:T(8,128)S(1)}, f32[256,256]{1,0:T(8,128)S(1)}, u32[]{:S(2)}, u32[]{:S(2)}) collective-permute-start(f32[256,256]{1,0:T(8,128)S(1)} %follow3.1.c_ref), channel_id=1, source_target_pairs={{0,16},{2,18},{4,20},{6,22},{8,24},{10,26},{12,28},{14,30},{16,32}... | collective-permute-start | bytes 786440 | tf_op jit(solution)/shard_map/ppermute | solution.py:262
  100.0 2.1 %all_gather.31.t_ref = f32[896,128]{1,0:T(8,128)S(1)} all-gather(f32[448,128]{1,0:T(8,128)S(1)} %get-tuple-element.74), channel_id=1, replica_groups=mesh['line'=256,'rhs'=2] {'rhs'}, dimensions={0}, use_global_device_ids=true | all-gather | bytes 688128 | tf_op jit(solution)/shard_map/all_gather | solution.py:265
  102.1 2.6 %invert4.1 = (f32[448,128]{1,0:T(8,128)S(1)}, f32[256,256]{1,0:T(8,128)S(1)}, f32[256,256]{1,0:T(8,128)S(1)}, f32[256,128]{1,0:T(8,128)S(1)}) custom-call(f32[256,256]{1,0:T(8,128)S(1)} %get-tuple-element.70.d_ref, f32[256,128]{1,0:T(8,128)S(1)} %get-tuple-element.71.b_ref, f32[896,128]{1,0:T(8,128)S(1)} %all_gather.31.t_ref, ...), custom_call_target="tpu_custom_call" | custom-call | tf_op jit(solution)/shard_map/invert4/pallas_call | solution.py:211
  107.1 6.4 %collective-permute-start.11 = (f32[256,256]{1,0:T(8,128)S(1)}, f32[256,256]{1,0:T(8,128)S(1)}, u32[]{:S(2)}, u32[]{:S(2)}) collective-permute-start(f32[256,256]{1,0:T(8,128)S(1)} %follow4.1.c_ref), channel_id=1, source_target_pairs={{0,32},{2,34},{4,36},{6,38},{8,40},{10,42},{12,44},{14,46},{16,48}... | collective-permute-start | bytes 786440 | tf_op jit(solution)/shard_map/ppermute | solution.py:262
  115.3 4.5 %all_gather.32.t_ref = f32[896,128]{1,0:T(8,128)S(1)} all-gather(f32[448,128]{1,0:T(8,128)S(1)} %get-tuple-element.80), channel_id=1, replica_groups=mesh['line'=256,'rhs'=2] {'rhs'}, dimensions={0}, use_global_device_ids=true | all-gather | bytes 688128 | tf_op jit(solution)/shard_map/all_gather | solution.py:265
  119.8 5.2 %invert5.1 = (f32[448,128]{1,0:T(8,128)S(1)}, f32[256,256]{1,0:T(8,128)S(1)}, f32[256,256]{1,0:T(8,128)S(1)}, f32[256,128]{1,0:T(8,128)S(1)}) custom-call(f32[256,256]{1,0:T(8,128)S(1)} %get-tuple-element.76.d_ref, f32[256,128]{1,0:T(8,128)S(1)} %get-tuple-element.77.b_ref, f32[896,128]{1,0:T(8,128)S(1)} %all_gather.32.t_ref, ...), custom_call_target="tpu_custom_call" | custom-call | tf_op jit(solution)/shard_map/invert5/pallas_call | solution.py:211
  125.0 6.7 %collective-permute-start.10 = (f32[448,128]{1,0:T(8,128)S(1)}, f32[448,128]{1,0:T(8,128)S(1)}, u32[]{:S(2)}, u32[]{:S(2)}) collective-permute-start(f32[448,128]{1,0:T(8,128)S(1)} %get-tuple-element.84), channel_id=1, source_target_pairs={{64,1},{66,3},{68,5},{70,7},{72,9},{74,11},{76,13},{78,15},{80,17}... | collective-permute-start | bytes 688136 | tf_op jit(solution)/shard_map/ppermute | solution.py:251
  132.1 4.2 %collective-permute-start.13 = (f32[256,256]{1,0:T(8,128)S(1)}, f32[256,256]{1,0:T(8,128)S(1)}, u32[]{:S(2)}, u32[]{:S(2)}) collective-permute-start(f32[256,256]{1,0:T(8,128)S(1)} %follow5.1.c_ref), channel_id=1, source_target_pairs={{0,64},{2,66},{4,68},{6,70},{8,72},{10,74},{12,76},{14,78},{16,80}... | collective-permute-start | bytes 786440 | tf_op jit(solution)/shard_map/ppermute | solution.py:262
  136.3 3.5 %collective-permute-done.10.m_ref = f32[448,128]{1,0:T(8,128)S(1)} collective-permute-done((f32[448,128]{1,0:T(8,128)S(1)}, f32[448,128]{1,0:T(8,128)S(1)}, u32[]{:S(2)}, u32[]{:S(2)}) %collective-permute-start.10) | collective-permute-done | bytes 229408 | tf_op jit(solution)/shard_map/ppermute | solution.py:251
  141.1 5.7 %all_gather.33.t_ref = f32[896,128]{1,0:T(8,128)S(1)} all-gather(f32[448,128]{1,0:T(8,128)S(1)} %get-tuple-element.86), channel_id=1, replica_groups=mesh['line'=256,'rhs'=2] {'rhs'}, dimensions={0}, use_global_device_ids=true | all-gather | bytes 688128 | tf_op jit(solution)/shard_map/all_gather | solution.py:265
  146.8 5.2 %invert6.1 = (f32[448,128]{1,0:T(8,128)S(1)}, f32[256,256]{1,0:T(8,128)S(1)}, f32[256,256]{1,0:T(8,128)S(1)}, f32[256,128]{1,0:T(8,128)S(1)}) custom-call(f32[256,256]{1,0:T(8,128)S(1)} %get-tuple-element.82.d_ref, f32[256,128]{1,0:T(8,128)S(1)} %get-tuple-element.83.b_ref, f32[896,128]{1,0:T(8,128)S(1)} %all_gather.33.t_ref, ...), custom_call_target="tpu_custom_call" | custom-call | tf_op jit(solution)/shard_map/invert6/pallas_call | solution.py:211
  153.0 7.7 %collective-permute-start.15 = (f32[256,256]{1,0:T(8,128)S(1)}, f32[256,256]{1,0:T(8,128)S(1)}, u32[]{:S(2)}, u32[]{:S(2)}) collective-permute-start(f32[256,256]{1,0:T(8,128)S(1)} %follow6.1.c_ref), channel_id=1, source_target_pairs={{0,128},{2,130},{4,132},{6,134},{8,136},{10,138},{12,140},{14,142}... | collective-permute-start | bytes 786440 | tf_op jit(solution)/shard_map/ppermute | solution.py:262
  162.1 4.0 %all_gather.34.t_ref = f32[896,128]{1,0:T(8,128)S(1)} all-gather(f32[448,128]{1,0:T(8,128)S(1)} %get-tuple-element.92), channel_id=1, replica_groups=mesh['line'=256,'rhs'=2] {'rhs'}, dimensions={0}, use_global_device_ids=true | all-gather | bytes 688128 | tf_op jit(solution)/shard_map/all_gather | solution.py:265
  166.1 4.6 %invert7.1 = (f32[448,128]{1,0:T(8,128)S(1)}, f32[256,256]{1,0:T(8,128)S(1)}, f32[256,256]{1,0:T(8,128)S(1)}, f32[256,128]{1,0:T(8,128)S(1)}) custom-call(f32[256,256]{1,0:T(8,128)S(1)} %get-tuple-element.88.d_ref, f32[256,128]{1,0:T(8,128)S(1)} %get-tuple-element.89.b_ref, f32[896,128]{1,0:T(8,128)S(1)} %all_gather.34.t_ref, ...), custom_call_target="tpu_custom_call" | custom-call | tf_op jit(solution)/shard_map/invert7/pallas_call | solution.py:211
  173.1 13.8 %all_gather.35.t_ref = f32[896,128]{1,0:T(8,128)S(1)} all-gather(f32[448,128]{1,0:T(8,128)S(1)} %couple7.1), channel_id=1, replica_groups=mesh['line'=256,'rhs'=2] {'rhs'}, dimensions={0}, use_global_device_ids=true | all-gather | bytes 688128 | tf_op jit(solution)/shard_map/all_gather | solution.py:265
  186.9 5.8 %end.1 = f32[1,32,256]{2,1,0:T(8,128)} custom-call(s32[2]{0:T(128)S(1)} %pad_add_fusion.info, f32[256,256]{1,0:T(8,128)S(1)} %get-tuple-element.94.d_ref, f32[256,128]{1,0:T(8,128)S(1)} %get-tuple-element.95.b_ref, f32[896,128]{1,0:T(8,128)S(1)} %all_gather.35.t_ref, f32[256,256]{1,0:T(8,128)S(1)} %get-tuple-element.98.guess_ref), custom_call_target="tpu_custom_call" | custom-call | tf_op jit(solution)/shard_map/end/pallas_call | solution.py:211
  (39 shorter events, 24.2 us)
Async XLA Ops:
  0.0 28.4 %collective-permute-start.2 = (f32[256,256]{1,0:T(8,128)}, f32[256,256]{1,0:T(8,128)S(1)}, u32[]{:S(2)}, u32[]{:S(2)}) collective-permute-start(f32[256,256]{1,0:T(8,128)} %bitcast.10), channel_id=1, source_target_pairs={{0,2},{2,4},{4,6},{5,1},{6,8},{7,3},{8,10},{9,5},{10,12},{11,7},{1... | collective-permute-start | bytes 786440 | tf_op jit(solution)/shard_map/ppermute | solution.py:243
  13.8 14.6 %collective-permute-start.1 = (f32[256,256]{1,0:T(8,128)}, f32[256,256]{1,0:T(8,128)S(1)}, u32[]{:S(2)}, u32[]{:S(2)}) collective-permute-start(f32[256,256]{1,0:T(8,128)} %bitcast.11), channel_id=1, source_target_pairs={{3,1},{5,3},{7,5},{9,7},{11,9},{13,11},{15,13},{17,15},{19,17},{21... | collective-permute-start | bytes 786440 | tf_op jit(solution)/shard_map/ppermute | solution.py:242
  18.1 1.0 copy-start
  19.0 9.4 %copy-start.2 = (f32[1,256,256]{2,1,0:T(8,128)S(1)}, f32[1,256,256]{2,1,0:T(8,128)}, u32[]{:S(2)}) copy-start(f32[1,256,256]{2,1,0:T(8,128)} %param.4) | copy-start | bytes 786436
  21.0 7.3 %collective-permute-start = (f32[448,128]{1,0:T(8,128)S(1)}, f32[448,128]{1,0:T(8,128)S(1)}, u32[]{:S(2)}, u32[]{:S(2)}) collective-permute-start(f32[448,128]{1,0:T(8,128)S(1)} %get-tuple-element.53), channel_id=1, source_target_pairs={{2,1},{4,3},{6,5},{8,7},{10,9},{12,11},{14,13},{16,15},{18,17},{20... | collective-permute-start | bytes 688136 | tf_op jit(solution)/shard_map/ppermute | solution.py:251
  30.2 6.3 %copy-start.1 = (f32[1,256,256]{2,1,0:T(8,128)S(1)}, f32[1,256,256]{2,1,0:T(8,128)}, u32[]{:S(2)}) copy-start(f32[1,256,256]{2,1,0:T(8,128)} %param.3) | copy-start | bytes 786436
  38.9 12.7 %collective-permute-start.3 = (f32[448,128]{1,0:T(8,128)S(1)}, f32[448,128]{1,0:T(8,128)S(1)}, u32[]{:S(2)}, u32[]{:S(2)}) collective-permute-start(f32[448,128]{1,0:T(8,128)S(1)} %get-tuple-element.58), channel_id=1, source_target_pairs={{4,1},{6,3},{8,5},{10,7},{12,9},{14,11},{16,13},{18,15},{20,17},{2... | collective-permute-start | bytes 688136 | tf_op jit(solution)/shard_map/ppermute | solution.py:251
  40.8 20.6 %collective-permute-start.5 = (f32[256,256]{1,0:T(8,128)S(1)}, f32[256,256]{1,0:T(8,128)S(1)}, u32[]{:S(2)}, u32[]{:S(2)}) collective-permute-start(f32[256,256]{1,0:T(8,128)S(1)} %get-tuple-element.59.c_ref), channel_id=1, source_target_pairs={{0,4},{2,6},{4,8},{5,1},{6,10},{7,3},{8,12},{9,5},{10,14},{11,7},{... | collective-permute-start | bytes 786440 | tf_op jit(solution)/shard_map/ppermute | solution.py:262
  57.9 13.6 %collective-permute-start.4 = (f32[448,128]{1,0:T(8,128)S(1)}, f32[448,128]{1,0:T(8,128)S(1)}, u32[]{:S(2)}, u32[]{:S(2)}) collective-permute-start(f32[448,128]{1,0:T(8,128)S(1)} %get-tuple-element.64), channel_id=1, source_target_pairs={{8,1},{10,3},{12,5},{14,7},{16,9},{18,11},{20,13},{22,15},{24,17},... | collective-permute-start | bytes 688136 | tf_op jit(solution)/shard_map/ppermute | solution.py:251
  71.5 15.3 %collective-permute-start.7 = (f32[256,256]{1,0:T(8,128)S(1)}, f32[256,256]{1,0:T(8,128)S(1)}, u32[]{:S(2)}, u32[]{:S(2)}) collective-permute-start(f32[256,256]{1,0:T(8,128)S(1)} %follow2.1.c_ref), channel_id=1, source_target_pairs={{0,8},{2,10},{4,12},{6,14},{8,16},{9,1},{10,18},{11,3},{12,20},{13... | collective-permute-start | bytes 786440 | tf_op jit(solution)/shard_map/ppermute | solution.py:262
  84.9 13.8 %collective-permute-start.6 = (f32[448,128]{1,0:T(8,128)S(1)}, f32[448,128]{1,0:T(8,128)S(1)}, u32[]{:S(2)}, u32[]{:S(2)}) collective-permute-start(f32[448,128]{1,0:T(8,128)S(1)} %get-tuple-element.72), channel_id=1, source_target_pairs={{16,1},{18,3},{20,5},{22,7},{24,9},{26,11},{28,13},{30,15},{32,17}... | collective-permute-start | bytes 688136 | tf_op jit(solution)/shard_map/ppermute | solution.py:251
  87.2 19.5 %collective-permute-start.9 = (f32[256,256]{1,0:T(8,128)S(1)}, f32[256,256]{1,0:T(8,128)S(1)}, u32[]{:S(2)}, u32[]{:S(2)}) collective-permute-start(f32[256,256]{1,0:T(8,128)S(1)} %follow3.1.c_ref), channel_id=1, source_target_pairs={{0,16},{2,18},{4,20},{6,22},{8,24},{10,26},{12,28},{14,30},{16,32}... | collective-permute-start | bytes 786440 | tf_op jit(solution)/shard_map/ppermute | solution.py:262
  104.8 9.1 %collective-permute-start.8 = (f32[448,128]{1,0:T(8,128)S(1)}, f32[448,128]{1,0:T(8,128)S(1)}, u32[]{:S(2)}, u32[]{:S(2)}) collective-permute-start(f32[448,128]{1,0:T(8,128)S(1)} %get-tuple-element.78), channel_id=1, source_target_pairs={{32,1},{34,3},{36,5},{38,7},{40,9},{42,11},{44,13},{46,15},{48,17}... | collective-permute-start | bytes 688136 | tf_op jit(solution)/shard_map/ppermute | solution.py:251
  107.1 24.6 %collective-permute-start.11 = (f32[256,256]{1,0:T(8,128)S(1)}, f32[256,256]{1,0:T(8,128)S(1)}, u32[]{:S(2)}, u32[]{:S(2)}) collective-permute-start(f32[256,256]{1,0:T(8,128)S(1)} %follow4.1.c_ref), channel_id=1, source_target_pairs={{0,32},{2,34},{4,36},{6,38},{8,40},{10,42},{12,44},{14,46},{16,48}... | collective-permute-start | bytes 786440 | tf_op jit(solution)/shard_map/ppermute | solution.py:262
  125.0 14.7 %collective-permute-start.10 = (f32[448,128]{1,0:T(8,128)S(1)}, f32[448,128]{1,0:T(8,128)S(1)}, u32[]{:S(2)}, u32[]{:S(2)}) collective-permute-start(f32[448,128]{1,0:T(8,128)S(1)} %get-tuple-element.84), channel_id=1, source_target_pairs={{64,1},{66,3},{68,5},{70,7},{72,9},{74,11},{76,13},{78,15},{80,17}... | collective-permute-start | bytes 688136 | tf_op jit(solution)/shard_map/ppermute | solution.py:251
  132.1 20.6 %collective-permute-start.13 = (f32[256,256]{1,0:T(8,128)S(1)}, f32[256,256]{1,0:T(8,128)S(1)}, u32[]{:S(2)}, u32[]{:S(2)}) collective-permute-start(f32[256,256]{1,0:T(8,128)S(1)} %follow5.1.c_ref), channel_id=1, source_target_pairs={{0,64},{2,66},{4,68},{6,70},{8,72},{10,74},{12,76},{14,78},{16,80}... | collective-permute-start | bytes 786440 | tf_op jit(solution)/shard_map/ppermute | solution.py:262
  152.0 8.8 %collective-permute-start.12 = (f32[448,128]{1,0:T(8,128)S(1)}, f32[448,128]{1,0:T(8,128)S(1)}, u32[]{:S(2)}, u32[]{:S(2)}) collective-permute-start(f32[448,128]{1,0:T(8,128)S(1)} %get-tuple-element.90), channel_id=1, source_target_pairs={{128,1},{130,3},{132,5},{134,7},{136,9},{138,11},{140,13},{142,15}... | collective-permute-start | bytes 688136 | tf_op jit(solution)/shard_map/ppermute | solution.py:251
  153.0 18.3 %collective-permute-start.15 = (f32[256,256]{1,0:T(8,128)S(1)}, f32[256,256]{1,0:T(8,128)S(1)}, u32[]{:S(2)}, u32[]{:S(2)}) collective-permute-start(f32[256,256]{1,0:T(8,128)S(1)} %follow6.1.c_ref), channel_id=1, source_target_pairs={{0,128},{2,130},{4,132},{6,134},{8,136},{10,138},{12,140},{14,142}... | collective-permute-start | bytes 786440 | tf_op jit(solution)/shard_map/ppermute | solution.py:262
  170.7 1.1 collective-permute-start.14

commit v6 on v5

--- a/solution.py
+++ b/solution.py
@@ -13,6 +13,7 @@
 STRETCH = (1.0, 1.5, 1.5, 1.5, 1.5, 1.5, 1.0, 1.0, 1.0)
 RESIDUAL_MAX = 5.0e-3
 SLOW_STEPS = 80
+GATHERED = (0,)
 HELD = (2,)
 
 
@@ -177,6 +178,10 @@
     return z
 
 
+def received(info, m_ref):
+    return m_ref[...] if len(m_ref.shape) == 2 else jnp.where(info[1] == 0, m_ref[1], m_ref[0])
+
+
 def following(z, far):
     return -product(split(z, 3), split(far, 3))
 
@@ -188,7 +193,7 @@
     far = far_ref[...]
     far = jnp.where(below, far, far.T)
     far = jnp.where(jnp.logical_and(below, info[0] == 1), 0.0, far)
-    c_out[...] = following(transfer(c, m_ref[...], t_ref), far)
+    c_out[...] = following(transfer(c, received(info, m_ref), t_ref), far)
 
 
 def coupling_kernel(m_ref, c_ref, t_ref, z_out):
@@ -219,6 +224,10 @@
     )(*operands)
 
 
+def pairs(line, stride):
+    return [[2 * p, 2 * ((p - stride) % line) + 1] for p in range(line)]
+
+
 def swapped(line, stride):
     both = [(2 * p, 2 * (p - stride) + 1) for p in range(stride, line)]
     return both + [(b, a) for a, b in both]
@@ -248,7 +257,10 @@
         functools.partial(start_kernel, DOUBLINGS[0]), "start", (d, sides), (packed, square, tall)
     )
     while stride < line:
-        near_m = lax.ppermute(message, BOTH, swapped(line, stride))
+        if level in GATHERED:
+            near_m = lax.all_gather(message, BOTH, axis_index_groups=pairs(line, stride))
+        else:
+            near_m = lax.ppermute(message, BOTH, swapped(line, stride))
         if level > 1:
             (c,) = call(following_kernel, f"follow{level}", (z, far), (square,))
         if level in HELD:

time: 195 us -> 193 us (0.990); the launches traced: 193 us -> 194 us
  starting transfers between devices: 81 us -> 76.9 us
  blocking collectives: 44.1 us -> 47.6 us
    ppermute x8 -> x7, starting transfers between devices: 20.4 us -> 13.2 us  [on_device(): near_m = lax.ppermute(message, BOTH, swapped(line, stride))]
    all_gather x0 -> x1, blocking collectives: none -> 6.54 us  [on_device(): lax.all_gather(message, BOTH, axis_index_groups=pairs(line, stride))]
    ppermute x6, starting transfers between devices: 44.6 us -> 47.7 us  [on_device(): far = lax.ppermute(c, BOTH, outward(line, stride, 1, 1))]
    all_gather x8, blocking collectives: 42 us -> 39 us  [on_device(): terms = lax.all_gather(term, 'rhs', tiled=True)]
    ppermute x8 -> x7, waiting for transfers between devices: 19.8 us -> 21.2 us  [on_device(): near_m = lax.ppermute(message, BOTH, swapped(line, stride))]
  transfers between devices with their start and end apart: 16 -> 15, of which waited for: 5 -> 4; matrix products, arithmetic and copies ran while one was open for 0% -> 0% of each run, Pallas kernels for 18% -> 18%
where the time goes in v6:
time: 193 us; the launch traced here: 194 us
  starting transfers between devices  76.9 us (40%)
  blocking collectives  47.6 us (25%)
  Pallas kernels  46.5 us (24%)
  waiting for transfers between devices  21.3 us (11%)
    ppermute x6, starting transfers between devices, on_device(): far = lax.ppermute(c, BOTH, outward(line, stride, 1, 1))  47.7 us
    pallas_call x23, Pallas kernels, call(): pl.pallas_call(kernel, name=name, in_specs=specs, out_specs=[pl.BlockSpec...  46.5 us
    all_gather x8, blocking collectives, on_device(): terms = lax.all_gather(term, 'rhs', tiled=True)  39 us
    ppermute x7, waiting for transfers between devices, on_device(): near_m = lax.ppermute(message, BOTH, swapped(line, stride))  21.2 us
    ppermute x1, starting transfers between devices, on_device(): far = lax.ppermute(low, BOTH, outward(line, 1, 1, 2))  13.8 us
    ppermute x7, starting transfers between devices, on_device(): near_m = lax.ppermute(message, BOTH, swapped(line, stride))  13.2 us
    all_gather x1, blocking collectives, on_device(): lax.all_gather(message, BOTH, axis_index_groups=pairs(line, stride))  6.54 us
  transfers between devices with their start and end apart: 15, of which 4 were waited for; matrix products, arithmetic and copies ran while one was open for 0% of the time, Pallas kernels for 18%

profile of v6, /device:TPU:7, one launch (start us, length us, event | category | flops | bytes accessed | tf_op | source)
XLA Modules:
  0.0 193.7 jit_solution(10645073511234965210)
XLA Ops:
  0.0 13.8 %collective-permute-start.1 = (f32[256,256]{1,0:T(8,128)}, f32[256,256]{1,0:T(8,128)S(1)}, u32[]{:S(2)}, u32[]{:S(2)}) collective-permute-start(f32[256,256]{1,0:T(8,128)} %bitcast.12), channel_id=1, source_target_pairs={{0,2},{2,4},{4,6},{5,1},{6,8},{7,3},{8,10},{9,5},{10,12},{11,7},{1... | collective-permute-start | bytes 786440 | tf_op jit(solution)/shard_map/ppermute | solution.py:252
  13.8 2.2 %collective-permute-start = (f32[256,256]{1,0:T(8,128)}, f32[256,256]{1,0:T(8,128)S(1)}, u32[]{:S(2)}, u32[]{:S(2)}) collective-permute-start(f32[256,256]{1,0:T(8,128)} %bitcast.13), channel_id=1, source_target_pairs={{3,1},{5,3},{7,5},{9,7},{11,9},{13,11},{15,13},{17,15},{19,17},{21... | collective-permute-start | bytes 786440 | tf_op jit(solution)/shard_map/ppermute | solution.py:251
  16.0 2.1 %all_gather.33.b_ref = f32[64,256]{1,0:T(8,128)S(1)} all-gather(f32[32,256]{1,0:T(8,128)} %bitcast.15), channel_id=1, replica_groups=mesh['line'=256,'rhs'=2] {'rhs'}, dimensions={0}, use_global_device_ids=true | all-gather | bytes 98304 | tf_op jit(solution)/shard_map/all_gather | solution.py:253
  21.1 6.5 %all-gather = f32[896,128]{1,0:T(8,128)S(1)} all-gather(f32[448,128]{1,0:T(8,128)S(1)} %get-tuple-element.53), channel_id=2, replica_groups={{0,511},{2,1},{4,3},{6,5},{8,7},{10,9},{12,11},{14,13},{16,15},{18,17},..., dimensions={0}, use_global_device_ids=true | all-gather | bytes 688128 | tf_op jit(solution)/shard_map/all_gather | solution.py:261
  29.5 6.0 %all_gather.36.t_ref = f32[896,128]{1,0:T(8,128)S(1)} all-gather(f32[448,128]{1,0:T(8,128)S(1)} %get-tuple-element.54), channel_id=1, replica_groups=mesh['line'=256,'rhs'=2] {'rhs'}, dimensions={0}, use_global_device_ids=true | all-gather | bytes 688128 | tf_op jit(solution)/shard_map/all_gather | solution.py:277
  35.5 2.4 %invert1.1 = (f32[448,128]{1,0:T(8,128)S(1)}, f32[256,256]{1,0:T(8,128)S(1)}, f32[256,256]{1,0:T(8,128)S(1)}, f32[256,128]{1,0:T(8,128)S(1)}) custom-call(f32[256,256]{1,0:T(8,128)S(1)} %bitcast.11, f32[256,128]{1,0:T(8,128)S(1)} %get-tuple-element.52.b_ref, f32[896,128]{1,0:T(8,128)S(1)} %all_gather.36.t_ref, f32[256,256]{1,0:T(8,128)S(1)} %get-tuple-element.55.guess_ref), custom_call_target="tpu_custom_call" | custom-call | tf_op jit(solution)/shard_map/invert1/pallas_call | solution.py:216
  39.8 8.7 %collective-permute-start.4 = (f32[256,256]{1,0:T(8,128)S(1)}, f32[256,256]{1,0:T(8,128)S(1)}, u32[]{:S(2)}, u32[]{:S(2)}) collective-permute-start(f32[256,256]{1,0:T(8,128)S(1)} %get-tuple-element.59.c_ref), channel_id=1, source_target_pairs={{0,4},{2,6},{4,8},{5,1},{6,10},{7,3},{8,12},{9,5},{10,14},{11,7},{... | collective-permute-start | bytes 786440 | tf_op jit(solution)/shard_map/ppermute | solution.py:274
  48.6 2.1 %collective-permute-done.2.m_ref = f32[448,128]{1,0:T(8,128)S(1)} collective-permute-done((f32[448,128]{1,0:T(8,128)S(1)}, f32[448,128]{1,0:T(8,128)S(1)}, u32[]{:S(2)}, u32[]{:S(2)}) %collective-permute-start.2) | collective-permute-done | bytes 229408 | tf_op jit(solution)/shard_map/ppermute | solution.py:263
  52.0 2.5 %all_gather.37.t_ref = f32[896,128]{1,0:T(8,128)S(1)} all-gather(f32[448,128]{1,0:T(8,128)S(1)} %get-tuple-element.60), channel_id=1, replica_groups=mesh['line'=256,'rhs'=2] {'rhs'}, dimensions={0}, use_global_device_ids=true | all-gather | bytes 688128 | tf_op jit(solution)/shard_map/all_gather | solution.py:277
  54.5 2.4 %invert2.1 = (f32[448,128]{1,0:T(8,128)S(1)}, f32[256,256]{1,0:T(8,128)S(1)}, f32[256,256]{1,0:T(8,128)S(1)}, f32[256,128]{1,0:T(8,128)S(1)}) custom-call(f32[256,256]{1,0:T(8,128)S(1)} %get-tuple-element.56.d_ref, f32[256,128]{1,0:T(8,128)S(1)} %get-tuple-element.57.b_ref, f32[896,128]{1,0:T(8,128)S(1)} %all_gather.37.t_ref, ...), custom_call_target="tpu_custom_call" | custom-call | tf_op jit(solution)/shard_map/invert2/pallas_call | solution.py:216
  56.9 3.4 %collective-permute-start.3 = (f32[448,128]{1,0:T(8,128)S(1)}, f32[448,128]{1,0:T(8,128)S(1)}, u32[]{:S(2)}, u32[]{:S(2)}) collective-permute-start(f32[448,128]{1,0:T(8,128)S(1)} %get-tuple-element.64), channel_id=1, source_target_pairs={{8,1},{10,3},{12,5},{14,7},{16,9},{18,11},{20,13},{22,15},{24,17},... | collective-permute-start | bytes 688136 | tf_op jit(solution)/shard_map/ppermute | solution.py:263
  60.7 9.9 %collective-permute-done.3.m_ref = f32[448,128]{1,0:T(8,128)S(1)} collective-permute-done((f32[448,128]{1,0:T(8,128)S(1)}, f32[448,128]{1,0:T(8,128)S(1)}, u32[]{:S(2)}, u32[]{:S(2)}) %collective-permute-start.3) | collective-permute-done | bytes 229408 | tf_op jit(solution)/shard_map/ppermute | solution.py:263
  70.6 7.1 %collective-permute-start.6 = (f32[256,256]{1,0:T(8,128)S(1)}, f32[256,256]{1,0:T(8,128)S(1)}, u32[]{:S(2)}, u32[]{:S(2)}) collective-permute-start(f32[256,256]{1,0:T(8,128)S(1)} %follow2.1.c_ref), channel_id=1, source_target_pairs={{0,8},{2,10},{4,12},{6,14},{8,16},{9,1},{10,18},{11,3},{12,20},{13... | collective-permute-start | bytes 786440 | tf_op jit(solution)/shard_map/ppermute | solution.py:274
  79.1 2.3 %all_gather.38.t_ref = f32[896,128]{1,0:T(8,128)S(1)} all-gather(f32[448,128]{1,0:T(8,128)S(1)} %get-tuple-element.68), channel_id=1, replica_groups=mesh['line'=256,'rhs'=2] {'rhs'}, dimensions={0}, use_global_device_ids=true | all-gather | bytes 688128 | tf_op jit(solution)/shard_map/all_gather | solution.py:277
  81.4 2.6 %invert3.1 = (f32[448,128]{1,0:T(8,128)S(1)}, f32[256,256]{1,0:T(8,128)S(1)}, f32[256,256]{1,0:T(8,128)S(1)}, f32[256,128]{1,0:T(8,128)S(1)}) custom-call(f32[256,256]{1,0:T(8,128)S(1)} %get-tuple-element.62.d_ref, f32[256,128]{1,0:T(8,128)S(1)} %get-tuple-element.63.b_ref, f32[896,128]{1,0:T(8,128)S(1)} %all_gather.38.t_ref, ...), custom_call_target="tpu_custom_call" | custom-call | tf_op jit(solution)/shard_map/invert3/pallas_call | solution.py:216
  84.0 2.6 %collective-permute-start.5 = (f32[448,128]{1,0:T(8,128)S(1)}, f32[448,128]{1,0:T(8,128)S(1)}, u32[]{:S(2)}, u32[]{:S(2)}) collective-permute-start(f32[448,128]{1,0:T(8,128)S(1)} %get-tuple-element.72), channel_id=1, source_target_pairs={{16,1},{18,3},{20,5},{22,7},{24,9},{26,11},{28,13},{30,15},{32,17}... | collective-permute-start | bytes 688136 | tf_op jit(solution)/shard_map/ppermute | solution.py:263
  87.1 12.0 %collective-permute-start.8 = (f32[256,256]{1,0:T(8,128)S(1)}, f32[256,256]{1,0:T(8,128)S(1)}, u32[]{:S(2)}, u32[]{:S(2)}) collective-permute-start(f32[256,256]{1,0:T(8,128)S(1)} %follow3.1.c_ref), channel_id=1, source_target_pairs={{0,16},{2,18},{4,20},{6,22},{8,24},{10,26},{12,28},{14,30},{16,32}... | collective-permute-start | bytes 786440 | tf_op jit(solution)/shard_map/ppermute | solution.py:274
  100.5 2.1 %all_gather.39.t_ref = f32[896,128]{1,0:T(8,128)S(1)} all-gather(f32[448,128]{1,0:T(8,128)S(1)} %get-tuple-element.74), channel_id=1, replica_groups=mesh['line'=256,'rhs'=2] {'rhs'}, dimensions={0}, use_global_device_ids=true | all-gather | bytes 688128 | tf_op jit(solution)/shard_map/all_gather | solution.py:277
  102.6 2.6 %invert4.1 = (f32[448,128]{1,0:T(8,128)S(1)}, f32[256,256]{1,0:T(8,128)S(1)}, f32[256,256]{1,0:T(8,128)S(1)}, f32[256,128]{1,0:T(8,128)S(1)}) custom-call(f32[256,256]{1,0:T(8,128)S(1)} %get-tuple-element.70.d_ref, f32[256,128]{1,0:T(8,128)S(1)} %get-tuple-element.71.b_ref, f32[896,128]{1,0:T(8,128)S(1)} %all_gather.39.t_ref, ...), custom_call_target="tpu_custom_call" | custom-call | tf_op jit(solution)/shard_map/invert4/pallas_call | solution.py:216
  107.6 6.4 %collective-permute-start.10 = (f32[256,256]{1,0:T(8,128)S(1)}, f32[256,256]{1,0:T(8,128)S(1)}, u32[]{:S(2)}, u32[]{:S(2)}) collective-permute-start(f32[256,256]{1,0:T(8,128)S(1)} %follow4.1.c_ref), channel_id=1, source_target_pairs={{0,32},{2,34},{4,36},{6,38},{8,40},{10,42},{12,44},{14,46},{16,48}... | collective-permute-start | bytes 786440 | tf_op jit(solution)/shard_map/ppermute | solution.py:274
  114.0 3.6 %collective-permute-done.7.m_ref = f32[448,128]{1,0:T(8,128)S(1)} collective-permute-done((f32[448,128]{1,0:T(8,128)S(1)}, f32[448,128]{1,0:T(8,128)S(1)}, u32[]{:S(2)}, u32[]{:S(2)}) %collective-permute-start.7) | collective-permute-done | bytes 229408 | tf_op jit(solution)/shard_map/ppermute | solution.py:263
  119.0 6.8 %all_gather.40.t_ref = f32[896,128]{1,0:T(8,128)S(1)} all-gather(f32[448,128]{1,0:T(8,128)S(1)} %get-tuple-element.80), channel_id=1, replica_groups=mesh['line'=256,'rhs'=2] {'rhs'}, dimensions={0}, use_global_device_ids=true | all-gather | bytes 688128 | tf_op jit(solution)/shard_map/all_gather | solution.py:277
  125.8 5.2 %invert5.1 = (f32[448,128]{1,0:T(8,128)S(1)}, f32[256,256]{1,0:T(8,128)S(1)}, f32[256,256]{1,0:T(8,128)S(1)}, f32[256,128]{1,0:T(8,128)S(1)}) custom-call(f32[256,256]{1,0:T(8,128)S(1)} %get-tuple-element.76.d_ref, f32[256,128]{1,0:T(8,128)S(1)} %get-tuple-element.77.b_ref, f32[896,128]{1,0:T(8,128)S(1)} %all_gather.40.t_ref, ...), custom_call_target="tpu_custom_call" | custom-call | tf_op jit(solution)/shard_map/invert5/pallas_call | solution.py:216
  133.3 8.6 %collective-permute-start.12 = (f32[256,256]{1,0:T(8,128)S(1)}, f32[256,256]{1,0:T(8,128)S(1)}, u32[]{:S(2)}, u32[]{:S(2)}) collective-permute-start(f32[256,256]{1,0:T(8,128)S(1)} %follow5.1.c_ref), channel_id=1, source_target_pairs={{0,64},{2,66},{4,68},{6,70},{8,72},{10,74},{12,76},{14,78},{16,80}... | collective-permute-start | bytes 786440 | tf_op jit(solution)/shard_map/ppermute | solution.py:274
  141.9 5.7 %collective-permute-done.9.m_ref = f32[448,128]{1,0:T(8,128)S(1)} collective-permute-done((f32[448,128]{1,0:T(8,128)S(1)}, f32[448,128]{1,0:T(8,128)S(1)}, u32[]{:S(2)}, u32[]{:S(2)}) %collective-permute-start.9) | collective-permute-done | bytes 229408 | tf_op jit(solution)/shard_map/ppermute | solution.py:263
  149.0 5.9 %all_gather.41.t_ref = f32[896,128]{1,0:T(8,128)S(1)} all-gather(f32[448,128]{1,0:T(8,128)S(1)} %get-tuple-element.86), channel_id=1, replica_groups=mesh['line'=256,'rhs'=2] {'rhs'}, dimensions={0}, use_global_device_ids=true | all-gather | bytes 688128 | tf_op jit(solution)/shard_map/all_gather | solution.py:277
  154.9 5.2 %invert6.1 = (f32[448,128]{1,0:T(8,128)S(1)}, f32[256,256]{1,0:T(8,128)S(1)}, f32[256,256]{1,0:T(8,128)S(1)}, f32[256,128]{1,0:T(8,128)S(1)}) custom-call(f32[256,256]{1,0:T(8,128)S(1)} %get-tuple-element.82.d_ref, f32[256,128]{1,0:T(8,128)S(1)} %get-tuple-element.83.b_ref, f32[896,128]{1,0:T(8,128)S(1)} %all_gather.41.t_ref, ...), custom_call_target="tpu_custom_call" | custom-call | tf_op jit(solution)/shard_map/invert6/pallas_call | solution.py:216
  161.2 4.9 %collective-permute-start.14 = (f32[256,256]{1,0:T(8,128)S(1)}, f32[256,256]{1,0:T(8,128)S(1)}, u32[]{:S(2)}, u32[]{:S(2)}) collective-permute-start(f32[256,256]{1,0:T(8,128)S(1)} %follow6.1.c_ref), channel_id=1, source_target_pairs={{0,128},{2,130},{4,132},{6,134},{8,136},{10,138},{12,140},{14,142}... | collective-permute-start | bytes 786440 | tf_op jit(solution)/shard_map/ppermute | solution.py:274
  167.4 3.5 %all_gather.42.t_ref = f32[896,128]{1,0:T(8,128)S(1)} all-gather(f32[448,128]{1,0:T(8,128)S(1)} %get-tuple-element.92), channel_id=1, replica_groups=mesh['line'=256,'rhs'=2] {'rhs'}, dimensions={0}, use_global_device_ids=true | all-gather | bytes 688128 | tf_op jit(solution)/shard_map/all_gather | solution.py:277
  170.9 4.6 %invert7.1 = (f32[448,128]{1,0:T(8,128)S(1)}, f32[256,256]{1,0:T(8,128)S(1)}, f32[256,256]{1,0:T(8,128)S(1)}, f32[256,128]{1,0:T(8,128)S(1)}) custom-call(f32[256,256]{1,0:T(8,128)S(1)} %get-tuple-element.88.d_ref, f32[256,128]{1,0:T(8,128)S(1)} %get-tuple-element.89.b_ref, f32[896,128]{1,0:T(8,128)S(1)} %all_gather.42.t_ref, ...), custom_call_target="tpu_custom_call" | custom-call | tf_op jit(solution)/shard_map/invert7/pallas_call | solution.py:216
  178.0 9.9 %all_gather.43.t_ref = f32[896,128]{1,0:T(8,128)S(1)} all-gather(f32[448,128]{1,0:T(8,128)S(1)} %couple7.1), channel_id=1, replica_groups=mesh['line'=256,'rhs'=2] {'rhs'}, dimensions={0}, use_global_device_ids=true | all-gather | bytes 688128 | tf_op jit(solution)/shard_map/all_gather | solution.py:277
  187.9 5.8 %end.1 = f32[1,32,256]{2,1,0:T(8,128)} custom-call(s32[2]{0:T(128)S(1)} %pad_add_fusion.info, f32[256,256]{1,0:T(8,128)S(1)} %get-tuple-element.94.d_ref, f32[256,128]{1,0:T(8,128)S(1)} %get-tuple-element.95.b_ref, f32[896,128]{1,0:T(8,128)S(1)} %all_gather.43.t_ref, f32[256,256]{1,0:T(8,128)S(1)} %get-tuple-element.98.guess_ref), custom_call_target="tpu_custom_call" | custom-call | tf_op jit(solution)/shard_map/end/pallas_call | solution.py:216
  (38 shorter events, 23.8 us)
Async XLA Ops:
  0.0 27.7 %collective-permute-start.1 = (f32[256,256]{1,0:T(8,128)}, f32[256,256]{1,0:T(8,128)S(1)}, u32[]{:S(2)}, u32[]{:S(2)}) collective-permute-start(f32[256,256]{1,0:T(8,128)} %bitcast.12), channel_id=1, source_target_pairs={{0,2},{2,4},{4,6},{5,1},{6,8},{7,3},{8,10},{9,5},{10,12},{11,7},{1... | collective-permute-start | bytes 786440 | tf_op jit(solution)/shard_map/ppermute | solution.py:252
  13.8 13.9 %collective-permute-start = (f32[256,256]{1,0:T(8,128)}, f32[256,256]{1,0:T(8,128)S(1)}, u32[]{:S(2)}, u32[]{:S(2)}) collective-permute-start(f32[256,256]{1,0:T(8,128)} %bitcast.13), channel_id=1, source_target_pairs={{3,1},{5,3},{7,5},{9,7},{11,9},{13,11},{15,13},{17,15},{19,17},{21... | collective-permute-start | bytes 786440 | tf_op jit(solution)/shard_map/ppermute | solution.py:251
  18.1 1.0 copy-start
  21.1 6.5 %copy-start.2 = (f32[1,256,256]{2,1,0:T(8,128)S(1)}, f32[1,256,256]{2,1,0:T(8,128)}, u32[]{:S(2)}) copy-start(f32[1,256,256]{2,1,0:T(8,128)} %param.4) | copy-start | bytes 786436
  29.5 6.0 %copy-start.1 = (f32[1,256,256]{2,1,0:T(8,128)S(1)}, f32[1,256,256]{2,1,0:T(8,128)}, u32[]{:S(2)}) copy-start(f32[1,256,256]{2,1,0:T(8,128)} %param.3) | copy-start | bytes 786436
  37.9 12.7 %collective-permute-start.2 = (f32[448,128]{1,0:T(8,128)S(1)}, f32[448,128]{1,0:T(8,128)S(1)}, u32[]{:S(2)}, u32[]{:S(2)}) collective-permute-start(f32[448,128]{1,0:T(8,128)S(1)} %get-tuple-element.58), channel_id=1, source_target_pairs={{4,1},{6,3},{8,5},{10,7},{12,9},{14,11},{16,13},{18,15},{20,17},{2... | collective-permute-start | bytes 688136 | tf_op jit(solution)/shard_map/ppermute | solution.py:263
  39.8 20.5 %collective-permute-start.4 = (f32[256,256]{1,0:T(8,128)S(1)}, f32[256,256]{1,0:T(8,128)S(1)}, u32[]{:S(2)}, u32[]{:S(2)}) collective-permute-start(f32[256,256]{1,0:T(8,128)S(1)} %get-tuple-element.59.c_ref), channel_id=1, source_target_pairs={{0,4},{2,6},{4,8},{5,1},{6,10},{7,3},{8,12},{9,5},{10,14},{11,7},{... | collective-permute-start | bytes 786440 | tf_op jit(solution)/shard_map/ppermute | solution.py:274
  56.9 13.7 %collective-permute-start.3 = (f32[448,128]{1,0:T(8,128)S(1)}, f32[448,128]{1,0:T(8,128)S(1)}, u32[]{:S(2)}, u32[]{:S(2)}) collective-permute-start(f32[448,128]{1,0:T(8,128)S(1)} %get-tuple-element.64), channel_id=1, source_target_pairs={{8,1},{10,3},{12,5},{14,7},{16,9},{18,11},{20,13},{22,15},{24,17},... | collective-permute-start | bytes 688136 | tf_op jit(solution)/shard_map/ppermute | solution.py:263
  70.6 16.1 %collective-permute-start.6 = (f32[256,256]{1,0:T(8,128)S(1)}, f32[256,256]{1,0:T(8,128)S(1)}, u32[]{:S(2)}, u32[]{:S(2)}) collective-permute-start(f32[256,256]{1,0:T(8,128)S(1)} %follow2.1.c_ref), channel_id=1, source_target_pairs={{0,8},{2,10},{4,12},{6,14},{8,16},{9,1},{10,18},{11,3},{12,20},{13... | collective-permute-start | bytes 786440 | tf_op jit(solution)/shard_map/ppermute | solution.py:274
  84.0 15.1 %collective-permute-start.5 = (f32[448,128]{1,0:T(8,128)S(1)}, f32[448,128]{1,0:T(8,128)S(1)}, u32[]{:S(2)}, u32[]{:S(2)}) collective-permute-start(f32[448,128]{1,0:T(8,128)S(1)} %get-tuple-element.72), channel_id=1, source_target_pairs={{16,1},{18,3},{20,5},{22,7},{24,9},{26,11},{28,13},{30,15},{32,17}... | collective-permute-start | bytes 688136 | tf_op jit(solution)/shard_map/ppermute | solution.py:263
  87.1 20.1 %collective-permute-start.8 = (f32[256,256]{1,0:T(8,128)S(1)}, f32[256,256]{1,0:T(8,128)S(1)}, u32[]{:S(2)}, u32[]{:S(2)}) collective-permute-start(f32[256,256]{1,0:T(8,128)S(1)} %follow3.1.c_ref), channel_id=1, source_target_pairs={{0,16},{2,18},{4,20},{6,22},{8,24},{10,26},{12,28},{14,30},{16,32}... | collective-permute-start | bytes 786440 | tf_op jit(solution)/shard_map/ppermute | solution.py:274
  105.3 12.4 %collective-permute-start.7 = (f32[448,128]{1,0:T(8,128)S(1)}, f32[448,128]{1,0:T(8,128)S(1)}, u32[]{:S(2)}, u32[]{:S(2)}) collective-permute-start(f32[448,128]{1,0:T(8,128)S(1)} %get-tuple-element.78), channel_id=1, source_target_pairs={{32,1},{34,3},{36,5},{38,7},{40,9},{42,11},{44,13},{46,15},{48,17}... | collective-permute-start | bytes 688136 | tf_op jit(solution)/shard_map/ppermute | solution.py:263
  107.6 25.3 %collective-permute-start.10 = (f32[256,256]{1,0:T(8,128)S(1)}, f32[256,256]{1,0:T(8,128)S(1)}, u32[]{:S(2)}, u32[]{:S(2)}) collective-permute-start(f32[256,256]{1,0:T(8,128)S(1)} %follow4.1.c_ref), channel_id=1, source_target_pairs={{0,32},{2,34},{4,36},{6,38},{8,40},{10,42},{12,44},{14,46},{16,48}... | collective-permute-start | bytes 786440 | tf_op jit(solution)/shard_map/ppermute | solution.py:274
  131.0 16.6 %collective-permute-start.9 = (f32[448,128]{1,0:T(8,128)S(1)}, f32[448,128]{1,0:T(8,128)S(1)}, u32[]{:S(2)}, u32[]{:S(2)}) collective-permute-start(f32[448,128]{1,0:T(8,128)S(1)} %get-tuple-element.84), channel_id=1, source_target_pairs={{64,1},{66,3},{68,5},{70,7},{72,9},{74,11},{76,13},{78,15},{80,17}... | collective-permute-start | bytes 688136 | tf_op jit(solution)/shard_map/ppermute | solution.py:263
  133.3 27.5 %collective-permute-start.12 = (f32[256,256]{1,0:T(8,128)S(1)}, f32[256,256]{1,0:T(8,128)S(1)}, u32[]{:S(2)}, u32[]{:S(2)}) collective-permute-start(f32[256,256]{1,0:T(8,128)S(1)} %follow5.1.c_ref), channel_id=1, source_target_pairs={{0,64},{2,66},{4,68},{6,70},{8,72},{10,74},{12,76},{14,78},{16,80}... | collective-permute-start | bytes 786440 | tf_op jit(solution)/shard_map/ppermute | solution.py:274
  160.1 6.0 %collective-permute-start.11 = (f32[448,128]{1,0:T(8,128)S(1)}, f32[448,128]{1,0:T(8,128)S(1)}, u32[]{:S(2)}, u32[]{:S(2)}) collective-permute-start(f32[448,128]{1,0:T(8,128)S(1)} %get-tuple-element.90), channel_id=1, source_target_pairs={{128,1},{130,3},{132,5},{134,7},{136,9},{138,11},{140,13},{142,15}... | collective-permute-start | bytes 688136 | tf_op jit(solution)/shard_map/ppermute | solution.py:263
  161.2 15.1 %collective-permute-start.14 = (f32[256,256]{1,0:T(8,128)S(1)}, f32[256,256]{1,0:T(8,128)S(1)}, u32[]{:S(2)}, u32[]{:S(2)}) collective-permute-start(f32[256,256]{1,0:T(8,128)S(1)} %follow6.1.c_ref), channel_id=1, source_target_pairs={{0,128},{2,130},{4,132},{6,134},{8,136},{10,138},{12,140},{14,142}... | collective-permute-start | bytes 786440 | tf_op jit(solution)/shard_map/ppermute | solution.py:274
  175.5 1.1 collective-permute-start.13
